TPU v7x, 512 devices: a whole 4x8x8 slice. The times are simulated.
512 devices in a mesh: dp: 64 (over y_lo, z, core), neg: 8 (over y_hi, x).
Axes of the slice: x: 4, y: 8 (y_hi: 2, y_lo: 4; y = y_hi * 4 + y_lo), z: 8, core: 2. Of those that a mesh axis runs over, the one named last changes fastest.
Arguments:
- queries: bfloat16 [131072, 256], P(('dp', 'neg')), may hold values from -6 to 6
- positives: bfloat16 [131072, 256], P(('dp', 'neg')), may hold values from -5 to 5
- negatives: bfloat16 [16384, 256], P('neg'), may hold values from -4.5 to 4.5
- pos_ids: int32 [131072], P(('dp', 'neg')), may hold values from 0 to 65535
- neg_ids: int32 [16384], P('neg'), may hold values from 0 to 65535
- counts: int32 [65536], replicated, may hold values from 1 to 1023
Outputs:
- query_grad: float32 [131072, 256], P(('dp', 'neg'))
- row_loss: float32 [131072], P(('dp', 'neg'))
- neg_grad: float32 [16384, 256], P(('neg', 'dp'))
All inputs are finite; a program needn't handle non-finite values.
Results may differ from a plain program's by a relative error of at most 0.0014.
Values may be sent and summed in bfloat16 or wider, within the bound.
No kernel may reach another device: no remote copies, remote signals or barrier semaphores. Data moves between devices by JAX's collectives and lax.ppermute only.
A program may use at most 64 MiB of HBM per device.

v0:
```python
import jax
import jax.numpy as jnp
from jax import lax
from jax.sharding import PartitionSpec as P


def joined_2(part, axis, combine):
    gathered = jax.tree.map(lambda a: lax.all_gather(a, axis), part)

    def take(source):
        return jax.tree.map(lambda a: lax.dynamic_index_in_dim(a, source, 0, False), gathered)

    return lax.fori_loop(
        1, lax.axis_size(axis), lambda source, state: combine(state, take(source)), take(0)
    )


def combine_stats(first, second):
    joined = jnp.maximum(first[0], second[0])
    total = first[1] * jnp.exp(first[0] - joined) + second[1] * jnp.exp(second[0] - joined)
    return (joined, total)


def per_device(queries, positives, negatives, pos_ids, neg_ids, counts):
    neg_corr = jnp.log(counts[neg_ids].astype(jnp.float32))
    pos_corr = jnp.log(counts[pos_ids].astype(jnp.float32))
    pos_float = positives.astype(jnp.float32)
    pos_score = jnp.sum(queries.astype(jnp.float32) * pos_float, axis=1) - pos_corr
    own_rows = queries.shape[0]
    width = queries.shape[1]
    shard_rows = negatives.shape[0]
    position = lax.axis_index("neg")

    def scores(block_rows):
        products = jnp.einsum(
            "rd,nd->rn", block_rows, negatives, preferred_element_type=jnp.float32
        )
        return products - neg_corr[None, :]

    def weights_of(block_rows, lse):
        return jnp.exp(scores(block_rows) - lse[:, None]).astype(jnp.bfloat16)

    def add_terms(neg_total, weight, block_rows):
        return neg_total + jnp.einsum(
            "rn,rd->nd", weight, block_rows, preferred_element_type=jnp.float32
        )

    neg_start = jnp.zeros((shard_rows, width), jnp.float32)
    gathered = lax.all_gather(queries, "neg", axis=0, tiled=True)
    total_rows = gathered.shape[0]
    row_block = min(512, total_rows)
    nblocks = total_rows // row_block
    blocks = gathered.reshape(nblocks, row_block, width)

    def block_stats(unused, block_rows):
        logits = scores(block_rows)
        block_max = jnp.max(logits, axis=1)
        block_sum = jnp.sum(jnp.exp(logits - block_max[:, None]), axis=1)
        return (unused, (block_max, block_sum))

    unused, (row_max, row_sum) = lax.scan(block_stats, jnp.zeros((), jnp.float32), blocks)
    row_max = row_max.reshape(total_rows)
    row_sum = row_sum.reshape(total_rows)
    begin = position * own_rows
    mine_max = lax.dynamic_slice_in_dim(row_max, begin, own_rows)
    mine_sum = lax.dynamic_slice_in_dim(row_sum, begin, own_rows)
    mine_max, mine_sum = combine_stats((mine_max, mine_sum), (pos_score, jnp.ones_like(pos_score)))
    row_max = lax.dynamic_update_slice_in_dim(row_max, mine_max, begin, 0)
    row_sum = lax.dynamic_update_slice_in_dim(row_sum, mine_sum, begin, 0)
    row_max, row_sum = joined_2((row_max, row_sum), "neg", combine_stats)
    lse_all = row_max + jnp.log(row_sum)

    def block_grads(neg_total, inputs):
        block_rows, block_lse = inputs
        weight = weights_of(block_rows, block_lse)
        grad_rows = jnp.dot(weight, negatives, preferred_element_type=jnp.float32)
        return (add_terms(neg_total, weight, block_rows), grad_rows)

    neg_total, grad_terms = lax.scan(
        block_grads, neg_start, (blocks, lse_all.reshape(nblocks, row_block))
    )
    query_acc = lax.psum_scatter(
        grad_terms.reshape(total_rows, width), "neg", scatter_dimension=0, tiled=True
    )
    lse = lax.dynamic_slice_in_dim(lse_all, begin, own_rows)
    pos_weight = jnp.exp(pos_score - lse)
    query_grad = query_acc + (pos_weight - 1.0)[:, None] * pos_float
    row_loss = lse - pos_score
    neg_grad = lax.psum_scatter(neg_total, "dp", scatter_dimension=0, tiled=True)
    return (query_grad, row_loss, neg_grad)


def solution(mesh):
    placed = (
        P(("dp", "neg"), None),
        P(("dp", "neg"), None),
        P("neg", None),
        P(("dp", "neg")),
        P("neg"),
        P(),
    )
    return jax.shard_map(
        per_device,
        mesh=mesh,
        in_specs=placed,
        out_specs=(P(("dp", "neg"), None), P(("dp", "neg")), P(("neg", "dp"), None)),
        check_vma=False,
    )
```

profile of v0, /device:TPU:4, one launch (start us, length us, event | category | flops | bytes accessed | tf_op | source)
XLA Modules:
  0.0 626.9 jit_solution(12267981539383369690)
XLA Ops:
  8.7 2.3 gather_fusion.1
  11.7 11.8 %gather_fusion = s32[2048]{0:T(1024)S(1)} fusion(s32[65536]{0:T(1024)S(1)} %copy-done, s32[2048]{0:T(1024)S(1)} %fusion.13), kind=kCustom, calls=%fused_computation | custom fusion | bytes 24576 | tf_op jit(solution)/shard_map/gather | solution.py:25
  23.5 1.6 fusion.11
  25.1 56.0 %all-gather.4.cloned.1.call-done = bf16[2048,256]{1,0:T(8,128)(2,1)} async-done(((bf16[256,256]{1,0:T(8,128)(2,1)}), bf16[2048,256]{1,0:T(8,128)(2,1)}) %all-gather.4.cloned.1.call-update) | async-done | bytes 1048592 | tf_op jit(solution)/shard_map/all_gather | solution.py:49
  81.1 21.0 %while.42 = (s32[]{:T(128)}, f32[4,512]{1,0:T(4,128)}, f32[4,512]{1,0:T(4,128)}, bf16[4,512,256]{2,1,0:T(8,128)(2,1)}, bf16[2048,256]{1,0:T(8,128)(2,1)S(1)}, /*index=5*/f32[2048]{0:T(1024)S(1)}, s32[]{:T(128)}, s32[]{:T(128)}) while((s32[]{:T(128)}, f32[4,512]{1,0:T(4,128)}, f32[4,512]{1,0:T(4,128)}, bf16[4,512,256]{2,1,0:T(8,128)(2,1)}, ...), condition=%wide.region_3.0_spmd, body=%wide.region_0.3_spmd.sunk | while | flops 542112768 | bytes 9730153 | solution.py:61
  81.1 1.8 subtract_reduce_fusion.2
  83.7 1.3 dynamic_update_slice.30
  85.0 1.3 dynamic_update_slice.31
  86.4 1.8 subtract_reduce_fusion.2
  89.0 1.3 dynamic_update_slice.30
  90.3 1.3 dynamic_update_slice.31
  91.6 1.8 subtract_reduce_fusion.2
  94.2 1.3 dynamic_update_slice.30
  95.6 1.3 dynamic_update_slice.31
  96.9 1.8 subtract_reduce_fusion.2
  99.5 1.3 dynamic_update_slice.30
  100.8 1.3 dynamic_update_slice.31
  102.8 1.3 copy.11
  104.1 1.3 reshape.64
  107.7 37.7 %all-gather = f32[8,1,2048]{2,1,0:T(1,128)S(1)} all-gather(f32[1,1,2048]{2,1,0:T(1,128)S(1)} %constant_dynamic-update-slice_fusion.1), channel_id=1, replica_groups=mesh['dp'=64,'neg'=8] {'neg'}, dimensions={0}, use_global_device_ids=true | all-gather | bytes 73728 | tf_op jit(solution)/shard_map/all_gather | solution.py:8
  146.6 44.0 %all-gather.1 = f32[8,1,2048]{2,1,0:T(1,128)S(1)} all-gather(f32[1,1,2048]{2,1,0:T(1,128)} %constant_dynamic-update-slice_fusion), channel_id=1, replica_groups=mesh['dp'=64,'neg'=8] {'neg'}, dimensions={0}, use_global_device_ids=true | all-gather | bytes 73728 | tf_op jit(solution)/shard_map/all_gather | solution.py:8
  191.9 15.4 %while.43 = (s32[]{:T(128)}, f32[2048]{0:T(1024)S(1)}, f32[2048]{0:T(1024)}, f32[8,2048]{1,0:T(8,128)}, f32[8,2048]{1,0:T(8,128)}, /*index=5*/s32[]{:T(128)}, s32[]{:T(128)}, s32[]{:T(128)}) while((s32[]{:T(128)}, f32[2048]{0:T(1024)S(1)}, f32[2048]{0:T(1024)}, f32[8,2048]{1,0:T(8,128)}, f32[8,2048]{1,0:T(8,128)}, /*index=5*/s32[]{:T(128)}, ...), condition=%wide.region_6.7_spmd, body=%wide.region_5.6_spmd.sunk | while | flops 12293 | bytes 82043 | solution.py:13
  192.7 1.3 multiply_add_fusion.2
  195.0 1.3 multiply_add_fusion.2
  197.2 1.3 multiply_add_fusion.2
  199.4 1.3 multiply_add_fusion.2
  201.6 1.3 multiply_add_fusion.2
  203.8 1.3 multiply_add_fusion.2
  206.0 1.3 multiply_add_fusion.2
  207.3 1.3 log_add_fusion
  209.3 23.4 %while.44 = (s32[]{:T(128)}, f32[2048,256]{1,0:T(8,128)S(1)}, f32[4,512,256]{2,1,0:T(8,128)}, bf16[4,512,256]{2,1,0:T(8,128)(2,1)}, bf16[2048,256]{1,0:T(8,128)(...) while((s32[]{:T(128)}, f32[2048,256]{1,0:T(8,128)S(1)}, ...), condition=%wide.region_8.9_spmd.clone, body=%wide.region_7.8_spmd.clone.sunk | while | flops 1614807040 | bytes 13645951 | solution.py:79
  209.3 1.8 exponential_convert_fusion.2
  211.1 2.5 convolution_add_fusion.2
  213.6 1.5 fusion.34
  215.1 1.8 exponential_convert_fusion.2
  216.9 2.5 convolution_add_fusion.2
  219.5 1.5 fusion.34
  221.0 1.8 exponential_convert_fusion.2
  222.8 2.5 convolution_add_fusion.2
  225.3 1.5 fusion.34
  226.9 1.8 exponential_convert_fusion.2
  228.6 2.5 convolution_add_fusion.2
  231.2 1.5 fusion.34
  232.8 1.2 copy-done.1
  234.0 1.3 dynamic-slice_subtract_fusion
  235.3 99.4 %reduce-scatter.3.cloned.1.call-done = f32[256,256]{1,0:T(8,128)} async-done(((f32[2048,256]{1,0:T(8,128)}), f32[256,256]{1,0:T(8,128)}) %reduce-scatter.3.cloned.1.call-update) | async-done | bytes 262160 | tf_op jit(solution)/shard_map/reduce_scatter | solution.py:82
  334.8 1.8 fusion.12
  336.5 283.9 %reduce-scatter.5.cloned.1.call-done = f32[32,256]{1,0:T(8,128)} async-done(((f32[2048,256]{1,0:T(8,128)}), f32[32,256]{1,0:T(8,128)}) %reduce-scatter.5.cloned.1.call-update) | async-done | bytes 32784 | tf_op jit(solution)/shard_map/reduce_scatter | solution.py:89
  (51 shorter events, 18.0 us)
Async XLA Ops:
  7.2 1.5 copy-start
  7.2 73.9 %all-gather.4.cloned.1.call-start = ((), (), s32[]{:S(2)}) async-start(), calls=%async_computation.2 | async-start | bytes 1179648 | tf_op jit(solution)/shard_map/all_gather | solution.py:49
  7.9 326.9 %reduce-scatter.3.cloned.1.call-start = ((), (), s32[]{:S(2)}) async-start(), calls=%async_computation.3 | async-start | bytes 2359296 | tf_op jit(solution)/shard_map/reduce_scatter | solution.py:82
  11.7 11.8 %copy-start.3 = (bf16[256,256]{1,0:T(8,128)(2,1)S(1)}, bf16[256,256]{1,0:T(8,128)(2,1)}, u32[]{:S(2)}) copy-start(bf16[256,256]{1,0:T(8,128)(2,1)} %param.13) | copy-start | bytes 393220
  11.7 69.4 %copy-start.2 = (bf16[2048,256]{1,0:T(8,128)(2,1)S(1)}, bf16[2048,256]{1,0:T(8,128)(2,1)}, u32[]{:S(2)}) copy-start(bf16[2048,256]{1,0:T(8,128)(2,1)} %param.14) | copy-start | bytes 3145732
  106.9 0.7 copy-start.4
  232.7 1.3 copy-start.1
  232.7 1.3 copy-start.5
  232.7 387.7 %reduce-scatter.5.cloned.1.call-start = ((), (), s32[]{:S(2)}) async-start(), calls=%async_computation.4 | async-start | bytes 2129920 | tf_op jit(solution)/shard_map/reduce_scatter | solution.py:89
Sparse Core Ops, SparseCore 0:
  11.2 69.8 all-gather.3
  232.8 101.9 reduce-scatter.2
  338.4 281.9 reduce-scatter.4
where the time goes:
time: 629 us; the launch traced here: 627 us
  waiting for transfers between devices  440 us (70%)
  blocking collectives  81.7 us (13%)
  local copies, waits for them, and re-layouts  39.3 us (6%)
  matrix products  30.4 us (5%)
  other arithmetic  21.4 us (3%)
  between operations  13.8 us (2%)
    reduce_scatter x1, waiting for transfers between devices, per_device(): lax.psum_scatter(neg_total, 'dp', scatter_dimension=0, tiled=True)  284 us
    reduce_scatter x1, waiting for transfers between devices, per_device(): lax.psum_scatter(grad_terms.reshape(total_rows, width), 'neg', scatter_di...  99.4 us
    all_gather x2, blocking collectives, joined_2(): gathered = jax.tree.map(lambda a: lax.all_gather(a, axis), part)  81.7 us
    all_gather x1, waiting for transfers between devices, per_device(): gathered = lax.all_gather(queries, 'neg', axis=0, tiled=True)  56 us
    dot_general x8, matrix products, scores(): jnp.einsum('rd,nd->rn', block_rows, negatives, preferred_element_type=jnp...  14.2 us
  transfers between devices with their start and end apart: 3, of which 3 were waited for; matrix products, arithmetic and copies ran while one was open for 3% of the time, Pallas kernels for 0%

commit v1 on v0

v1 whole, which is shorter than its diff:
```python
import jax
import jax.numpy as jnp
from jax import lax
from jax.experimental import pallas as pl
from jax.experimental.pallas import tpu as pltpu
from jax.sharding import PartitionSpec as P

LANES = 128
CHUNK = 512
SPAN = 60.0
VMEM_BYTES = 48 * 1024 * 1024
FAR, NEAR = 2, 4
LINE, RING, CORES = 4, 8, 2


def dot(a, b, dims):
    return lax.dot_general(a, b, (dims, ((), ())), preferred_element_type=jnp.float32)


def params():
    return pltpu.CompilerParams(vmem_limit_bytes=VMEM_BYTES)


def cost(flops, nbytes, exps):
    return pl.CostEstimate(flops=flops, bytes_accessed=nbytes, transcendentals=exps)


def mirror(value):
    perm = []
    for l in range(LINE):
        for g in range(RING * CORES):
            for n in range(FAR * NEAR):
                to = ((LINE - 1 - l) * RING * CORES + g) * FAR * NEAR + (n + NEAR) % (FAR * NEAR)
                perm.append(((l * RING * CORES + g) * FAR * NEAR + n, to))
    return lax.ppermute(value, ("dp", "neg"), perm)


def other_core(value):
    perm = [(index, index ^ 1) for index in range(LINE * RING * CORES)]
    return lax.ppermute(value, "dp", perm)


def lookup_kernel(
    place_ref, counts_ref, neg_ids_ref, pos_ids_ref, queries_ref, pos_ref, negatives_ref,
    corr_ref, score_ref, order_ref,
):
    counts = counts_ref[...].astype(jnp.float32)
    high = jnp.floor(counts * 0.125)
    digits = jnp.concatenate([high, counts - 8.0 * high], axis=1)
    table = digits.T.astype(jnp.bfloat16)
    table_rows = counts_ref.shape[0]
    total = negatives_ref.shape[0]
    block = total // (LINE * RING * CORES)
    place = place_ref[0]
    core = place & (CORES - 1)

    def corrections(ids):
        row = ids >> 7
        column = ids & (LANES - 1)
        width = ids.shape[1]
        spots = lax.broadcasted_iota(jnp.int32, (table_rows, width), 0)
        hot = jnp.where(spots == row, 1.0, 0.0).astype(jnp.bfloat16)
        found = dot(table, hot, ((1,), (0,)))
        value = 8.0 * found[:LANES] + found[LANES:]
        lanes = lax.broadcasted_iota(jnp.int32, (LANES, width), 0)
        picked = jnp.sum(jnp.where(lanes == column, value, 0.0), axis=0, keepdims=True)
        return jnp.log(picked)

    def target(index):
        l, r, c = index // (RING * CORES), (index // CORES) % RING, index % CORES
        away = (c - core) & (CORES - 1)
        return pl.ds(pl.multiple_of((away * LINE + l) * RING * block, block) + r * block, block)

    for k in range(neg_ids_ref.shape[0]):
        corr = corrections(neg_ids_ref[k : k + 1, :])
        tall = jnp.broadcast_to(corr, (LANES, LANES)).T
        for b in range(LANES // block):
            rows = target(k * (LANES // block) + b)
            corr_ref[rows, :] = tall[b * block : (b + 1) * block, :]
    for k in range(total // block):
        order_ref[target(k), :] = negatives_ref[k * block : (k + 1) * block, :]
    products = queries_ref[...].astype(jnp.float32) * pos_ref[...].astype(jnp.float32)
    scores = jnp.sum(products.T, axis=0, keepdims=True)
    for k in range(pos_ids_ref.shape[0]):
        corr = corrections(pos_ids_ref[k : k + 1, :])
        lanes = slice(k * LANES, (k + 1) * LANES)
        score_ref[:, lanes] = scores[:, lanes] - corr


def wide(block, width):
    return jnp.concatenate([block] * (width // LANES), axis=1)


def row_stats(block, negatives_ref, corr_ref):
    rows = block.shape[0]
    top = None
    for start in range(0, negatives_ref.shape[0], CHUNK):
        part = slice(start, start + CHUNK)
        scores = dot(negatives_ref[part, :], block, ((1,), (1,)))
        scores = scores - wide(corr_ref[part, :], rows)
        tiles = scores.reshape(CHUNK // 8, 8, rows)
        best = jnp.max(tiles, axis=0)
        if top is None:
            top = best
            mass = jnp.sum(jnp.exp(tiles - top[None]), axis=0)
        else:
            new = jnp.maximum(top, best)
            mass = mass * jnp.exp(top - new) + jnp.sum(jnp.exp(tiles - new[None]), axis=0)
            top = new
    row_max = jnp.max(top, axis=0, keepdims=True)
    return row_max, jnp.sum(mass * jnp.exp(top - row_max), axis=0, keepdims=True)


def near_stats_kernel(spot_ref, queries_ref, negatives_ref, corr_ref, score_ref, out_ref):
    score = score_ref[...]
    for k in range(NEAR):
        row_max, row_sum = row_stats(queries_ref[k], negatives_ref, corr_ref)
        own = spot_ref[0] == k
        joined = jnp.where(own, jnp.maximum(row_max, score), row_max)
        extra = jnp.exp(jnp.where(own, score, joined) - joined)
        row_sum = row_sum * jnp.exp(row_max - joined) + jnp.where(own, extra, 0.0)
        out_ref[k : k + 1, :] = joined + jnp.log(row_sum)


def far_stats_kernel(queries_ref, negatives_ref, corr_ref, near_ref, out_ref):
    for c in range(NEAR):
        out_ref[c, :NEAR, :] = near_ref[...]
    for k in range(NEAR):
        row_max, row_sum = row_stats(queries_ref[k], negatives_ref, corr_ref)
        lse = row_max + jnp.log(row_sum)
        for c in range(NEAR):
            out_ref[c, NEAR + k : NEAR + k + 1, :] = lse


def join_kernel(parts_ref, out_ref):
    top = parts_ref[0]
    for c in range(1, NEAR):
        top = jnp.maximum(top, parts_ref[c])
    total = jnp.exp(parts_ref[0] - top)
    for c in range(1, NEAR):
        total = total + jnp.exp(parts_ref[c] - top)
    out_ref[...] = top + jnp.log(total)


def grads_kernel(
    spot_ref, near_ref, far_ref, parts_ref, joined_ref, other_ref, negatives_ref, turned_ref,
    corr_ref, query_out, keep_out, send_out, lse_out, share_out,
):
    total = negatives_ref.shape[0]
    spot = spot_ref[0]
    joined = joined_ref[...]
    other = jnp.concatenate([other_ref[NEAR:, :], other_ref[:NEAR, :]], axis=0)
    top = jnp.maximum(joined, other)
    lse_out[...] = top + jnp.log(jnp.exp(joined - top) + jnp.exp(other - top))
    lse_all = lse_out[...]
    local = parts_ref[spot]
    boost = jnp.exp(jnp.minimum(lse_all - local, SPAN))
    own = lse_out[pl.ds(spot, 1), :]
    mirrored = lse_out[pl.ds(spot + NEAR, 1), :]
    sent = jnp.minimum(mirrored - joined_ref[pl.ds(spot + NEAR, 1), :], SPAN)
    for c in range(NEAR):
        part = jnp.minimum(own - parts_ref[c, pl.ds(spot, 1), :], SPAN)
        share_out[c, 0] = jnp.exp(-part)
        part = jnp.minimum(mirrored - parts_ref[c, pl.ds(spot + NEAR, 1), :], SPAN)
        share_out[c, 1] = jnp.exp(sent - part)
    half = total // CORES
    for k in range(FAR * NEAR):
        block = near_ref[k] if k < NEAR else far_ref[k - NEAR]
        rows = block.shape[0]
        lse = lse_all[k : k + 1, :]
        query_total = None
        for start in range(0, total, CHUNK):
            part = slice(start, start + CHUNK)
            scores = dot(negatives_ref[part, :], block, ((1,), (1,)))
            scores = scores - wide(corr_ref[part, :], rows)
            weight = jnp.exp(scores - lse).astype(jnp.bfloat16)
            neg_term = dot(weight, block, ((1,), (0,)))
            out, place = (keep_out, start) if start < half else (send_out, start - half)
            place = slice(place, place + CHUNK)
            if k > 0:
                neg_term = out[place, :] + neg_term
            out[place, :] = neg_term
            term = dot(turned_ref[:, part], weight, ((1,), (0,)))
            query_total = term if query_total is None else query_total + term
        query_out[k % NEAR, k // NEAR] = query_total * boost[k : k + 1, :]


def sum_cores_kernel(keep_ref, got_ref, out_ref):
    total = keep_ref[...] + got_ref[...]
    top = jnp.max(jnp.max(jnp.abs(total), axis=0, keepdims=True), axis=1, keepdims=True)
    power = jnp.clip(jnp.floor(jnp.log2(jnp.maximum(top, 1e-30))), -99.0, 99.0)
    scaled = total * jnp.exp2(13.0 - power)
    count, padded, width = out_ref.shape
    block = total.shape[0] // count
    for k in range(count):
        out_ref[k, :block, :] = scaled[k * block : (k + 1) * block, :]
        out_ref[k, block:, :] = jnp.broadcast_to(power, (padded - block, width))


def finish_kernel(
    spot_ref, own_ref, far_ref, pos_ref, score_ref, lse_ref, other_ref, grad_ref, loss_ref
):
    spot = spot_ref[0]
    lse = lse_ref[pl.ds(spot, 1), :]
    share = jnp.exp(-jnp.minimum(lse - other_ref[pl.ds(spot + NEAR, 1), :], SPAN))
    score = score_ref[...]
    pos_weight = jnp.exp(score - lse)
    turned = own_ref[...] + far_ref[...] * share
    turned = turned + (pos_weight - 1.0) * pos_ref[...].astype(jnp.float32).T
    grad_ref[...] = turned.T
    loss_ref[...] = lse - score


def trade(value, axis, groups):
    return lax.all_to_all(value, axis, 0, 0, tiled=True, axis_index_groups=groups)


def per_device(queries, positives, negatives, pos_ids, neg_ids, counts):
    own, width = queries.shape
    shard = negatives.shape[0]
    parts = FAR * NEAR
    f32, f16 = jnp.float32, jnp.float16
    like = jax.ShapeDtypeStruct
    place = lax.axis_index("dp").astype(jnp.int32).reshape(1)
    spot = (lax.axis_index("neg").astype(jnp.int32) % NEAR).reshape(1)
    smem = pl.BlockSpec(memory_space=pltpu.SMEM)
    vmem = pl.BlockSpec(memory_space=pltpu.VMEM)
    rows = [[f * NEAR + n for n in range(NEAR)] for f in range(FAR)]
    sheets = [[g * CORES + c for g in range(LINE * RING)] for c in range(CORES)]

    def spread(value):
        return trade(jnp.broadcast_to(value[None], (NEAR,) + value.shape), "neg", rows)

    across = mirror(queries)
    near_blocks = spread(queries)
    far_blocks = spread(across)

    corr, score, ordered = pl.pallas_call(
        lookup_kernel,
        in_specs=[smem] + [vmem] * 6,
        out_specs=(vmem, vmem, vmem),
        out_shape=(
            like((shard, LANES), f32),
            like((1, own), f32),
            like((shard, width), jnp.bfloat16),
        ),
        compiler_params=params(),
        cost_estimate=cost(10**9, 2 * 10**6, 4096),
        name="lookup",
    )(
        place,
        counts.reshape(-1, LANES),
        neg_ids.reshape(-1, LANES),
        pos_ids.reshape(-1, LANES),
        queries,
        positives,
        negatives,
    )
    turned = ordered.T

    pairs = parts * own * shard
    near_stats = pl.pallas_call(
        near_stats_kernel,
        in_specs=[smem] + [vmem] * 4,
        out_specs=vmem,
        out_shape=like((NEAR, own), f32),
        compiler_params=params(),
        cost_estimate=cost(pairs * width, 2 * 10**6, pairs // 2),
        name="near_stats",
    )(spot, near_blocks, ordered, corr, score)
    stats = pl.pallas_call(
        far_stats_kernel,
        in_specs=[vmem] * 4,
        out_specs=vmem,
        out_shape=like((NEAR, parts, own), f32),
        compiler_params=params(),
        cost_estimate=cost(pairs * width, 2 * 10**6, pairs // 2),
        name="far_stats",
    )(far_blocks, ordered, corr, near_stats)
    stats = trade(stats, "neg", rows)
    joined = pl.pallas_call(
        join_kernel,
        in_specs=[vmem],
        out_specs=vmem,
        out_shape=like((parts, own), f32),
        compiler_params=params(),
        name="join",
    )(stats)
    other = mirror(joined)

    query_terms, keep, send, lse, share = pl.pallas_call(
        grads_kernel,
        in_specs=[smem] + [vmem] * 8,
        out_specs=(vmem,) * 5,
        out_shape=(
            like((NEAR, FAR, width, own), f32),
            like((shard // CORES, width), f32),
            like((shard // CORES, width), f32),
            like((parts, own), f32),
            like((NEAR, FAR, 1, own), f32),
        ),
        compiler_params=params(),
        cost_estimate=cost(6 * pairs * width, 8 * 10**6, pairs),
        name="grads",
    )(spot, near_blocks, far_blocks, stats, joined, other, ordered, turned, corr)

    query_acc = trade(query_terms.astype(f16), "neg", rows)
    query_acc = jnp.sum(query_acc.astype(f32) * share, axis=0)
    query_far = mirror(query_acc[1].astype(f16)).astype(f32)

    count = LINE * RING
    block = shard // CORES // count
    neg_acc = pl.pallas_call(
        sum_cores_kernel,
        in_specs=[vmem] * 2,
        out_specs=vmem,
        out_shape=like((count, block + 8, width), f32),
        compiler_params=params(),
        name="sum_cores",
    )(keep, other_core(send))
    neg_acc = trade(neg_acc.astype(f16), "dp", sheets).astype(f32)
    power = jnp.exp2(neg_acc[:, block : block + 1, :1] - 13.0)
    neg_grad = jnp.sum(neg_acc[:, :block, :] * power, axis=0)

    query_grad, row_loss = pl.pallas_call(
        finish_kernel,
        in_specs=[smem] + [vmem] * 6,
        out_specs=(vmem, vmem),
        out_shape=(like((own, width), f32), like((1, own), f32)),
        compiler_params=params(),
        name="finish",
    )(spot, query_acc[0], query_far, positives, score, lse, other)
    return (query_grad, row_loss.reshape(own), neg_grad)


def solution(mesh):
    placed = (
        P(("dp", "neg"), None),
        P(("dp", "neg"), None),
        P("neg", None),
        P(("dp", "neg")),
        P("neg"),
        P(),
    )
    return jax.shard_map(
        per_device,
        mesh=mesh,
        in_specs=placed,
        out_specs=(P(("dp", "neg"), None), P(("dp", "neg")), P(("neg", "dp"), None)),
        check_vma=False,
    )
```

time: 629 us -> 122 us (0.19)
  the two profiles are of different devices: /device:TPU:4 before, /device:TPU:2 now
where the time goes in v1:
time: 122 us; the launch traced here: 121 us
  starting transfers between devices  44.9 us (37%)
  waiting for transfers between devices  35.4 us (29%)
  Pallas kernels  17.9 us (15%)
  local copies, waits for them, and re-layouts  8.87 us (7%)
  blocking collectives  8.46 us (7%)
  other arithmetic  5.13 us (4%)
    all_to_all x4, starting transfers between devices, trade(): lax.all_to_all(value, axis, 0, 0, tiled=True, axis_index_groups=groups)  31 us
    all_to_all x4, waiting for transfers between devices, trade(): lax.all_to_all(value, axis, 0, 0, tiled=True, axis_index_groups=groups)  23.4 us
    ppermute x3, starting transfers between devices, mirror(): return lax.ppermute(value, ('dp', 'neg'), perm)  12 us
    ppermute x3, waiting for transfers between devices, mirror(): return lax.ppermute(value, ('dp', 'neg'), perm)  12 us
    pallas_call x1, Pallas kernels, per_device(): pl.pallas_call(grads_kernel, in_specs=[smem] + [vmem] * 8, out_specs=(vme...  9.9 us
    all_to_all x1, blocking collectives, trade(): lax.all_to_all(value, axis, 0, 0, tiled=True, axis_index_groups=groups)  8.46 us
    unnamed x25, local copies, waits for them, and re-layouts  5.53 us
    convert_element_type x1, other arithmetic, per_device(): query_acc = trade(query_terms.astype(f16), 'neg', rows)  2.74 us
  transfers between devices with their start and end apart: 8, of which 6 were waited for; matrix products, arithmetic and copies ran while one was open for 4% of the time, Pallas kernels for 4%

profile of v1, /device:TPU:2, one launch (start us, length us, event | category | flops | bytes accessed | tf_op | source)
XLA Modules:
  0.0 121.5 jit_solution(6883853887688345562)
XLA Ops:
  0.6 0.0 copy-start.4
  0.6 0.0 copy-start.5
  0.7 0.0 copy-start.7
  0.7 0.0 copy-start.8
  0.7 0.0 copy-start.9
  0.7 1.8 %broadcast_in_dim.4 = bf16[4,256,256]{2,1,0:T(8,128)(2,1)} broadcast(bf16[256,256]{1,0:T(8,128)(2,1)} %queries_ref.1), dimensions={1,2} | broadcast | bytes 655360 | tf_op jit(solution)/shard_map/broadcast_in_dim | solution.py:232
  2.5 9.3 %all-to-all-start = ((bf16[4,256,256]{2,1,0:T(8,128)(2,1)}), bf16[4,256,256]{2,1,0:T(8,128)(2,1)S(1)}, u32[]{:S(2)}, u32[]{:S(2)}) async-start(bf16[4,256,256]{2,1,0:T(8,128)(2,1)} %broadcast_in_dim.4), calls=%async_computation | async-start | bytes 1048576 | tf_op jit(solution)/shard_map/all_to_all | solution.py:215
  11.8 1.9 %collective-permute-start = (bf16[256,256]{1,0:T(8,128)(2,1)}, bf16[256,256]{1,0:T(8,128)(2,1)S(1)}, u32[]{:S(2)}, u32[]{:S(2)}) collective-permute-start(bf16[256,256]{1,0:T(8,128)(2,1)} %queries_ref.1), channel_id=1, source_target_pairs={{0,388},{1,389},{2,390},{3,391},{4,384},{5,385},{6,386},{7,387},{8... | collective-permute-start | bytes 393224 | tf_op jit(solution)/shard_map/ppermute | solution.py:35
  13.8 6.4 %collective-permute-done = bf16[256,256]{1,0:T(8,128)(2,1)S(1)} collective-permute-done((bf16[256,256]{1,0:T(8,128)(2,1)}, bf16[256,256]{1,0:T(8,128)(2,1)S(1)}, u32[]{:S(2)}, u32[]{:S(2)}) %collective-permute-start) | collective-permute-done | bytes 131104 | tf_op jit(solution)/shard_map/ppermute | solution.py:35
  20.1 0.0 all-to-all-done.queries_ref.near_ref
  20.1 0.9 broadcast_in_dim.5
  21.0 4.8 %all-to-all-start.1 = ((bf16[4,256,256]{2,1,0:T(8,128)(2,1)}), bf16[4,256,256]{2,1,0:T(8,128)(2,1)S(1)}, u32[]{:S(2)}, u32[]{:S(2)}) async-start(bf16[4,256,256]{2,1,0:T(8,128)(2,1)} %broadcast_in_dim.5), calls=%async_computation.1 | async-start | bytes 1048576 | tf_op jit(solution)/shard_map/all_to_all | solution.py:215
  25.8 0.0 copy-done.4
  25.8 0.0 copy-done.7
  25.8 0.0 copy-done.8
  25.8 0.0 copy-done.9
  25.8 0.0 copy-start.6
  25.8 1.2 %copy-done.6 = bf16[2048,256]{1,0:T(8,128)(2,1)S(1)} copy-done((bf16[2048,256]{1,0:T(8,128)(2,1)S(1)}, bf16[2048,256]{1,0:T(8,128)(2,1)}, u32[]{:S(2)}) %copy-start.6) | copy-done | bytes 1048600
  27.1 1.5 %lookup.1 = (f32[2048,128]{1,0:T(8,128)S(1)}, f32[1,256]{1,0:T(1,128)S(1)}, bf16[2048,256]{1,0:T(8,128)(2,1)S(1)}) custom-call(s32[1]{0:T(128)} %bitcast.1.place_ref, s32[512,128]{1,0:T(8,128)S(1)} %bitcast.15, s32[16,128]{1,0:T(8,128)S(1)} %bitcast.16, s32[2,128]{1,0:T(2,128)S(1)} %bitcast.17, bf16[256,256]{1,0:T(8,128)(2,1)S(1)} %copy-done.4, ...), custom_call_target="tpu_custom_call" | custom-call | flops 1000000000 | bytes 2000000 | tf_op jit(solution)/shard_map/lookup/pallas_call | solution.py:238
  28.6 0.0 copy-done
  28.6 2.7 %near_stats.1.near_ref = f32[4,256]{1,0:T(4,128)S(1)} custom-call(s32[1]{0:T(128)} %bitcast.spot_ref, bf16[4,256,256]{2,1,0:T(8,128)(2,1)S(1)} %all-to-all-done.queries_ref.near_ref, bf16[2048,256]{1,0:T(8,128)(2,1)S(1)} %get-tuple-element.13.negatives_ref, f32[2048,128]{1,0:T(8,128)S(1)} %get-tuple-element.14.corr_ref, f32[1,256]{1,0:T(1,128)S(1)} %get-tuple-element.15.score_ref), custom_call_target="tpu_custom_call" | custom-call | flops 1073741824 | bytes 2000000 | tf_op jit(solution)/shard_map/near_stats/pallas_call | solution.py:262
  31.3 1.0 copy-done.10
  32.3 0.1 all-to-all-done.1.queries_ref.far_ref
  32.4 1.2 %copy-done.11 = f32[2048,128]{1,0:T(8,128)S(1)} copy-done((f32[2048,128]{1,0:T(8,128)S(1)}, f32[2048,128]{1,0:T(8,128)}, u32[]{:S(2)}) %copy-start.11) | copy-done | bytes 1048600
  33.7 2.5 %far_stats.1 = f32[4,8,256]{2,1,0:T(8,128)S(1)} custom-call(bf16[4,256,256]{2,1,0:T(8,128)(2,1)S(1)} %all-to-all-done.1.queries_ref.far_ref, bf16[2048,256]{1,0:T(8,128)(2,1)S(1)} %get-tuple-element.13.negatives_ref, f32[2048,128]{1,0:T(8,128)S(1)} %copy-done.11, f32[4,256]{1,0:T(4,128)S(1)} %near_stats.1.near_ref), custom_call_target="tpu_custom_call" | custom-call | flops 1073741824 | bytes 2000000 | tf_op jit(solution)/shard_map/far_stats/pallas_call | solution.py:271
  36.2 8.5 %all_to_all.25.parts_ref = f32[4,8,256]{2,1,0:T(8,128)S(1)} all-to-all(f32[4,8,256]{2,1,0:T(8,128)S(1)} %far_stats.1), channel_id=1, replica_groups={{0,1,2,3},{4,5,6,7},{8,9,10,11},{12,13,14,15},{16,17,18,19},{20,21,22,2..., dimensions={0} | all-to-all | bytes 65536 | tf_op jit(solution)/shard_map/all_to_all | solution.py:215
  44.6 3.8 %collective-permute-start.1 = (f32[8,256]{1,0:T(8,128)S(1)}, f32[8,256]{1,0:T(8,128)S(1)}, u32[]{:S(2)}, u32[]{:S(2)}) collective-permute-start(f32[8,256]{1,0:T(8,128)S(1)} %join.1.joined_ref), channel_id=1, source_target_pairs={{0,388},{1,389},{2,390},{3,391},{4,384},{5,385},{6,386},{7,387},{8... | collective-permute-start | bytes 24584 | tf_op jit(solution)/shard_map/ppermute | solution.py:35
  48.5 0.6 copy.10
  49.2 2.3 %collective-permute-done.1.other_ref = f32[8,256]{1,0:T(8,128)S(1)} collective-permute-done((f32[8,256]{1,0:T(8,128)S(1)}, f32[8,256]{1,0:T(8,128)S(1)}, u32[]{:S(2)}, u32[]{:S(2)}) %collective-permute-start.1) | collective-permute-done | bytes 8224 | tf_op jit(solution)/shard_map/ppermute | solution.py:35
  51.4 1.0 copy-done.1
  52.4 1.0 copy-done.3
  53.5 9.9 %grads.1 = (f32[4,2,256,256]{3,2,1,0:T(8,128)}, f32[1024,256]{1,0:T(8,128)S(1)}, f32[1024,256]{1,0:T(8,128)}, f32[8,256]{1,0:T(8,128)S(1)}, f32[4,2,1,256]{3,2,1,0:T(1,128)S(1)}) custom-call(s32[1]{0:T(128)} %bitcast.spot_ref, bf16[4,256,256]{2,1,0:T(8,128)(2,1)S(1)} %copy-done.1, bf16[4,256,256]{2,1,0:T(8,128)(2,1)S(1)} %copy-done.3, ...), custom_call_target="tpu_custom_call" | custom-call | flops 6442450944 | bytes 8000000 | tf_op jit(solution)/shard_map/grads/pallas_call | solution.py:291
  63.4 1.9 %collective-permute-start.3 = (f32[1024,256]{1,0:T(8,128)}, f32[1024,256]{1,0:T(8,128)S(1)}, u32[]{:S(2)}, u32[]{:S(2)}) collective-permute-start(f32[1024,256]{1,0:T(8,128)} %get-tuple-element.22), channel_id=1, source_target_pairs={{0,8},{8,0},{16,24},{24,16},{32,40},{40,32},{48,56},{56,48},{64,72... | collective-permute-start | bytes 3145736 | tf_op jit(solution)/shard_map/ppermute | solution.py:40
  65.3 2.7 %convert_element_type.19 = f16[4,2,256,256]{3,2,1,0:T(8,128)(2,1)} convert(f32[4,2,256,256]{3,2,1,0:T(8,128)} %get-tuple-element.16) | non-fusion elementwise | flops 524288 | bytes 3145728 | tf_op jit(solution)/shard_map/convert_element_type | solution.py:307
  68.0 4.9 %all-to-all-start.3 = ((f16[4,2,256,256]{3,2,1,0:T(8,128)(2,1)}), f16[4,2,256,256]{3,2,1,0:T(8,128)(2,1)S(1)}, u32[]{:S(2)}, u32[]{:S(2)}) async-start(f16[4,2,256,256]{3,2,1,0:T(8,128)(2,1)} %convert_element_type.19), calls=%async_computation.3 | async-start | bytes 2097152 | tf_op jit(solution)/shard_map/all_to_all | solution.py:215
  73.0 0.0 collective-permute-done.3.got_ref
  73.0 0.3 sum_cores.1
  73.3 1.0 convert_element_type.23
  74.2 13.3 %all-to-all-done.3 = f16[4,2,256,256]{3,2,1,0:T(8,128)(2,1)S(1)} async-done(((f16[4,2,256,256]{3,2,1,0:T(8,128)(2,1)}), f16[4,2,256,256]{3,2,1,0:T(8,128)(2,1)S(1)}, u32[]{:S(2)}, u32[]{:S(2)}) %all-to-all-start.3) | async-done | bytes 1048608 | tf_op jit(solution)/shard_map/all_to_all | solution.py:215
  87.6 11.9 %all-to-all-start.4 = ((f16[32,40,256]{2,1,0:T(8,128)(2,1)}), f16[32,40,256]{2,1,0:T(8,128)(2,1)S(1)}, u32[]{:S(2)}, u32[]{:S(2)}) async-start(f16[32,40,256]{2,1,0:T(8,128)(2,1)} %convert_element_type.23), calls=%async_computation.4 | async-start | bytes 1310720 | tf_op jit(solution)/shard_map/all_to_all | solution.py:215
  99.5 0.2 multiply_reduce_fusion
  99.7 6.3 %collective-permute-start.2 = (f16[256,256]{1,0:T(8,128)(2,1)S(1)}, f16[256,256]{1,0:T(8,128)(2,1)S(1)}, u32[]{:S(2)}, u32[]{:S(2)}) collective-permute-start(f16[256,256]{1,0:T(8,128)(2,1)S(1)} %get-tuple-element.23), channel_id=1, source_target_pairs={{0,388},{1,389},{2,390},{3,391},{4,384},{5,385},{6,386},{7,387},{8... | collective-permute-start | bytes 393224 | tf_op jit(solution)/shard_map/ppermute | solution.py:35
  106.0 3.4 %collective-permute-done.2 = f16[256,256]{1,0:T(8,128)(2,1)S(1)} collective-permute-done((f16[256,256]{1,0:T(8,128)(2,1)S(1)}, f16[256,256]{1,0:T(8,128)(2,1)S(1)}, u32[]{:S(2)}, u32[]{:S(2)}) %collective-permute-start.2) | collective-permute-done | bytes 131104 | tf_op jit(solution)/shard_map/ppermute | solution.py:35
  109.5 0.9 finish.1
  110.4 9.9 %all-to-all-done.4 = f16[32,40,256]{2,1,0:T(8,128)(2,1)S(1)} async-done(((f16[32,40,256]{2,1,0:T(8,128)(2,1)}), f16[32,40,256]{2,1,0:T(8,128)(2,1)S(1)}, u32[]{:S(2)}, u32[]{:S(2)}) %all-to-all-start.4) | async-done | bytes 655392 | tf_op jit(solution)/shard_map/all_to_all | solution.py:215
  120.3 0.1 convert_element_type.24
  120.4 0.3 fusion.4
  120.7 0.8 fusion
  (12 shorter events, 0.1 us)
Async XLA Ops:
  0.6 25.2 %copy-start.4 = (bf16[256,256]{1,0:T(8,128)(2,1)S(1)}, bf16[256,256]{1,0:T(8,128)(2,1)}, u32[]{:S(2)}) copy-start(bf16[256,256]{1,0:T(8,128)(2,1)} %queries_ref.1) | copy-start | bytes 393220
  0.6 25.2 %copy-start.5 = (bf16[256,256]{1,0:T(8,128)(2,1)S(1)}, bf16[256,256]{1,0:T(8,128)(2,1)}, u32[]{:S(2)}) copy-start(bf16[256,256]{1,0:T(8,128)(2,1)} %pos_ref.3) | copy-start | bytes 393220
  0.7 25.2 %copy-start.7 = (s32[65536]{0:T(1024)S(1)}, s32[65536]{0:T(1024)}, u32[]{:S(2)}) copy-start(s32[65536]{0:T(1024)} %param.11) | copy-start | bytes 786436
  0.7 25.1 %copy-start.8 = (s32[2048]{0:T(1024)S(1)}, s32[2048]{0:T(1024)}, u32[]{:S(2)}) copy-start(s32[2048]{0:T(1024)} %param.10) | copy-start | bytes 24580
  0.7 25.1 %copy-start.9 = (s32[256]{0:T(256)S(1)}, s32[256]{0:T(256)}, u32[]{:S(2)}) copy-start(s32[256]{0:T(256)} %param.9) | copy-start | bytes 3076
  2.5 17.6 %all-to-all-start = ((bf16[4,256,256]{2,1,0:T(8,128)(2,1)}), bf16[4,256,256]{2,1,0:T(8,128)(2,1)S(1)}, u32[]{:S(2)}, u32[]{:S(2)}) async-start(bf16[4,256,256]{2,1,0:T(8,128)(2,1)} %broadcast_in_dim.4), calls=%async_computation | async-start | bytes 1048576 | tf_op jit(solution)/shard_map/all_to_all | solution.py:215
  11.8 8.3 %collective-permute-start = (bf16[256,256]{1,0:T(8,128)(2,1)}, bf16[256,256]{1,0:T(8,128)(2,1)S(1)}, u32[]{:S(2)}, u32[]{:S(2)}) collective-permute-start(bf16[256,256]{1,0:T(8,128)(2,1)} %queries_ref.1), channel_id=1, source_target_pairs={{0,388},{1,389},{2,390},{3,391},{4,384},{5,385},{6,386},{7,387},{8... | collective-permute-start | bytes 393224 | tf_op jit(solution)/shard_map/ppermute | solution.py:35
  20.1 8.5 %copy-start = (bf16[4,256,256]{2,1,0:T(8,128)(2,1)}, bf16[4,256,256]{2,1,0:T(8,128)(2,1)S(1)}, u32[]{:S(2)}) copy-start(bf16[4,256,256]{2,1,0:T(8,128)(2,1)S(1)} %all-to-all-done.queries_ref.near_ref) | copy-start | bytes 1572868
  21.0 11.4 %all-to-all-start.1 = ((bf16[4,256,256]{2,1,0:T(8,128)(2,1)}), bf16[4,256,256]{2,1,0:T(8,128)(2,1)S(1)}, u32[]{:S(2)}, u32[]{:S(2)}) async-start(bf16[4,256,256]{2,1,0:T(8,128)(2,1)} %broadcast_in_dim.5), calls=%async_computation.1 | async-start | bytes 1048576 | tf_op jit(solution)/shard_map/all_to_all | solution.py:215
  25.8 1.2 %copy-start.6 = (bf16[2048,256]{1,0:T(8,128)(2,1)S(1)}, bf16[2048,256]{1,0:T(8,128)(2,1)}, u32[]{:S(2)}) copy-start(bf16[2048,256]{1,0:T(8,128)(2,1)} %negatives_ref.1) | copy-start | bytes 3145732
  31.3 1.0 copy-start.10
  32.4 1.2 %copy-start.11 = (f32[2048,128]{1,0:T(8,128)S(1)}, f32[2048,128]{1,0:T(8,128)}, u32[]{:S(2)}) copy-start(f32[2048,128]{1,0:T(8,128)} %copy-done.10) | copy-start | bytes 3145732
  33.7 15.5 %copy-start.2 = (bf16[4,256,256]{2,1,0:T(8,128)(2,1)}, bf16[4,256,256]{2,1,0:T(8,128)(2,1)S(1)}, u32[]{:S(2)}) copy-start(bf16[4,256,256]{2,1,0:T(8,128)(2,1)S(1)} %all-to-all-done.1.queries_ref.far_ref) | copy-start | bytes 1572868
  44.6 6.8 %collective-permute-start.1 = (f32[8,256]{1,0:T(8,128)S(1)}, f32[8,256]{1,0:T(8,128)S(1)}, u32[]{:S(2)}, u32[]{:S(2)}) collective-permute-start(f32[8,256]{1,0:T(8,128)S(1)} %join.1.joined_ref), channel_id=1, source_target_pairs={{0,388},{1,389},{2,390},{3,391},{4,384},{5,385},{6,386},{7,387},{8... | collective-permute-start | bytes 24584 | tf_op jit(solution)/shard_map/ppermute | solution.py:35
  51.4 1.0 copy-start.1
  52.4 1.0 copy-start.3
  63.4 9.6 %collective-permute-start.3 = (f32[1024,256]{1,0:T(8,128)}, f32[1024,256]{1,0:T(8,128)S(1)}, u32[]{:S(2)}, u32[]{:S(2)}) collective-permute-start(f32[1024,256]{1,0:T(8,128)} %get-tuple-element.22), channel_id=1, source_target_pairs={{0,8},{8,0},{16,24},{24,16},{32,40},{40,32},{48,56},{56,48},{64,72... | collective-permute-start | bytes 3145736 | tf_op jit(solution)/shard_map/ppermute | solution.py:40
  68.0 19.5 %all-to-all-start.3 = ((f16[4,2,256,256]{3,2,1,0:T(8,128)(2,1)}), f16[4,2,256,256]{3,2,1,0:T(8,128)(2,1)S(1)}, u32[]{:S(2)}, u32[]{:S(2)}) async-start(f16[4,2,256,256]{3,2,1,0:T(8,128)(2,1)} %convert_element_type.19), calls=%async_computation.3 | async-start | bytes 2097152 | tf_op jit(solution)/shard_map/all_to_all | solution.py:215
  87.6 32.7 %all-to-all-start.4 = ((f16[32,40,256]{2,1,0:T(8,128)(2,1)}), f16[32,40,256]{2,1,0:T(8,128)(2,1)S(1)}, u32[]{:S(2)}, u32[]{:S(2)}) async-start(f16[32,40,256]{2,1,0:T(8,128)(2,1)} %convert_element_type.23), calls=%async_computation.4 | async-start | bytes 1310720 | tf_op jit(solution)/shard_map/all_to_all | solution.py:215
  99.7 9.7 %collective-permute-start.2 = (f16[256,256]{1,0:T(8,128)(2,1)S(1)}, f16[256,256]{1,0:T(8,128)(2,1)S(1)}, u32[]{:S(2)}, u32[]{:S(2)}) collective-permute-start(f16[256,256]{1,0:T(8,128)(2,1)S(1)} %get-tuple-element.23), channel_id=1, source_target_pairs={{0,388},{1,389},{2,390},{3,391},{4,384},{5,385},{6,386},{7,387},{8... | collective-permute-start | bytes 393224 | tf_op jit(solution)/shard_map/ppermute | solution.py:35

commit v2 on v1

v2 whole, which is shorter than its diff:
```python
import functools
import jax
import jax.numpy as jnp
from jax import lax
from jax.experimental import pallas as pl
from jax.experimental.pallas import tpu as pltpu
from jax.sharding import PartitionSpec as P

LANES = 128
CHUNK = 512
SPLIT = 256
SPAN = 60.0
MIB = 1024 * 1024
FAR, NEAR = 2, 4
HALVING = (3, 1)
LINE, RING, CORES = 4, 8, 2


def dot(a, b, dims):
    return lax.dot_general(a, b, (dims, ((), ())), preferred_element_type=jnp.float32)


def params(mib=16):
    return pltpu.CompilerParams(vmem_limit_bytes=mib * MIB)


def cost(flops, nbytes, exps):
    return pl.CostEstimate(flops=flops, bytes_accessed=nbytes, transcendentals=exps)


def mirror(value):
    perm = []
    for l in range(LINE):
        for g in range(RING * CORES):
            for n in range(FAR * NEAR):
                to = ((LINE - 1 - l) * RING * CORES + g) * FAR * NEAR + (n + NEAR) % (FAR * NEAR)
                perm.append(((l * RING * CORES + g) * FAR * NEAR + n, to))
    return lax.ppermute(value, ("dp", "neg"), perm)


def swap_near(value, bits):
    perm = [(index, index ^ bits) for index in range(FAR * NEAR)]
    return lax.ppermute(value, "neg", perm)


def other_core(value):
    perm = [(index, index ^ 1) for index in range(LINE * RING * CORES)]
    return lax.ppermute(value, "dp", perm)


def lookup_kernel(
    place_ref, counts_ref, neg_ids_ref, pos_ids_ref, queries_ref, pos_ref, negatives_ref,
    corr_ref, score_ref, order_ref, tall_ref,
):
    counts = counts_ref[...].astype(jnp.float32)
    high = jnp.floor(counts * 0.125)
    digits = jnp.concatenate([high, counts - 8.0 * high], axis=1)
    table = digits.T.astype(jnp.bfloat16)
    table_rows = counts_ref.shape[0]
    total = negatives_ref.shape[0]
    block = total // (LINE * RING * CORES)
    place = place_ref[0]
    core = place & (CORES - 1)

    def corrections(ids):
        row = ids >> 7
        column = ids & (LANES - 1)
        width = ids.shape[1]
        spots = lax.broadcasted_iota(jnp.int32, (table_rows, width), 0)
        hot = jnp.where(spots == row, 1.0, 0.0).astype(jnp.bfloat16)
        found = dot(table, hot, ((1,), (0,)))
        value = 8.0 * found[:LANES] + found[LANES:]
        lanes = lax.broadcasted_iota(jnp.int32, (LANES, width), 0)
        picked = jnp.sum(jnp.where(lanes == column, value, 0.0), axis=0, keepdims=True)
        return jnp.log(picked)

    def target(index):
        l, r, c = index // (RING * CORES), (index // CORES) % RING, index % CORES
        away = (c - core) & (CORES - 1)
        return pl.ds(pl.multiple_of((away * LINE + l) * RING * block, block) + r * block, block)

    for k in range(neg_ids_ref.shape[0]):
        corr = corrections(neg_ids_ref[k : k + 1, :])
        tall = jnp.broadcast_to(corr, (LANES, LANES)).T
        for b in range(LANES // block):
            rows = target(k * (LANES // block) + b)
            tall_ref[rows, :] = tall[b * block : (b + 1) * block, :]
    for k in range(total // LANES):
        corr_ref[k : k + 1, :] = tall_ref[k * LANES : (k + 1) * LANES, :].T[:1, :]
    for k in range(total // block):
        order_ref[target(k), :] = negatives_ref[k * block : (k + 1) * block, :]
    products = queries_ref[...].astype(jnp.float32) * pos_ref[...].astype(jnp.float32)
    scores = jnp.sum(products.T, axis=0, keepdims=True)
    for k in range(pos_ids_ref.shape[0]):
        corr = corrections(pos_ids_ref[k : k + 1, :])
        lanes = slice(k * LANES, (k + 1) * LANES)
        score_ref[:, lanes] = scores[:, lanes] - corr


def wide(block, width):
    return jnp.concatenate([block] * (width // LANES), axis=1)


def row_stats(block, negatives_ref, corr_ref):
    rows = block.shape[0]
    top = None
    for start in range(0, negatives_ref.shape[0], CHUNK):
        part = slice(start, start + CHUNK)
        scores = dot(negatives_ref[part, :], block, ((1,), (1,)))
        scores = scores - wide(corr_ref[part, :], rows)
        tiles = scores.reshape(CHUNK // 8, 8, rows)
        best = jnp.max(tiles, axis=0)
        if top is None:
            top = best
            mass = jnp.sum(jnp.exp(tiles - top[None]), axis=0)
        else:
            new = jnp.maximum(top, best)
            mass = mass * jnp.exp(top - new) + jnp.sum(jnp.exp(tiles - new[None]), axis=0)
            top = new
    row_max = jnp.max(top, axis=0, keepdims=True)
    return row_max, jnp.sum(mass * jnp.exp(top - row_max), axis=0, keepdims=True)


def to_columns(rows_ref, out_ref):
    for k in range(rows_ref.shape[0]):
        tall = jnp.broadcast_to(rows_ref[k : k + 1, :], (LANES, LANES)).T
        out_ref[k * LANES : (k + 1) * LANES, :] = tall


def stats_kernel(
    spot_ref, blocks_hbm, negatives_ref, rows_ref, score_ref, out_ref, blocks_ref, corr_ref, sem
):
    fetch = pltpu.make_async_copy(blocks_hbm, blocks_ref, sem)
    fetch.start()
    to_columns(rows_ref, corr_ref)
    fetch.wait()
    score = score_ref[...]
    for side in range(FAR):
        for k in range(NEAR):
            row_max, row_sum = row_stats(blocks_ref[k, side], negatives_ref, corr_ref)
            if side == 0:
                own = spot_ref[0] == k
                joined = jnp.where(own, jnp.maximum(row_max, score), row_max)
                extra = jnp.exp(jnp.where(own, score, joined) - joined)
                row_sum = row_sum * jnp.exp(row_max - joined) + jnp.where(own, extra, 0.0)
                row_max = joined
            lse = row_max + jnp.log(row_sum)
            place = side * NEAR + k
            for c in range(NEAR):
                out_ref[c, place : place + 1, :] = lse


def join(parts):
    top = functools.reduce(jnp.maximum, parts)
    return top + jnp.log(sum(jnp.exp(part - top) for part in parts))


def join_kernel(parts_ref, out_ref):
    out_ref[...] = join([parts_ref[c] for c in range(NEAR)])


def grads_kernel(
    side, spot_ref, blocks_hbm, joined_ref, other_ref, negatives_ref, turned_ref, rows_ref, *refs
):
    sums, refs = refs[: 2 - 2 * side], refs[2 - 2 * side :]
    query_outs, refs = refs[: 2 - side], refs[2 - side :]
    keep_out, send_out, lse_out, boost_ref, weight_ref, blocks_ref, corr_ref, sem = refs
    fetch = pltpu.make_async_copy(blocks_hbm, blocks_ref, sem)
    fetch.start()
    to_columns(rows_ref, corr_ref)
    total = negatives_ref.shape[0]
    spot = spot_ref[0]
    offset = side * NEAR
    joined = joined_ref[offset : offset + NEAR, :]
    lse_all = join([joined, other_ref[NEAR - offset : 2 * NEAR - offset, :]])
    lse_out[...] = lse_all
    boost_ref[...] = jnp.exp(jnp.minimum(lse_all - joined, SPAN))
    places = list(range(NEAR)) if side else [spot ^ k for k in range(NEAR)]
    lse = jnp.concatenate([lse_out[pl.ds(k, 1), :] for k in places], axis=1)
    fetch.wait()
    block = jnp.concatenate([blocks_ref[k, side] for k in places], axis=0)
    rows = block.shape[0]
    own = rows // NEAR
    half = total // CORES
    for start in range(0, total, SPLIT):
        part = slice(start, start + SPLIT)
        scores = dot(negatives_ref[part, :], block, ((1,), (1,)))
        scores = scores - wide(corr_ref[part, :], rows)
        weight = jnp.exp(scores - lse).astype(jnp.bfloat16)
        weight_ref[part, :] = weight
        neg_term = dot(weight, block, ((1,), (0,)))
        which, place = start // half, slice(start % half, start % half + SPLIT)
        if sums:
            neg_term = sums[which][place, :] + neg_term
        (keep_out, send_out)[which][place, :] = neg_term
    first, onward = HALVING
    for index, k in enumerate(places):
        weight = weight_ref[:, index * own : (index + 1) * own]
        term = dot(turned_ref[...], weight, ((1,), (0,))) * boost_ref[pl.ds(k, 1), :]
        if side:
            query_outs[0][index] = term
        else:
            out = query_outs[index in (first, first ^ onward)]
            out[int(index in (onward, first ^ onward))] = term


def spread_kernel(near_ref, far_ref, out_ref):
    for k in range(NEAR):
        out_ref[k, 0] = near_ref[...]
        out_ref[k, 1] = far_ref[...]


def sum_cores_kernel(keep_ref, got_ref, out_ref):
    total = keep_ref[...] + got_ref[...]
    top = jnp.max(jnp.max(jnp.abs(total), axis=0, keepdims=True), axis=1, keepdims=True)
    power = jnp.clip(jnp.floor(jnp.log2(jnp.maximum(top, 1e-30))), -99.0, 99.0)
    scaled = total * jnp.exp2(13.0 - power)
    count, padded, width = out_ref.shape
    block = total.shape[0] // count
    for k in range(count):
        out_ref[k, :block, :] = scaled[k * block : (k + 1) * block, :]
        out_ref[k, block:, :] = jnp.broadcast_to(power, (padded - block, width))


def finish_kernel(
    spot_ref, near_ref, far_ref, pos_ref, score_ref, lse_ref, joined_ref, other_ref,
    grad_ref, loss_ref,
):
    spot = spot_ref[0]
    lse = lse_ref[pl.ds(spot, 1), :]
    near_share = jnp.exp(-jnp.minimum(lse - joined_ref[pl.ds(spot, 1), :], SPAN))
    far_share = jnp.exp(-jnp.minimum(lse - other_ref[pl.ds(spot + NEAR, 1), :], SPAN))
    score = score_ref[...]
    pos_weight = jnp.exp(score - lse)
    turned = near_ref[...] * near_share + far_ref[...] * far_share
    turned = turned + (pos_weight - 1.0) * pos_ref[...].astype(jnp.float32).T
    grad_ref[...] = turned.T
    loss_ref[...] = lse - score


def trade(value, axis, groups):
    return lax.all_to_all(value, axis, 0, 0, tiled=True, axis_index_groups=groups)


def per_device(queries, positives, negatives, pos_ids, neg_ids, counts):
    own, width = queries.shape
    shard = negatives.shape[0]
    parts = FAR * NEAR
    f32, f16 = jnp.float32, jnp.float16
    like = jax.ShapeDtypeStruct
    place = lax.axis_index("dp").astype(jnp.int32).reshape(1)
    spot = (lax.axis_index("neg").astype(jnp.int32) % NEAR).reshape(1)
    smem = pl.BlockSpec(memory_space=pltpu.SMEM)
    vmem = pl.BlockSpec(memory_space=pltpu.VMEM)
    hbm = pl.BlockSpec(memory_space=pltpu.HBM)
    rows = [[f * NEAR + n for n in range(NEAR)] for f in range(FAR)]
    sheets = [[g * CORES + c for g in range(LINE * RING)] for c in range(CORES)]

    across = mirror(queries)

    corr, score, ordered = pl.pallas_call(
        lookup_kernel,
        in_specs=[smem] + [vmem] * 6,
        out_specs=(vmem, vmem, vmem),
        out_shape=(
            like((shard // LANES, LANES), f32),
            like((1, own), f32),
            like((shard, width), jnp.bfloat16),
        ),
        scratch_shapes=[pltpu.VMEM((shard, LANES), f32)],
        compiler_params=params(),
        cost_estimate=cost(10**9, 2 * 10**6, 4096),
        name="lookup",
    )(
        place,
        counts.reshape(-1, LANES),
        neg_ids.reshape(-1, LANES),
        pos_ids.reshape(-1, LANES),
        queries,
        positives,
        negatives,
    )
    turned = ordered.T

    blocks = pl.pallas_call(
        spread_kernel,
        in_specs=[vmem] * 2,
        out_specs=vmem,
        out_shape=like((NEAR, FAR, own, width), jnp.bfloat16),
        compiler_params=params(),
        name="spread",
    )(queries, across)
    blocks = trade(blocks, "neg", rows)

    pairs = parts * own * shard
    fetched = [
        pltpu.VMEM((NEAR, FAR, own, width), jnp.bfloat16),
        pltpu.VMEM((shard, LANES), f32),
        pltpu.SemaphoreType.DMA,
    ]
    stats = pl.pallas_call(
        stats_kernel,
        in_specs=[smem, hbm] + [vmem] * 3,
        out_specs=vmem,
        out_shape=like((NEAR, parts, own), f32),
        scratch_shapes=fetched,
        compiler_params=params(),
        cost_estimate=cost(2 * pairs * width, 4 * 10**6, pairs),
        name="stats",
    )(spot, blocks, ordered, corr, score)
    joined = pl.pallas_call(
        join_kernel,
        in_specs=[vmem],
        out_specs=vmem,
        out_shape=like((parts, own), f32),
        compiler_params=params(),
        name="join",
    )(trade(stats, "neg", rows))
    other = mirror(joined)

    def grads(side, query_outs, *sums):
        neg_like = like((shard // CORES, width), f32)
        outs = [*query_outs, neg_like, neg_like, like((NEAR, own), f32)]
        return pl.pallas_call(
            functools.partial(grads_kernel, side),
            in_specs=[smem, hbm] + [vmem] * (5 + len(sums)),
            out_specs=(vmem,) * len(outs),
            out_shape=tuple(outs),
            scratch_shapes=[
                pltpu.VMEM((NEAR, own), f32),
                pltpu.VMEM((shard, NEAR * own), jnp.bfloat16),
                *fetched,
            ],
            compiler_params=params(32),
            cost_estimate=cost(3 * pairs * width, 8 * 10**6, pairs // 2),
            name="grads",
        )(spot, blocks, joined, other, ordered, turned, corr, *sums)

    far_terms, *sums, _ = grads(1, [like((NEAR, width, own), f32)])
    far_acc = trade(far_terms.astype(f16), "neg", rows).astype(f32).sum(axis=0)
    query_far = mirror(far_acc.astype(f16)).astype(f32)

    near_keep, near_send, keep, send, lse = grads(0, [like((2, width, own), f32)] * 2, *sums)
    from_core = other_core(send)
    got = swap_near(near_send.astype(f16), HALVING[0])
    onward = (near_keep[1] + got[1].astype(f32)).astype(f16)
    near_acc = near_keep[0] + got[0].astype(f32) + swap_near(onward, HALVING[1]).astype(f32)

    count = LINE * RING
    block = shard // CORES // count
    neg_acc = pl.pallas_call(
        sum_cores_kernel,
        in_specs=[vmem] * 2,
        out_specs=vmem,
        out_shape=like((count, block + 8, width), f32),
        compiler_params=params(),
        name="sum_cores",
    )(keep, from_core)
    neg_acc = trade(neg_acc.astype(f16), "dp", sheets).astype(f32)
    power = jnp.exp2(neg_acc[:, block : block + 1, :1] - 13.0)
    neg_grad = jnp.sum(neg_acc[:, :block, :] * power, axis=0)

    query_grad, row_loss = pl.pallas_call(
        finish_kernel,
        in_specs=[smem] + [vmem] * 7,
        out_specs=(vmem, vmem),
        out_shape=(like((own, width), f32), like((1, own), f32)),
        compiler_params=params(),
        name="finish",
    )(spot, near_acc, query_far, positives, score, lse, joined, other)
    return (query_grad, row_loss.reshape(own), neg_grad)


def solution(mesh):
    placed = (
        P(("dp", "neg"), None),
        P(("dp", "neg"), None),
        P("neg", None),
        P(("dp", "neg")),
        P("neg"),
        P(),
    )
    return jax.shard_map(
        per_device,
        mesh=mesh,
        in_specs=placed,
        out_specs=(P(("dp", "neg"), None), P(("dp", "neg")), P(("neg", "dp"), None)),
        check_vma=False,
    )
```

time: 122 us -> 122 us (level)
  waiting for transfers between devices: 35.4 us -> 39.2 us
  local copies, waits for them, and re-layouts: 8.87 us -> 6.41 us
  other arithmetic: 5.13 us -> 3.24 us
    ppermute x0 -> x2, waiting for transfers between devices: none -> 7.61 us  [swap_near(): return lax.ppermute(value, 'neg', perm)]
    all_to_all x4 -> x3, starting transfers between devices: 31 us -> 24 us  [trade(): lax.all_to_all(value, axis, 0, 0, tiled=True, axis_index_groups=groups)]
    ppermute x0 -> x2, starting transfers between devices: none -> 6.63 us  [swap_near(): return lax.ppermute(value, 'neg', perm)]
    all_to_all x4 -> x3, waiting for transfers between devices: 23.4 us -> 16.8 us  [trade(): lax.all_to_all(value, axis, 0, 0, tiled=True, axis_index_groups=groups)]
    ppermute x3, waiting for transfers between devices: 12 us -> 14.8 us  [mirror(): return lax.ppermute(value, ('dp', 'neg'), perm)]
    broadcast_in_dim x2 -> x0, local copies, waits for them, and re-layouts: 2.69 us -> none  [spread(): jnp.broadcast_to(value[None], (NEAR,) + value.shape)]
    convert_element_type x3 -> x5, other arithmetic: 2.79 us -> 0.98 us  [the longest x1 0.87 us: per_device(): far_acc = trade(far_terms.astype(f16), 'neg', rows).astype(f32).sum(axis=0)]
    unnamed x25 -> x30, local copies, waits for them, and re-layouts: 5.53 us -> 5.76 us
  transfers between devices with their start and end apart: 8 -> 9, of which waited for: 6 -> 6; matrix products, arithmetic and copies ran while one was open for 4% -> 2% of each run, Pallas kernels for 4% -> 2%
where the time goes in v2:
time: 122 us; the launch traced here: 121 us
  starting transfers between devices  45.6 us (37%)
  waiting for transfers between devices  39.2 us (32%)
  Pallas kernels  18 us (15%)
  blocking collectives  7.81 us (6%)
  local copies, waits for them, and re-layouts  6.41 us (5%)
  other arithmetic  3.24 us (3%)
    all_to_all x3, starting transfers between devices, trade(): lax.all_to_all(value, axis, 0, 0, tiled=True, axis_index_groups=groups)  24 us
    all_to_all x3, waiting for transfers between devices, trade(): lax.all_to_all(value, axis, 0, 0, tiled=True, axis_index_groups=groups)  16.8 us
    ppermute x3, waiting for transfers between devices, mirror(): return lax.ppermute(value, ('dp', 'neg'), perm)  14.8 us
    ppermute x3, starting transfers between devices, mirror(): return lax.ppermute(value, ('dp', 'neg'), perm)  13.1 us
    pallas_call x2, Pallas kernels, grads(): pl.pallas_call(functools.partial(grads_kernel, side), in_specs=[smem, hbm...  8.57 us
    all_to_all x1, blocking collectives, trade(): lax.all_to_all(value, axis, 0, 0, tiled=True, axis_index_groups=groups)  7.81 us
    ppermute x2, waiting for transfers between devices, swap_near(): return lax.ppermute(value, 'neg', perm)  7.61 us
    ppermute x2, starting transfers between devices, swap_near(): return lax.ppermute(value, 'neg', perm)  6.63 us
  transfers between devices with their start and end apart: 9, of which 6 were waited for; matrix products, arithmetic and copies ran while one was open for 2% of the time, Pallas kernels for 2%

profile of v2, /device:TPU:2, one launch (start us, length us, event | category | flops | bytes accessed | tf_op | source)
XLA Modules:
  0.0 121.2 jit_solution(294921573816068806)
XLA Ops:
  0.6 5.4 %collective-permute-start = (bf16[256,256]{1,0:T(8,128)(2,1)}, bf16[256,256]{1,0:T(8,128)(2,1)S(1)}, u32[]{:S(2)}, u32[]{:S(2)}) collective-permute-start(bf16[256,256]{1,0:T(8,128)(2,1)} %queries_ref.1), channel_id=1, source_target_pairs={{0,388},{1,389},{2,390},{3,391},{4,384},{5,385},{6,386},{7,387},{8... | collective-permute-start | bytes 393224 | tf_op jit(solution)/shard_map/ppermute | solution.py:38
  6.0 6.5 %collective-permute-done.far_ref = bf16[256,256]{1,0:T(8,128)(2,1)S(1)} collective-permute-done((bf16[256,256]{1,0:T(8,128)(2,1)}, bf16[256,256]{1,0:T(8,128)(2,1)S(1)}, u32[]{:S(2)}, u32[]{:S(2)}) %collective-permute-start) | collective-permute-done | bytes 131104 | tf_op jit(solution)/shard_map/ppermute | solution.py:38
  12.5 0.9 copy-done.6
  13.4 1.1 spread.1
  14.5 0.0 copy-start.12
  14.5 5.9 %all-to-all-start = ((bf16[4,2,256,256]{3,2,1,0:T(8,128)(2,1)}), bf16[4,2,256,256]{3,2,1,0:T(8,128)(2,1)S(1)}, u32[]{:S(2)}, u32[]{:S(2)}) async-start(bf16[4,2,256,256]{3,2,1,0:T(8,128)(2,1)} %spread.1), calls=%async_computation | async-start | bytes 2097152 | tf_op jit(solution)/shard_map/all_to_all | solution.py:242
  20.4 0.0 copy-done.7
  20.4 0.0 copy-done.8
  20.5 0.0 copy-done.10
  20.5 0.0 copy-done.11
  20.5 0.0 copy-done.12
  20.5 0.0 copy-start.9
  20.5 1.2 %copy-done.9 = bf16[2048,256]{1,0:T(8,128)(2,1)S(1)} copy-done((bf16[2048,256]{1,0:T(8,128)(2,1)S(1)}, bf16[2048,256]{1,0:T(8,128)(2,1)}, u32[]{:S(2)}) %copy-start.9) | copy-done | bytes 1048600
  21.7 1.8 %lookup.1 = (f32[16,128]{1,0:T(8,128)S(1)}, f32[1,256]{1,0:T(1,128)S(1)}, bf16[2048,256]{1,0:T(8,128)(2,1)S(1)}) custom-call(s32[1]{0:T(128)} %bitcast.1.place_ref, s32[512,128]{1,0:T(8,128)S(1)} %bitcast.13, s32[16,128]{1,0:T(8,128)S(1)} %bitcast.14, s32[2,128]{1,0:T(2,128)S(1)} %bitcast.15, bf16[256,256]{1,0:T(8,128)(2,1)S(1)} %copy-done.7, ...), custom_call_target="tpu_custom_call" | custom-call | flops 1000000000 | bytes 2000000 | tf_op jit(solution)/shard_map/lookup/pallas_call | solution.py:261
  23.5 9.1 %all-to-all-done.blocks_hbm = bf16[4,2,256,256]{3,2,1,0:T(8,128)(2,1)S(1)} async-done(((bf16[4,2,256,256]{3,2,1,0:T(8,128)(2,1)}), bf16[4,2,256,256]{3,2,1,0:T(8,128)(2,1)S(1)}, u32[]{:S(2)}, u32[]{:S(2)}) %all-to-all-start) | async-done | bytes 1048608 | tf_op jit(solution)/shard_map/all_to_all | solution.py:242
  32.6 5.3 %stats.1 = f32[4,8,256]{2,1,0:T(8,128)S(1)} custom-call(s32[1]{0:T(128)} %bitcast.spot_ref, bf16[4,2,256,256]{3,2,1,0:T(8,128)(2,1)S(1)} %all-to-all-done.blocks_hbm, bf16[2048,256]{1,0:T(8,128)(2,1)S(1)} %get-tuple-element.16.negatives_ref, f32[16,128]{1,0:T(8,128)S(1)} %get-tuple-element.17.rows_ref, f32[1,256]{1,0:T(1,128)S(1)} %get-tuple-element.18.score_ref), custom_call_target="tpu_custom_call" | custom-call | flops 2147483648 | bytes 4000000 | tf_op jit(solution)/shard_map/stats/pallas_call | solution.py:301
  37.9 7.8 %all_to_all.20.parts_ref = f32[4,8,256]{2,1,0:T(8,128)S(1)} all-to-all(f32[4,8,256]{2,1,0:T(8,128)S(1)} %stats.1), channel_id=1, replica_groups={{0,1,2,3},{4,5,6,7},{8,9,10,11},{12,13,14,15},{16,17,18,19},{20,21,22,2..., dimensions={0} | all-to-all | bytes 65536 | tf_op jit(solution)/shard_map/all_to_all | solution.py:242
  45.7 2.1 %collective-permute-start.1 = (f32[8,256]{1,0:T(8,128)S(1)}, f32[8,256]{1,0:T(8,128)S(1)}, u32[]{:S(2)}, u32[]{:S(2)}) collective-permute-start(f32[8,256]{1,0:T(8,128)S(1)} %join.1.joined_ref), channel_id=1, source_target_pairs={{0,388},{1,389},{2,390},{3,391},{4,384},{5,385},{6,386},{7,387},{8... | collective-permute-start | bytes 24584 | tf_op jit(solution)/shard_map/ppermute | solution.py:38
  47.8 0.6 copy.10
  48.5 4.0 %collective-permute-done.1.other_ref = f32[8,256]{1,0:T(8,128)S(1)} collective-permute-done((f32[8,256]{1,0:T(8,128)S(1)}, f32[8,256]{1,0:T(8,128)S(1)}, u32[]{:S(2)}, u32[]{:S(2)}) %collective-permute-start.1) | collective-permute-done | bytes 8224 | tf_op jit(solution)/shard_map/ppermute | solution.py:38
  52.5 4.0 %grads.2 = (f32[4,256,256]{2,1,0:T(8,128)S(1)}, f32[1024,256]{1,0:T(8,128)S(1)}, f32[1024,256]{1,0:T(8,128)S(1)}, f32[4,256]{1,0:T(4,128)}) custom-call(s32[1]{0:T(128)} %bitcast.spot_ref, bf16[4,2,256,256]{3,2,1,0:T(8,128)(2,1)S(1)} %all-to-all-done.blocks_hbm, f32[8,256]{1,0:T(8,128)S(1)} %join.1.joined_ref, ...), custom_call_target="tpu_custom_call" | custom-call | flops 3221225472 | bytes 8000000 | tf_op jit(solution)/shard_map/grads/pallas_call | solution.py:324
  56.5 1.2 %copy-done.1 = bf16[2048,256]{0,1:T(8,128)(2,1)S(1)} copy-done((bf16[2048,256]{0,1:T(8,128)(2,1)S(1)}, bf16[2048,256]{0,1:T(8,128)(2,1)}, u32[]{:S(2)}) %copy-start.1) | copy-done | bytes 1048600
  57.7 4.6 %grads.3 = (f32[2,256,256]{2,1,0:T(8,128)S(1)}, f32[2,256,256]{2,1,0:T(8,128)S(1)}, f32[1024,256]{1,0:T(8,128)S(1)}, f32[1024,256]{1,0:T(8,128)}, f32[4,256]{1,0:T(4,128)S(1)}) custom-call(s32[1]{0:T(128)} %bitcast.spot_ref, bf16[4,2,256,256]{3,2,1,0:T(8,128)(2,1)S(1)} %all-to-all-done.blocks_hbm, f32[8,256]{1,0:T(8,128)S(1)} %join.1.joined_ref, ...), custom_call_target="tpu_custom_call" | custom-call | flops 3221225472 | bytes 8000000 | tf_op jit(solution)/shard_map/grads/pallas_call | solution.py:324
  62.3 0.8 copy-done.2
  63.1 0.8 copy-done.4
  63.9 1.9 %collective-permute-start.5 = (f32[1024,256]{1,0:T(8,128)}, f32[1024,256]{1,0:T(8,128)S(1)}, u32[]{:S(2)}, u32[]{:S(2)}) collective-permute-start(f32[1024,256]{1,0:T(8,128)} %get-tuple-element.28), channel_id=1, source_target_pairs={{0,8},{8,0},{16,24},{24,16},{32,40},{40,32},{48,56},{56,48},{64,72... | collective-permute-start | bytes 3145736 | tf_op jit(solution)/shard_map/ppermute | solution.py:48
  65.8 0.9 convert_element_type.44
  66.7 4.9 %all-to-all-start.2 = ((f16[4,256,256]{2,1,0:T(8,128)(2,1)}), f16[4,256,256]{2,1,0:T(8,128)(2,1)S(1)}, u32[]{:S(2)}, u32[]{:S(2)}) async-start(f16[4,256,256]{2,1,0:T(8,128)(2,1)} %convert_element_type.44), calls=%async_computation.2 | async-start | bytes 1048576 | tf_op jit(solution)/shard_map/all_to_all | solution.py:242
  71.6 0.0 collective-permute-done.5.got_ref
  71.6 0.3 sum_cores.1
  71.9 1.0 convert_element_type.48
  72.9 7.7 %all-to-all-done.2 = f16[4,256,256]{2,1,0:T(8,128)(2,1)S(1)} async-done(((f16[4,256,256]{2,1,0:T(8,128)(2,1)}), f16[4,256,256]{2,1,0:T(8,128)(2,1)S(1)}, u32[]{:S(2)}, u32[]{:S(2)}) %all-to-all-start.2) | async-done | bytes 524320 | tf_op jit(solution)/shard_map/all_to_all | solution.py:242
  80.6 0.8 copy-done.13
  81.3 13.1 %all-to-all-start.3 = ((f16[32,40,256]{2,1,0:T(8,128)(2,1)}), f16[32,40,256]{2,1,0:T(8,128)(2,1)S(1)}, u32[]{:S(2)}, u32[]{:S(2)}) async-start(f16[32,40,256]{2,1,0:T(8,128)(2,1)} %convert_element_type.48), calls=%async_computation.3 | async-start | bytes 1310720 | tf_op jit(solution)/shard_map/all_to_all | solution.py:242
  94.5 0.0 copy-start.14
  94.5 0.0 copy-done.5
  94.6 2.1 %collective-permute-start.2 = (f16[2,256,256]{2,1,0:T(8,128)(2,1)S(1)}, f16[2,256,256]{2,1,0:T(8,128)(2,1)S(1)}, u32[]{:S(2)}, u32[]{:S(2)}) collective-permute-start(f16[2,256,256]{2,1,0:T(8,128)(2,1)S(1)} %convert_element_type.38), channel_id=1, source_target_pairs={{0,3},{1,2},{2,1},{3,0},{4,7},{5,6},{6,5},{7,4},{8,11},{9,10},{10,... | collective-permute-start | bytes 786440 | tf_op jit(solution)/shard_map/ppermute | solution.py:43
  96.6 7.6 %collective-permute-done.2 = f16[2,256,256]{2,1,0:T(8,128)(2,1)S(1)} collective-permute-done((f16[2,256,256]{2,1,0:T(8,128)(2,1)S(1)}, f16[2,256,256]{2,1,0:T(8,128)(2,1)S(1)}, u32[]{:S(2)}, u32[]{:S(2)}) %collective-permute-start.2) | collective-permute-done | bytes 262176 | tf_op jit(solution)/shard_map/ppermute | solution.py:43
  104.3 4.6 %collective-permute-start.3 = (f16[256,256]{1,0:T(8,128)(2,1)S(1)}, f16[256,256]{1,0:T(8,128)(2,1)S(1)}, u32[]{:S(2)}, u32[]{:S(2)}) collective-permute-start(f16[256,256]{1,0:T(8,128)(2,1)S(1)} %fusion.1), channel_id=1, source_target_pairs={{0,1},{1,0},{2,3},{3,2},{4,5},{5,4},{6,7},{7,6},{8,9},{9,8},{10,11... | collective-permute-start | bytes 393224 | tf_op jit(solution)/shard_map/ppermute | solution.py:43
  108.9 0.1 convert_reduce_fusion
  109.0 5.6 %collective-permute-start.4 = (f16[256,256]{1,0:T(8,128)(2,1)S(1)}, f16[256,256]{1,0:T(8,128)(2,1)S(1)}, u32[]{:S(2)}, u32[]{:S(2)}) collective-permute-start(f16[256,256]{1,0:T(8,128)(2,1)S(1)} %convert_element_type.46), channel_id=1, source_target_pairs={{0,388},{1,389},{2,390},{3,391},{4,384},{5,385},{6,386},{7,387},{8... | collective-permute-start | bytes 393224 | tf_op jit(solution)/shard_map/ppermute | solution.py:38
  114.6 0.0 collective-permute-done.3
  114.7 4.3 %collective-permute-done.4 = f16[256,256]{1,0:T(8,128)(2,1)S(1)} collective-permute-done((f16[256,256]{1,0:T(8,128)(2,1)S(1)}, f16[256,256]{1,0:T(8,128)(2,1)S(1)}, u32[]{:S(2)}, u32[]{:S(2)}) %collective-permute-start.4) | collective-permute-done | bytes 131104 | tf_op jit(solution)/shard_map/ppermute | solution.py:38
  119.0 0.9 finish.1
  120.0 0.0 all-to-all-done.3
  120.0 0.1 convert_element_type.49
  120.1 0.3 fusion.4
  120.4 0.8 fusion
  (21 shorter events, 0.2 us)
Async XLA Ops:
  0.6 11.9 %collective-permute-start = (bf16[256,256]{1,0:T(8,128)(2,1)}, bf16[256,256]{1,0:T(8,128)(2,1)S(1)}, u32[]{:S(2)}, u32[]{:S(2)}) collective-permute-start(bf16[256,256]{1,0:T(8,128)(2,1)} %queries_ref.1), channel_id=1, source_target_pairs={{0,388},{1,389},{2,390},{3,391},{4,384},{5,385},{6,386},{7,387},{8... | collective-permute-start | bytes 393224 | tf_op jit(solution)/shard_map/ppermute | solution.py:38
  12.5 0.9 copy-start.6
  14.5 6.0 %copy-start.7 = (bf16[256,256]{1,0:T(8,128)(2,1)S(1)}, bf16[256,256]{1,0:T(8,128)(2,1)}, u32[]{:S(2)}) copy-start(bf16[256,256]{1,0:T(8,128)(2,1)} %queries_ref.1) | copy-start | bytes 393220
  14.5 6.0 %copy-start.8 = (bf16[256,256]{1,0:T(8,128)(2,1)S(1)}, bf16[256,256]{1,0:T(8,128)(2,1)}, u32[]{:S(2)}) copy-start(bf16[256,256]{1,0:T(8,128)(2,1)} %pos_ref.3) | copy-start | bytes 393220
  14.5 6.0 %copy-start.10 = (s32[65536]{0:T(1024)S(1)}, s32[65536]{0:T(1024)}, u32[]{:S(2)}) copy-start(s32[65536]{0:T(1024)} %param.11) | copy-start | bytes 786436
  14.5 6.0 %copy-start.11 = (s32[2048]{0:T(1024)S(1)}, s32[2048]{0:T(1024)}, u32[]{:S(2)}) copy-start(s32[2048]{0:T(1024)} %param.10) | copy-start | bytes 24580
  14.5 6.0 %copy-start.12 = (s32[256]{0:T(256)S(1)}, s32[256]{0:T(256)}, u32[]{:S(2)}) copy-start(s32[256]{0:T(256)} %param.9) | copy-start | bytes 3076
  14.5 18.1 %all-to-all-start = ((bf16[4,2,256,256]{3,2,1,0:T(8,128)(2,1)}), bf16[4,2,256,256]{3,2,1,0:T(8,128)(2,1)S(1)}, u32[]{:S(2)}, u32[]{:S(2)}) async-start(bf16[4,2,256,256]{3,2,1,0:T(8,128)(2,1)} %spread.1), calls=%async_computation | async-start | bytes 2097152 | tf_op jit(solution)/shard_map/all_to_all | solution.py:242
  20.5 1.2 %copy-start.9 = (bf16[2048,256]{1,0:T(8,128)(2,1)S(1)}, bf16[2048,256]{1,0:T(8,128)(2,1)}, u32[]{:S(2)}) copy-start(bf16[2048,256]{1,0:T(8,128)(2,1)} %negatives_ref.1) | copy-start | bytes 3145732
  45.7 6.8 %collective-permute-start.1 = (f32[8,256]{1,0:T(8,128)S(1)}, f32[8,256]{1,0:T(8,128)S(1)}, u32[]{:S(2)}, u32[]{:S(2)}) collective-permute-start(f32[8,256]{1,0:T(8,128)S(1)} %join.1.joined_ref), channel_id=1, source_target_pairs={{0,388},{1,389},{2,390},{3,391},{4,384},{5,385},{6,386},{7,387},{8... | collective-permute-start | bytes 24584 | tf_op jit(solution)/shard_map/ppermute | solution.py:38
  48.5 8.0 %copy-start = (bf16[2048,256]{0,1:T(8,128)(2,1)}, bf16[2048,256]{0,1:T(8,128)(2,1)S(1)}, u32[]{:S(2)}) copy-start(bf16[2048,256]{0,1:T(8,128)(2,1)S(1)} %copy.10) | copy-start | bytes 3145732
  56.5 1.2 %copy-start.1 = (bf16[2048,256]{0,1:T(8,128)(2,1)S(1)}, bf16[2048,256]{0,1:T(8,128)(2,1)}, u32[]{:S(2)}) copy-start(bf16[2048,256]{0,1:T(8,128)(2,1)} %copy-done) | copy-start | bytes 3145732
  62.3 0.8 copy-start.2
  63.1 0.8 copy-start.4
  63.9 7.7 %collective-permute-start.5 = (f32[1024,256]{1,0:T(8,128)}, f32[1024,256]{1,0:T(8,128)S(1)}, u32[]{:S(2)}, u32[]{:S(2)}) collective-permute-start(f32[1024,256]{1,0:T(8,128)} %get-tuple-element.28), channel_id=1, source_target_pairs={{0,8},{8,0},{16,24},{24,16},{32,40},{40,32},{48,56},{56,48},{64,72... | collective-permute-start | bytes 3145736 | tf_op jit(solution)/shard_map/ppermute | solution.py:48
  66.7 13.9 %all-to-all-start.2 = ((f16[4,256,256]{2,1,0:T(8,128)(2,1)}), f16[4,256,256]{2,1,0:T(8,128)(2,1)S(1)}, u32[]{:S(2)}, u32[]{:S(2)}) async-start(f16[4,256,256]{2,1,0:T(8,128)(2,1)} %convert_element_type.44), calls=%async_computation.2 | async-start | bytes 1048576 | tf_op jit(solution)/shard_map/all_to_all | solution.py:242
  71.9 22.6 %copy-start.5 = (f32[2,256,256]{2,1,0:T(8,128)S(1)}, f32[2,256,256]{2,1,0:T(8,128)}, u32[]{:S(2)}) copy-start(f32[2,256,256]{2,1,0:T(8,128)} %copy-done.4) | copy-start | bytes 1572868
  72.9 31.4 %copy-start.3 = (f32[2,256,256]{2,1,0:T(8,128)S(1)}, f32[2,256,256]{2,1,0:T(8,128)}, u32[]{:S(2)}) copy-start(f32[2,256,256]{2,1,0:T(8,128)} %copy-done.2) | copy-start | bytes 1572868
  80.6 0.8 copy-start.13
  81.3 38.6 %all-to-all-start.3 = ((f16[32,40,256]{2,1,0:T(8,128)(2,1)}), f16[32,40,256]{2,1,0:T(8,128)(2,1)S(1)}, u32[]{:S(2)}, u32[]{:S(2)}) async-start(f16[32,40,256]{2,1,0:T(8,128)(2,1)} %convert_element_type.48), calls=%async_computation.3 | async-start | bytes 1310720 | tf_op jit(solution)/shard_map/all_to_all | solution.py:242
  94.5 14.4 %copy-start.14 = (f16[4,256,256]{2,1,0:T(8,128)(2,1)S(1)}, f16[4,256,256]{2,1,0:T(8,128)(2,1)}, u32[]{:S(2)}) copy-start(f16[4,256,256]{2,1,0:T(8,128)(2,1)} %copy-done.13) | copy-start | bytes 1572868
  94.6 9.7 %collective-permute-start.2 = (f16[2,256,256]{2,1,0:T(8,128)(2,1)S(1)}, f16[2,256,256]{2,1,0:T(8,128)(2,1)S(1)}, u32[]{:S(2)}, u32[]{:S(2)}) collective-permute-start(f16[2,256,256]{2,1,0:T(8,128)(2,1)S(1)} %convert_element_type.38), channel_id=1, source_target_pairs={{0,3},{1,2},{2,1},{3,0},{4,7},{5,6},{6,5},{7,4},{8,11},{9,10},{10,... | collective-permute-start | bytes 786440 | tf_op jit(solution)/shard_map/ppermute | solution.py:43
  104.3 10.3 %collective-permute-start.3 = (f16[256,256]{1,0:T(8,128)(2,1)S(1)}, f16[256,256]{1,0:T(8,128)(2,1)S(1)}, u32[]{:S(2)}, u32[]{:S(2)}) collective-permute-start(f16[256,256]{1,0:T(8,128)(2,1)S(1)} %fusion.1), channel_id=1, source_target_pairs={{0,1},{1,0},{2,3},{3,2},{4,5},{5,4},{6,7},{7,6},{8,9},{9,8},{10,11... | collective-permute-start | bytes 393224 | tf_op jit(solution)/shard_map/ppermute | solution.py:43
  109.0 10.1 %collective-permute-start.4 = (f16[256,256]{1,0:T(8,128)(2,1)S(1)}, f16[256,256]{1,0:T(8,128)(2,1)S(1)}, u32[]{:S(2)}, u32[]{:S(2)}) collective-permute-start(f16[256,256]{1,0:T(8,128)(2,1)S(1)} %convert_element_type.46), channel_id=1, source_target_pairs={{0,388},{1,389},{2,390},{3,391},{4,384},{5,385},{6,386},{7,387},{8... | collective-permute-start | bytes 393224 | tf_op jit(solution)/shard_map/ppermute | solution.py:38

commit v3 on v2

--- a/solution.py
+++ b/solution.py
@@ -12,7 +12,7 @@
 SPAN = 60.0
 MIB = 1024 * 1024
 FAR, NEAR = 2, 4
-HALVING = (3, 1)
+HALVING = ((3, 1), (1, 3))
 LINE, RING, CORES = 4, 8, 2
 
 
@@ -160,48 +160,48 @@
 
 
 def grads_kernel(
-    side, spot_ref, blocks_hbm, joined_ref, other_ref, negatives_ref, turned_ref, rows_ref, *refs
+    spot_ref, blocks_hbm, joined_ref, other_ref, negatives_ref, turned_ref, rows_ref, *refs
 ):
-    sums, refs = refs[: 2 - 2 * side], refs[2 - 2 * side :]
-    query_outs, refs = refs[: 2 - side], refs[2 - side :]
+    query_outs, refs = refs[: 2 * FAR], refs[2 * FAR :]
     keep_out, send_out, lse_out, boost_ref, weight_ref, blocks_ref, corr_ref, sem = refs
     fetch = pltpu.make_async_copy(blocks_hbm, blocks_ref, sem)
     fetch.start()
     to_columns(rows_ref, corr_ref)
     total = negatives_ref.shape[0]
     spot = spot_ref[0]
-    offset = side * NEAR
-    joined = joined_ref[offset : offset + NEAR, :]
-    lse_all = join([joined, other_ref[NEAR - offset : 2 * NEAR - offset, :]])
+    joined = joined_ref[...]
+    other = jnp.concatenate([other_ref[NEAR:, :], other_ref[:NEAR, :]], axis=0)
+    lse_all = join([joined, other])
     lse_out[...] = lse_all
     boost_ref[...] = jnp.exp(jnp.minimum(lse_all - joined, SPAN))
-    places = list(range(NEAR)) if side else [spot ^ k for k in range(NEAR)]
-    lse = jnp.concatenate([lse_out[pl.ds(k, 1), :] for k in places], axis=1)
+    half = total // CORES
     fetch.wait()
-    block = jnp.concatenate([blocks_ref[k, side] for k in places], axis=0)
-    rows = block.shape[0]
-    own = rows // NEAR
-    half = total // CORES
-    for start in range(0, total, SPLIT):
-        part = slice(start, start + SPLIT)
-        scores = dot(negatives_ref[part, :], block, ((1,), (1,)))
-        scores = scores - wide(corr_ref[part, :], rows)
-        weight = jnp.exp(scores - lse).astype(jnp.bfloat16)
-        weight_ref[part, :] = weight
-        neg_term = dot(weight, block, ((1,), (0,)))
-        which, place = start // half, slice(start % half, start % half + SPLIT)
-        if sums:
-            neg_term = sums[which][place, :] + neg_term
-        (keep_out, send_out)[which][place, :] = neg_term
-    first, onward = HALVING
-    for index, k in enumerate(places):
-        weight = weight_ref[:, index * own : (index + 1) * own]
-        term = dot(turned_ref[...], weight, ((1,), (0,))) * boost_ref[pl.ds(k, 1), :]
-        if side:
-            query_outs[0][index] = term
-        else:
-            out = query_outs[index in (first, first ^ onward)]
-            out[int(index in (onward, first ^ onward))] = term
+    for side in range(FAR):
+        places = [spot ^ k for k in range(NEAR)]
+        lse = [lse_out[pl.ds(side * NEAR + k, 1), :] for k in places]
+        lse = jnp.concatenate(lse, axis=1)
+        block = jnp.concatenate([blocks_ref[k, side] for k in places], axis=0)
+        rows = block.shape[0]
+        own = rows // NEAR
+        for start in range(0, total, SPLIT):
+            part = slice(start, start + SPLIT)
+            scores = dot(negatives_ref[part, :], block, ((1,), (1,)))
+            scores = scores - wide(corr_ref[part, :], rows)
+            weight = jnp.exp(scores - lse).astype(jnp.bfloat16)
+            weight_ref[part, :] = weight
+            neg_term = dot(weight, block, ((1,), (0,)))
+            which, place = start // half, slice(start % half, start % half + SPLIT)
+            out = (keep_out, send_out)[which]
+            if side > 0:
+                neg_term = out[place, :] + neg_term
+            out[place, :] = neg_term
+        first, onward = HALVING[side]
+        for index, k in enumerate(places):
+            weight = weight_ref[:, index * own : (index + 1) * own]
+            term = dot(turned_ref[...], weight, ((1,), (0,)))
+            out = query_outs[side * 2 + (index in (first, first ^ onward))]
+            place = int(index in (onward, first ^ onward))
+            out[place] = term * boost_ref[pl.ds(side * NEAR + k, 1), :]
 
 
 def spread_kernel(near_ref, far_ref, out_ref):
@@ -210,7 +210,7 @@
         out_ref[k, 1] = far_ref[...]
 
 
-def sum_cores_kernel(keep_ref, got_ref, out_ref):
+def sum_cores_kernel(keep_ref, got_ref, arrived_ref, out_ref):
     total = keep_ref[...] + got_ref[...]
     top = jnp.max(jnp.max(jnp.abs(total), axis=0, keepdims=True), axis=1, keepdims=True)
     power = jnp.clip(jnp.floor(jnp.log2(jnp.maximum(top, 1e-30))), -99.0, 99.0)
@@ -318,44 +318,50 @@
     )(trade(stats, "neg", rows))
     other = mirror(joined)
 
-    def grads(side, query_outs, *sums):
-        neg_like = like((shard // CORES, width), f32)
-        outs = [*query_outs, neg_like, neg_like, like((NEAR, own), f32)]
-        return pl.pallas_call(
-            functools.partial(grads_kernel, side),
-            in_specs=[smem, hbm] + [vmem] * (5 + len(sums)),
-            out_specs=(vmem,) * len(outs),
-            out_shape=tuple(outs),
-            scratch_shapes=[
-                pltpu.VMEM((NEAR, own), f32),
-                pltpu.VMEM((shard, NEAR * own), jnp.bfloat16),
-                *fetched,
-            ],
-            compiler_params=params(32),
-            cost_estimate=cost(3 * pairs * width, 8 * 10**6, pairs // 2),
-            name="grads",
-        )(spot, blocks, joined, other, ordered, turned, corr, *sums)
-
-    far_terms, *sums, _ = grads(1, [like((NEAR, width, own), f32)])
-    far_acc = trade(far_terms.astype(f16), "neg", rows).astype(f32).sum(axis=0)
+    near_keep, near_send, far_keep, far_send, keep, send, lse = pl.pallas_call(
+        grads_kernel,
+        in_specs=[smem, hbm] + [vmem] * 5,
+        out_specs=(vmem,) * (2 * FAR + 3),
+        out_shape=(
+            *[like((2, width, own), f32)] * (2 * FAR),
+            like((shard // CORES, width), f32),
+            like((shard // CORES, width), f32),
+            like((parts, own), f32),
+        ),
+        scratch_shapes=[
+            pltpu.VMEM((parts, own), f32),
+            pltpu.VMEM((shard, NEAR * own), jnp.bfloat16),
+            *fetched,
+        ],
+        compiler_params=params(24),
+        cost_estimate=cost(6 * pairs * width, 8 * 10**6, pairs),
+        name="grads",
+    )(spot, blocks, joined, other, ordered, turned, corr)
+    from_core = other_core(send)
+
+    def halve(side, keep, got):
+        sent = (keep[1] + got[1].astype(f32)).astype(f16)
+        sent = swap_near(sent, HALVING[side][1])
+        return keep[0] + got[0].astype(f32) + sent.astype(f32)
+
+    far_got = swap_near(far_send.astype(f16), HALVING[1][0])
+    near_got = swap_near(near_send.astype(f16), HALVING[0][0])
+    arrived = near_got[0, :8, :LANES].astype(f32) + far_got[0, :8, :LANES].astype(f32)
+    far_acc = halve(1, far_keep, far_got)
+    near_acc = halve(0, near_keep, near_got)
     query_far = mirror(far_acc.astype(f16)).astype(f32)
-
-    near_keep, near_send, keep, send, lse = grads(0, [like((2, width, own), f32)] * 2, *sums)
-    from_core = other_core(send)
-    got = swap_near(near_send.astype(f16), HALVING[0])
-    onward = (near_keep[1] + got[1].astype(f32)).astype(f16)
-    near_acc = near_keep[0] + got[0].astype(f32) + swap_near(onward, HALVING[1]).astype(f32)
 
     count = LINE * RING
     block = shard // CORES // count
     neg_acc = pl.pallas_call(
         sum_cores_kernel,
-        in_specs=[vmem] * 2,
+        in_specs=[vmem] * 3,
         out_specs=vmem,
         out_shape=like((count, block + 8, width), f32),
         compiler_params=params(),
+        cost_estimate=cost(10**6, 10**6, 0),
         name="sum_cores",
-    )(keep, from_core)
+    )(keep, from_core, arrived)
     neg_acc = trade(neg_acc.astype(f16), "dp", sheets).astype(f32)
     power = jnp.exp2(neg_acc[:, block : block + 1, :1] - 13.0)
     neg_grad = jnp.sum(neg_acc[:, :block, :] * power, axis=0)

time: 122 us -> 113 us (0.926)
  the two profiles are of different devices: /device:TPU:2 before, /device:TPU:8 now
where the time goes in v3:
time: 113 us; the launch traced here: 112 us
  starting transfers between devices  48.1 us (43%)
  waiting for transfers between devices  33.5 us (30%)
  Pallas kernels  16.8 us (15%)
  blocking collectives  7.8 us (7%)
  local copies, waits for them, and re-layouts  2.81 us (2%)
  other arithmetic  2.42 us (2%)
    all_to_all x2, starting transfers between devices, trade(): lax.all_to_all(value, axis, 0, 0, tiled=True, axis_index_groups=groups)  18 us
    ppermute x3, starting transfers between devices, mirror(): return lax.ppermute(value, ('dp', 'neg'), perm)  17.8 us
    ppermute x4, waiting for transfers between devices, swap_near(): return lax.ppermute(value, 'neg', perm)  11.6 us
    all_to_all x2, waiting for transfers between devices, trade(): lax.all_to_all(value, axis, 0, 0, tiled=True, axis_index_groups=groups)  11.1 us
    ppermute x3, waiting for transfers between devices, mirror(): return lax.ppermute(value, ('dp', 'neg'), perm)  10.7 us
    ppermute x4, starting transfers between devices, swap_near(): return lax.ppermute(value, 'neg', perm)  10.4 us
    all_to_all x1, blocking collectives, trade(): lax.all_to_all(value, axis, 0, 0, tiled=True, axis_index_groups=groups)  7.8 us
    pallas_call x1, Pallas kernels, per_device(): pl.pallas_call(grads_kernel, in_specs=[smem, hbm] + [vmem] * 5, out_specs...  7.41 us
  transfers between devices with their start and end apart: 10, of which 7 were waited for; matrix products, arithmetic and copies ran while one was open for 1% of the time, Pallas kernels for 2%

profile of v3, /device:TPU:8, one launch (start us, length us, event | category | flops | bytes accessed | tf_op | source)
XLA Modules:
  0.0 112.4 jit_solution(17666021695517542760)
XLA Ops:
  0.6 6.1 %collective-permute-start = (bf16[256,256]{1,0:T(8,128)(2,1)}, bf16[256,256]{1,0:T(8,128)(2,1)S(1)}, u32[]{:S(2)}, u32[]{:S(2)}) collective-permute-start(bf16[256,256]{1,0:T(8,128)(2,1)} %queries_ref.1), channel_id=1, source_target_pairs={{0,388},{1,389},{2,390},{3,391},{4,384},{5,385},{6,386},{7,387},{8... | collective-permute-start | bytes 393224 | tf_op jit(solution)/shard_map/ppermute | solution.py:38
  6.7 4.3 %collective-permute-done.far_ref = bf16[256,256]{1,0:T(8,128)(2,1)S(1)} collective-permute-done((bf16[256,256]{1,0:T(8,128)(2,1)}, bf16[256,256]{1,0:T(8,128)(2,1)S(1)}, u32[]{:S(2)}, u32[]{:S(2)}) %collective-permute-start) | collective-permute-done | bytes 131104 | tf_op jit(solution)/shard_map/ppermute | solution.py:38
  11.0 0.9 copy-done.4
  11.9 1.1 spread.1
  13.0 0.0 copy-start.10
  13.0 4.5 %all-to-all-start = ((bf16[4,2,256,256]{3,2,1,0:T(8,128)(2,1)}), bf16[4,2,256,256]{3,2,1,0:T(8,128)(2,1)S(1)}, u32[]{:S(2)}, u32[]{:S(2)}) async-start(bf16[4,2,256,256]{3,2,1,0:T(8,128)(2,1)} %spread.1), calls=%async_computation | async-start | bytes 2097152 | tf_op jit(solution)/shard_map/all_to_all | solution.py:242
  17.5 0.0 copy-done.5
  17.5 0.0 copy-done.6
  17.5 0.0 copy-done.8
  17.5 0.0 copy-done.9
  17.5 0.0 copy-done.10
  17.5 0.0 copy-start.7
  17.6 1.2 %copy-done.7 = bf16[2048,256]{1,0:T(8,128)(2,1)S(1)} copy-done((bf16[2048,256]{1,0:T(8,128)(2,1)S(1)}, bf16[2048,256]{1,0:T(8,128)(2,1)}, u32[]{:S(2)}) %copy-start.7) | copy-done | bytes 1048600
  18.8 1.8 %lookup.1 = (f32[16,128]{1,0:T(8,128)S(1)}, f32[1,256]{1,0:T(1,128)S(1)}, bf16[2048,256]{1,0:T(8,128)(2,1)S(1)}) custom-call(s32[1]{0:T(128)} %bitcast.1.place_ref, s32[512,128]{1,0:T(8,128)S(1)} %bitcast.20, s32[16,128]{1,0:T(8,128)S(1)} %bitcast.21, s32[2,128]{1,0:T(2,128)S(1)} %bitcast.22, bf16[256,256]{1,0:T(8,128)(2,1)S(1)} %copy-done.5, ...), custom_call_target="tpu_custom_call" | custom-call | flops 1000000000 | bytes 2000000 | tf_op jit(solution)/shard_map/lookup/pallas_call | solution.py:261
  20.6 11.1 %all-to-all-done.blocks_hbm = bf16[4,2,256,256]{3,2,1,0:T(8,128)(2,1)S(1)} async-done(((bf16[4,2,256,256]{3,2,1,0:T(8,128)(2,1)}), bf16[4,2,256,256]{3,2,1,0:T(8,128)(2,1)S(1)}, u32[]{:S(2)}, u32[]{:S(2)}) %all-to-all-start) | async-done | bytes 1048608 | tf_op jit(solution)/shard_map/all_to_all | solution.py:242
  31.7 5.3 %stats.1 = f32[4,8,256]{2,1,0:T(8,128)S(1)} custom-call(s32[1]{0:T(128)} %bitcast.spot_ref, bf16[4,2,256,256]{3,2,1,0:T(8,128)(2,1)S(1)} %all-to-all-done.blocks_hbm, bf16[2048,256]{1,0:T(8,128)(2,1)S(1)} %get-tuple-element.15.negatives_ref, f32[16,128]{1,0:T(8,128)S(1)} %get-tuple-element.16.rows_ref, f32[1,256]{1,0:T(1,128)S(1)} %get-tuple-element.17.score_ref), custom_call_target="tpu_custom_call" | custom-call | flops 2147483648 | bytes 4000000 | tf_op jit(solution)/shard_map/stats/pallas_call | solution.py:301
  37.0 7.8 %all_to_all.15.parts_ref = f32[4,8,256]{2,1,0:T(8,128)S(1)} all-to-all(f32[4,8,256]{2,1,0:T(8,128)S(1)} %stats.1), channel_id=1, replica_groups={{0,1,2,3},{4,5,6,7},{8,9,10,11},{12,13,14,15},{16,17,18,19},{20,21,22,2..., dimensions={0} | all-to-all | bytes 65536 | tf_op jit(solution)/shard_map/all_to_all | solution.py:242
  44.9 6.2 %collective-permute-start.1 = (f32[8,256]{1,0:T(8,128)S(1)}, f32[8,256]{1,0:T(8,128)S(1)}, u32[]{:S(2)}, u32[]{:S(2)}) collective-permute-start(f32[8,256]{1,0:T(8,128)S(1)} %join.1.joined_ref), channel_id=1, source_target_pairs={{0,388},{1,389},{2,390},{3,391},{4,384},{5,385},{6,386},{7,387},{8... | collective-permute-start | bytes 24584 | tf_op jit(solution)/shard_map/ppermute | solution.py:38
  51.1 0.6 copy.10
  51.8 1.7 %collective-permute-done.1.other_ref = f32[8,256]{1,0:T(8,128)S(1)} collective-permute-done((f32[8,256]{1,0:T(8,128)S(1)}, f32[8,256]{1,0:T(8,128)S(1)}, u32[]{:S(2)}, u32[]{:S(2)}) %collective-permute-start.1) | collective-permute-done | bytes 8224 | tf_op jit(solution)/shard_map/ppermute | solution.py:38
  53.4 7.4 %grads.1 = (f32[2,256,256]{2,1,0:T(8,128)S(1)}, f32[2,256,256]{2,1,0:T(8,128)S(1)}, f32[2,256,256]{2,1,0:T(8,128)S(1)}, f32[2,256,256]{2,1,0:T(8,128)S(1)}, f32[...) custom-call(s32[1]{0:T(128)} %bitcast.spot_ref, ...), custom_call_target="tpu_custom_call" | custom-call | flops 6442450944 | bytes 8000000 | tf_op jit(solution)/shard_map/grads/pallas_call | solution.py:321
  60.8 0.0 copy-start
  60.9 0.0 copy-start.2
  60.9 1.9 %collective-permute-start.7 = (f32[1024,256]{1,0:T(8,128)S(1)}, f32[1024,256]{1,0:T(8,128)S(1)}, u32[]{:S(2)}, u32[]{:S(2)}) collective-permute-start(f32[1024,256]{1,0:T(8,128)S(1)} %get-tuple-element.26), channel_id=1, source_target_pairs={{0,8},{8,0},{16,24},{24,16},{32,40},{40,32},{48,56},{56,48},{64,72... | collective-permute-start | bytes 3145736 | tf_op jit(solution)/shard_map/ppermute | solution.py:48
  62.9 2.5 %collective-permute-start.4 = (f16[2,256,256]{2,1,0:T(8,128)(2,1)S(1)}, f16[2,256,256]{2,1,0:T(8,128)(2,1)S(1)}, u32[]{:S(2)}, u32[]{:S(2)}) collective-permute-start(f16[2,256,256]{2,1,0:T(8,128)(2,1)S(1)} %convert_element_type.66), channel_id=1, source_target_pairs={{0,1},{1,0},{2,3},{3,2},{4,5},{5,4},{6,7},{7,6},{8,9},{9,8},{10,11... | collective-permute-start | bytes 786440 | tf_op jit(solution)/shard_map/ppermute | solution.py:43
  65.4 3.0 %collective-permute-start.2 = (f16[2,256,256]{2,1,0:T(8,128)(2,1)S(1)}, f16[2,256,256]{2,1,0:T(8,128)(2,1)S(1)}, u32[]{:S(2)}, u32[]{:S(2)}) collective-permute-start(f16[2,256,256]{2,1,0:T(8,128)(2,1)S(1)} %convert_element_type.60), channel_id=1, source_target_pairs={{0,3},{1,2},{2,1},{3,0},{4,7},{5,6},{6,5},{7,4},{8,11},{9,10},{10,... | collective-permute-start | bytes 786440 | tf_op jit(solution)/shard_map/ppermute | solution.py:43
  68.4 5.1 %collective-permute-done.4 = f16[2,256,256]{2,1,0:T(8,128)(2,1)S(1)} collective-permute-done((f16[2,256,256]{2,1,0:T(8,128)(2,1)S(1)}, f16[2,256,256]{2,1,0:T(8,128)(2,1)S(1)}, u32[]{:S(2)}, u32[]{:S(2)}) %collective-permute-start.4) | collective-permute-done | bytes 262176 | tf_op jit(solution)/shard_map/ppermute | solution.py:43
  73.5 3.4 %collective-permute-done.2 = f16[2,256,256]{2,1,0:T(8,128)(2,1)S(1)} collective-permute-done((f16[2,256,256]{2,1,0:T(8,128)(2,1)S(1)}, f16[2,256,256]{2,1,0:T(8,128)(2,1)S(1)}, u32[]{:S(2)}, u32[]{:S(2)}) %collective-permute-start.2) | collective-permute-done | bytes 262176 | tf_op jit(solution)/shard_map/ppermute | solution.py:43
  76.9 0.0 collective-permute-done.7.got_ref
  76.9 0.3 sum_cores.1
  77.2 0.0 copy-done
  77.2 0.0 copy-done.2
  77.3 1.0 convert_element_type.76
  78.2 13.5 %all-to-all-start.2 = ((f16[32,40,256]{2,1,0:T(8,128)(2,1)}), f16[32,40,256]{2,1,0:T(8,128)(2,1)S(1)}, u32[]{:S(2)}, u32[]{:S(2)}) async-start(f16[32,40,256]{2,1,0:T(8,128)(2,1)} %convert_element_type.76), calls=%async_computation.2 | async-start | bytes 1310720 | tf_op jit(solution)/shard_map/all_to_all | solution.py:242
  91.7 0.0 copy-done.3
  91.8 3.0 %collective-permute-start.5 = (f16[256,256]{1,0:T(8,128)(2,1)S(1)}, f16[256,256]{1,0:T(8,128)(2,1)S(1)}, u32[]{:S(2)}, u32[]{:S(2)}) collective-permute-start(f16[256,256]{1,0:T(8,128)(2,1)S(1)} %fusion.3), channel_id=1, source_target_pairs={{0,3},{1,2},{2,1},{3,0},{4,7},{5,6},{6,5},{7,4},{8,11},{9,10},{10,... | collective-permute-start | bytes 393224 | tf_op jit(solution)/shard_map/ppermute | solution.py:43
  94.8 0.0 copy-done.1
  94.8 1.9 %collective-permute-start.3 = (f16[256,256]{1,0:T(8,128)(2,1)S(1)}, f16[256,256]{1,0:T(8,128)(2,1)S(1)}, u32[]{:S(2)}, u32[]{:S(2)}) collective-permute-start(f16[256,256]{1,0:T(8,128)(2,1)S(1)} %fusion.2), channel_id=1, source_target_pairs={{0,1},{1,0},{2,3},{3,2},{4,5},{5,4},{6,7},{7,6},{8,9},{9,8},{10,11... | collective-permute-start | bytes 393224 | tf_op jit(solution)/shard_map/ppermute | solution.py:43
  96.7 3.1 %collective-permute-done.5 = f16[256,256]{1,0:T(8,128)(2,1)S(1)} collective-permute-done((f16[256,256]{1,0:T(8,128)(2,1)S(1)}, f16[256,256]{1,0:T(8,128)(2,1)S(1)}, u32[]{:S(2)}, u32[]{:S(2)}) %collective-permute-start.5) | collective-permute-done | bytes 131104 | tf_op jit(solution)/shard_map/ppermute | solution.py:43
  99.8 0.1 fusion.1
  99.9 5.5 %collective-permute-start.6 = (f16[256,256]{1,0:T(8,128)(2,1)S(1)}, f16[256,256]{1,0:T(8,128)(2,1)S(1)}, u32[]{:S(2)}, u32[]{:S(2)}) collective-permute-start(f16[256,256]{1,0:T(8,128)(2,1)S(1)} %fusion.1), channel_id=1, source_target_pairs={{0,388},{1,389},{2,390},{3,391},{4,384},{5,385},{6,386},{7,387},{8... | collective-permute-start | bytes 393224 | tf_op jit(solution)/shard_map/ppermute | solution.py:38
  105.4 0.0 collective-permute-done.3
  105.5 4.7 %collective-permute-done.6 = f16[256,256]{1,0:T(8,128)(2,1)S(1)} collective-permute-done((f16[256,256]{1,0:T(8,128)(2,1)S(1)}, f16[256,256]{1,0:T(8,128)(2,1)S(1)}, u32[]{:S(2)}, u32[]{:S(2)}) %collective-permute-start.6) | collective-permute-done | bytes 131104 | tf_op jit(solution)/shard_map/ppermute | solution.py:38
  110.3 0.9 finish.1
  111.2 0.0 all-to-all-done.2
  111.2 0.1 convert_element_type.77
  111.3 0.3 fusion.6
  111.6 0.8 fusion
  (15 shorter events, 0.3 us)
Async XLA Ops:
  0.6 10.4 %collective-permute-start = (bf16[256,256]{1,0:T(8,128)(2,1)}, bf16[256,256]{1,0:T(8,128)(2,1)S(1)}, u32[]{:S(2)}, u32[]{:S(2)}) collective-permute-start(bf16[256,256]{1,0:T(8,128)(2,1)} %queries_ref.1), channel_id=1, source_target_pairs={{0,388},{1,389},{2,390},{3,391},{4,384},{5,385},{6,386},{7,387},{8... | collective-permute-start | bytes 393224 | tf_op jit(solution)/shard_map/ppermute | solution.py:38
  11.0 0.9 copy-start.4
  13.0 4.5 %copy-start.5 = (bf16[256,256]{1,0:T(8,128)(2,1)S(1)}, bf16[256,256]{1,0:T(8,128)(2,1)}, u32[]{:S(2)}) copy-start(bf16[256,256]{1,0:T(8,128)(2,1)} %queries_ref.1) | copy-start | bytes 393220
  13.0 4.5 %copy-start.6 = (bf16[256,256]{1,0:T(8,128)(2,1)S(1)}, bf16[256,256]{1,0:T(8,128)(2,1)}, u32[]{:S(2)}) copy-start(bf16[256,256]{1,0:T(8,128)(2,1)} %pos_ref.3) | copy-start | bytes 393220
  13.0 4.6 %copy-start.8 = (s32[65536]{0:T(1024)S(1)}, s32[65536]{0:T(1024)}, u32[]{:S(2)}) copy-start(s32[65536]{0:T(1024)} %param.11) | copy-start | bytes 786436
  13.0 4.6 %copy-start.9 = (s32[2048]{0:T(1024)S(1)}, s32[2048]{0:T(1024)}, u32[]{:S(2)}) copy-start(s32[2048]{0:T(1024)} %param.10) | copy-start | bytes 24580
  13.0 4.6 %copy-start.10 = (s32[256]{0:T(256)S(1)}, s32[256]{0:T(256)}, u32[]{:S(2)}) copy-start(s32[256]{0:T(256)} %param.9) | copy-start | bytes 3076
  13.0 18.7 %all-to-all-start = ((bf16[4,2,256,256]{3,2,1,0:T(8,128)(2,1)}), bf16[4,2,256,256]{3,2,1,0:T(8,128)(2,1)S(1)}, u32[]{:S(2)}, u32[]{:S(2)}) async-start(bf16[4,2,256,256]{3,2,1,0:T(8,128)(2,1)} %spread.1), calls=%async_computation | async-start | bytes 2097152 | tf_op jit(solution)/shard_map/all_to_all | solution.py:242
  17.5 1.2 %copy-start.7 = (bf16[2048,256]{1,0:T(8,128)(2,1)S(1)}, bf16[2048,256]{1,0:T(8,128)(2,1)}, u32[]{:S(2)}) copy-start(bf16[2048,256]{1,0:T(8,128)(2,1)} %negatives_ref.1) | copy-start | bytes 3145732
  44.9 8.6 %collective-permute-start.1 = (f32[8,256]{1,0:T(8,128)S(1)}, f32[8,256]{1,0:T(8,128)S(1)}, u32[]{:S(2)}, u32[]{:S(2)}) collective-permute-start(f32[8,256]{1,0:T(8,128)S(1)} %join.1.joined_ref), channel_id=1, source_target_pairs={{0,388},{1,389},{2,390},{3,391},{4,384},{5,385},{6,386},{7,387},{8... | collective-permute-start | bytes 24584 | tf_op jit(solution)/shard_map/ppermute | solution.py:38
  60.8 16.4 %copy-start = (f32[2,256,256]{2,1,0:T(8,128)}, f32[2,256,256]{2,1,0:T(8,128)S(1)}, u32[]{:S(2)}) copy-start(f32[2,256,256]{2,1,0:T(8,128)S(1)} %get-tuple-element.18) | copy-start | bytes 1572868
  60.9 16.4 %copy-start.2 = (f32[2,256,256]{2,1,0:T(8,128)}, f32[2,256,256]{2,1,0:T(8,128)S(1)}, u32[]{:S(2)}) copy-start(f32[2,256,256]{2,1,0:T(8,128)S(1)} %get-tuple-element.20) | copy-start | bytes 1572868
  60.9 16.0 %collective-permute-start.7 = (f32[1024,256]{1,0:T(8,128)S(1)}, f32[1024,256]{1,0:T(8,128)S(1)}, u32[]{:S(2)}, u32[]{:S(2)}) collective-permute-start(f32[1024,256]{1,0:T(8,128)S(1)} %get-tuple-element.26), channel_id=1, source_target_pairs={{0,8},{8,0},{16,24},{24,16},{32,40},{40,32},{48,56},{56,48},{64,72... | collective-permute-start | bytes 3145736 | tf_op jit(solution)/shard_map/ppermute | solution.py:48
  62.9 10.6 %collective-permute-start.4 = (f16[2,256,256]{2,1,0:T(8,128)(2,1)S(1)}, f16[2,256,256]{2,1,0:T(8,128)(2,1)S(1)}, u32[]{:S(2)}, u32[]{:S(2)}) collective-permute-start(f16[2,256,256]{2,1,0:T(8,128)(2,1)S(1)} %convert_element_type.66), channel_id=1, source_target_pairs={{0,1},{1,0},{2,3},{3,2},{4,5},{5,4},{6,7},{7,6},{8,9},{9,8},{10,11... | collective-permute-start | bytes 786440 | tf_op jit(solution)/shard_map/ppermute | solution.py:43
  65.4 11.5 %collective-permute-start.2 = (f16[2,256,256]{2,1,0:T(8,128)(2,1)S(1)}, f16[2,256,256]{2,1,0:T(8,128)(2,1)S(1)}, u32[]{:S(2)}, u32[]{:S(2)}) collective-permute-start(f16[2,256,256]{2,1,0:T(8,128)(2,1)S(1)} %convert_element_type.60), channel_id=1, source_target_pairs={{0,3},{1,2},{2,1},{3,0},{4,7},{5,6},{6,5},{7,4},{8,11},{9,10},{10,... | collective-permute-start | bytes 786440 | tf_op jit(solution)/shard_map/ppermute | solution.py:43
  78.2 13.5 %copy-start.3 = (f32[2,256,256]{2,1,0:T(8,128)S(1)}, f32[2,256,256]{2,1,0:T(8,128)}, u32[]{:S(2)}) copy-start(f32[2,256,256]{2,1,0:T(8,128)} %copy-done.2) | copy-start | bytes 1572868
  78.2 16.5 %copy-start.1 = (f32[2,256,256]{2,1,0:T(8,128)S(1)}, f32[2,256,256]{2,1,0:T(8,128)}, u32[]{:S(2)}) copy-start(f32[2,256,256]{2,1,0:T(8,128)} %copy-done) | copy-start | bytes 1572868
  78.2 32.9 %all-to-all-start.2 = ((f16[32,40,256]{2,1,0:T(8,128)(2,1)}), f16[32,40,256]{2,1,0:T(8,128)(2,1)S(1)}, u32[]{:S(2)}, u32[]{:S(2)}) async-start(f16[32,40,256]{2,1,0:T(8,128)(2,1)} %convert_element_type.76), calls=%async_computation.2 | async-start | bytes 1310720 | tf_op jit(solution)/shard_map/all_to_all | solution.py:242
  91.8 8.1 %collective-permute-start.5 = (f16[256,256]{1,0:T(8,128)(2,1)S(1)}, f16[256,256]{1,0:T(8,128)(2,1)S(1)}, u32[]{:S(2)}, u32[]{:S(2)}) collective-permute-start(f16[256,256]{1,0:T(8,128)(2,1)S(1)} %fusion.3), channel_id=1, source_target_pairs={{0,3},{1,2},{2,1},{3,0},{4,7},{5,6},{6,5},{7,4},{8,11},{9,10},{10,... | collective-permute-start | bytes 393224 | tf_op jit(solution)/shard_map/ppermute | solution.py:43
  94.8 10.6 %collective-permute-start.3 = (f16[256,256]{1,0:T(8,128)(2,1)S(1)}, f16[256,256]{1,0:T(8,128)(2,1)S(1)}, u32[]{:S(2)}, u32[]{:S(2)}) collective-permute-start(f16[256,256]{1,0:T(8,128)(2,1)S(1)} %fusion.2), channel_id=1, source_target_pairs={{0,1},{1,0},{2,3},{3,2},{4,5},{5,4},{6,7},{7,6},{8,9},{9,8},{10,11... | collective-permute-start | bytes 393224 | tf_op jit(solution)/shard_map/ppermute | solution.py:43
  99.9 10.3 %collective-permute-start.6 = (f16[256,256]{1,0:T(8,128)(2,1)S(1)}, f16[256,256]{1,0:T(8,128)(2,1)S(1)}, u32[]{:S(2)}, u32[]{:S(2)}) collective-permute-start(f16[256,256]{1,0:T(8,128)(2,1)S(1)} %fusion.1), channel_id=1, source_target_pairs={{0,388},{1,389},{2,390},{3,391},{4,384},{5,385},{6,386},{7,387},{8... | collective-permute-start | bytes 393224 | tf_op jit(solution)/shard_map/ppermute | solution.py:38

commit v4 on v3

--- a/solution.py
+++ b/solution.py
@@ -127,27 +127,38 @@
         out_ref[k * LANES : (k + 1) * LANES, :] = tall
 
 
-def stats_kernel(
-    spot_ref, blocks_hbm, negatives_ref, rows_ref, score_ref, out_ref, blocks_ref, corr_ref, sem
+def near_stats_kernel(
+    spot_ref, own_ref, first_ref, second_ref, negatives_ref, rows_ref, score_ref, out_ref, corr_ref
+):
+    to_columns(rows_ref, corr_ref)
+    for k, block in enumerate(near_order(own_ref, first_ref, second_ref)):
+        row_max, row_sum = row_stats(block, negatives_ref, corr_ref)
+        if k == 0:
+            score = score_ref[...]
+            joined = jnp.maximum(row_max, score)
+            row_sum = row_sum * jnp.exp(row_max - joined) + jnp.exp(score - joined)
+            row_max = joined
+        out_ref[pl.ds(spot_ref[0] ^ k, 1), :] = row_max + jnp.log(row_sum)
+
+
+def far_stats_kernel(
+    blocks_hbm, negatives_ref, rows_ref, near_ref, out_ref, blocks_ref, corr_ref, sem
 ):
     fetch = pltpu.make_async_copy(blocks_hbm, blocks_ref, sem)
     fetch.start()
     to_columns(rows_ref, corr_ref)
+    for c in range(NEAR):
+        out_ref[c, :NEAR, :] = near_ref[...]
     fetch.wait()
-    score = score_ref[...]
-    for side in range(FAR):
-        for k in range(NEAR):
-            row_max, row_sum = row_stats(blocks_ref[k, side], negatives_ref, corr_ref)
-            if side == 0:
-                own = spot_ref[0] == k
-                joined = jnp.where(own, jnp.maximum(row_max, score), row_max)
-                extra = jnp.exp(jnp.where(own, score, joined) - joined)
-                row_sum = row_sum * jnp.exp(row_max - joined) + jnp.where(own, extra, 0.0)
-                row_max = joined
-            lse = row_max + jnp.log(row_sum)
-            place = side * NEAR + k
-            for c in range(NEAR):
-                out_ref[c, place : place + 1, :] = lse
+    for k in range(NEAR):
+        row_max, row_sum = row_stats(blocks_ref[k], negatives_ref, corr_ref)
+        lse = row_max + jnp.log(row_sum)
+        for c in range(NEAR):
+            out_ref[c, NEAR + k : NEAR + k + 1, :] = lse
+
+
+def near_order(own_ref, first_ref, second_ref):
+    return [own_ref[...], second_ref[0], second_ref[1], first_ref[...]]
 
 
 def join(parts):
@@ -160,7 +171,8 @@
 
 
 def grads_kernel(
-    spot_ref, blocks_hbm, joined_ref, other_ref, negatives_ref, turned_ref, rows_ref, *refs
+    spot_ref, own_ref, first_ref, second_ref, blocks_hbm, joined_ref, other_ref, negatives_ref,
+    turned_ref, rows_ref, *refs
 ):
     query_outs, refs = refs[: 2 * FAR], refs[2 * FAR :]
     keep_out, send_out, lse_out, boost_ref, weight_ref, blocks_ref, corr_ref, sem = refs
@@ -175,12 +187,16 @@
     lse_out[...] = lse_all
     boost_ref[...] = jnp.exp(jnp.minimum(lse_all - joined, SPAN))
     half = total // CORES
-    fetch.wait()
     for side in range(FAR):
         places = [spot ^ k for k in range(NEAR)]
         lse = [lse_out[pl.ds(side * NEAR + k, 1), :] for k in places]
         lse = jnp.concatenate(lse, axis=1)
-        block = jnp.concatenate([blocks_ref[k, side] for k in places], axis=0)
+        if side == 0:
+            block = near_order(own_ref, first_ref, second_ref)
+        else:
+            fetch.wait()
+            block = [blocks_ref[k] for k in places]
+        block = jnp.concatenate(block, axis=0)
         rows = block.shape[0]
         own = rows // NEAR
         for start in range(0, total, SPLIT):
@@ -204,10 +220,9 @@
             out[place] = term * boost_ref[pl.ds(side * NEAR + k, 1), :]
 
 
-def spread_kernel(near_ref, far_ref, out_ref):
+def spread_kernel(block_ref, arrived_ref, out_ref):
     for k in range(NEAR):
-        out_ref[k, 0] = near_ref[...]
-        out_ref[k, 1] = far_ref[...]
+        out_ref[k] = block_ref[...]
 
 
 def sum_cores_kernel(keep_ref, got_ref, arrived_ref, out_ref):
@@ -257,6 +272,7 @@
     sheets = [[g * CORES + c for g in range(LINE * RING)] for c in range(CORES)]
 
     across = mirror(queries)
+    first = swap_near(queries, 3)
 
     corr, score, ordered = pl.pallas_call(
         lookup_kernel,
@@ -282,32 +298,44 @@
     )
     turned = ordered.T
 
-    blocks = pl.pallas_call(
+    far_blocks = pl.pallas_call(
         spread_kernel,
-        in_specs=[vmem] * 2,
+        in_specs=[vmem, hbm],
         out_specs=vmem,
-        out_shape=like((NEAR, FAR, own, width), jnp.bfloat16),
-        compiler_params=params(),
+        out_shape=like((NEAR, own, width), jnp.bfloat16),
+        compiler_params=params(),
+        cost_estimate=cost(10**6, 10**6, 0),
         name="spread",
-    )(queries, across)
-    blocks = trade(blocks, "neg", rows)
+    )(across, first)
+    far_blocks = trade(far_blocks, "neg", rows)
+    near_blocks = (queries, first, swap_near(jnp.stack([queries, first]), 1))
 
     pairs = parts * own * shard
     fetched = [
-        pltpu.VMEM((NEAR, FAR, own, width), jnp.bfloat16),
+        pltpu.VMEM((NEAR, own, width), jnp.bfloat16),
         pltpu.VMEM((shard, LANES), f32),
         pltpu.SemaphoreType.DMA,
     ]
+    near_stats = pl.pallas_call(
+        near_stats_kernel,
+        in_specs=[smem] + [vmem] * 6,
+        out_specs=vmem,
+        out_shape=like((NEAR, own), f32),
+        scratch_shapes=[pltpu.VMEM((shard, LANES), f32)],
+        compiler_params=params(),
+        cost_estimate=cost(pairs * width, 2 * 10**6, pairs // 2),
+        name="near_stats",
+    )(spot, *near_blocks, ordered, corr, score)
     stats = pl.pallas_call(
-        stats_kernel,
-        in_specs=[smem, hbm] + [vmem] * 3,
+        far_stats_kernel,
+        in_specs=[hbm] + [vmem] * 3,
         out_specs=vmem,
         out_shape=like((NEAR, parts, own), f32),
         scratch_shapes=fetched,
         compiler_params=params(),
-        cost_estimate=cost(2 * pairs * width, 4 * 10**6, pairs),
-        name="stats",
-    )(spot, blocks, ordered, corr, score)
+        cost_estimate=cost(pairs * width, 2 * 10**6, pairs // 2),
+        name="far_stats",
+    )(far_blocks, ordered, corr, near_stats)
     joined = pl.pallas_call(
         join_kernel,
         in_specs=[vmem],
@@ -320,7 +348,7 @@
 
     near_keep, near_send, far_keep, far_send, keep, send, lse = pl.pallas_call(
         grads_kernel,
-        in_specs=[smem, hbm] + [vmem] * 5,
+        in_specs=[smem] + [vmem] * 3 + [hbm] + [vmem] * 5,
         out_specs=(vmem,) * (2 * FAR + 3),
         out_shape=(
             *[like((2, width, own), f32)] * (2 * FAR),
@@ -336,7 +364,7 @@
         compiler_params=params(24),
         cost_estimate=cost(6 * pairs * width, 8 * 10**6, pairs),
         name="grads",
-    )(spot, blocks, joined, other, ordered, turned, corr)
+    )(spot, *near_blocks, far_blocks, joined, other, ordered, turned, corr)
     from_core = other_core(send)
 
     def halve(side, keep, got):

time: 113 us -> 117 us (1.035)
  starting transfers between devices: 48.1 us -> 50.5 us
  blocking collectives: 7.8 us -> 9.16 us
  waiting for transfers between devices: 33.5 us -> 32.2 us
    all_to_all x2, waiting for transfers between devices: 11.1 us -> 0.01 us  [trade(): lax.all_to_all(value, axis, 0, 0, tiled=True, axis_index_groups=groups)]
    ppermute x4 -> x6, waiting for transfers between devices: 11.6 us -> 20.9 us  [swap_near(): return lax.ppermute(value, 'neg', perm)]
    ppermute x4 -> x6, starting transfers between devices: 10.4 us -> 19 us  [swap_near(): return lax.ppermute(value, 'neg', perm)]
    ppermute x3, starting transfers between devices: 17.8 us -> 12.7 us  [mirror(): return lax.ppermute(value, ('dp', 'neg'), perm)]
    all_to_all x1, blocking collectives: 7.8 us -> 9.16 us  [trade(): lax.all_to_all(value, axis, 0, 0, tiled=True, axis_index_groups=groups)]
    unnamed x22 -> x34, local copies, waits for them, and re-layouts: 2.16 us -> 3 us
    pallas_call x3 -> x4, Pallas kernels: 13.8 us -> 13.6 us  [the longest x1 7.28 us: per_device(): pl.pallas_call(grads_kernel, in_specs=[smem] + [vmem] * 3 + [hbm] + [vmem...]
  transfers between devices with their start and end apart: 10 -> 12, of which waited for: 7 -> 7; matrix products, arithmetic and copies ran while one was open for 1% -> 1% of each run, Pallas kernels for 2% -> 5%
where the time goes in v4:
time: 117 us; the launch traced here: 116 us
  starting transfers between devices  50.5 us (43%)
  waiting for transfers between devices  32.2 us (28%)
  Pallas kernels  16.6 us (14%)
  blocking collectives  9.16 us (8%)
  local copies, waits for them, and re-layouts  3.64 us (3%)
  other arithmetic  3.14 us (3%)
    ppermute x6, waiting for transfers between devices, swap_near(): return lax.ppermute(value, 'neg', perm)  20.9 us
    ppermute x6, starting transfers between devices, swap_near(): return lax.ppermute(value, 'neg', perm)  19 us
    all_to_all x2, starting transfers between devices, trade(): lax.all_to_all(value, axis, 0, 0, tiled=True, axis_index_groups=groups)  16.9 us
    ppermute x3, starting transfers between devices, mirror(): return lax.ppermute(value, ('dp', 'neg'), perm)  12.7 us
    ppermute x3, waiting for transfers between devices, mirror(): return lax.ppermute(value, ('dp', 'neg'), perm)  11.2 us
    all_to_all x1, blocking collectives, trade(): lax.all_to_all(value, axis, 0, 0, tiled=True, axis_index_groups=groups)  9.16 us
    pallas_call x1, Pallas kernels, per_device(): pl.pallas_call(grads_kernel, in_specs=[smem] + [vmem] * 3 + [hbm] + [vmem...  7.28 us
    unnamed x34, local copies, waits for them, and re-layouts  3 us
  transfers between devices with their start and end apart: 12, of which 7 were waited for; matrix products, arithmetic and copies ran while one was open for 1% of the time, Pallas kernels for 5%

profile of v4, /device:TPU:8, one launch (start us, length us, event | category | flops | bytes accessed | tf_op | source)
XLA Modules:
  0.0 116.2 jit_solution(6142064890757894783)
XLA Ops:
  0.7 6.2 %collective-permute-start.2 = (bf16[256,256]{1,0:T(8,128)(2,1)}, bf16[256,256]{1,0:T(8,128)(2,1)S(1)}, u32[]{:S(2)}, u32[]{:S(2)}) collective-permute-start(bf16[256,256]{1,0:T(8,128)(2,1)} %own_ref.3), channel_id=1, source_target_pairs={{0,388},{1,389},{2,390},{3,391},{4,384},{5,385},{6,386},{7,387},{8... | collective-permute-start | bytes 393224 | tf_op jit(solution)/shard_map/ppermute | solution.py:38
  6.9 4.7 %collective-permute-start = (bf16[256,256]{1,0:T(8,128)(2,1)}, bf16[256,256]{1,0:T(8,128)(2,1)S(1)}, u32[]{:S(2)}, u32[]{:S(2)}) collective-permute-start(bf16[256,256]{1,0:T(8,128)(2,1)} %own_ref.3), channel_id=1, source_target_pairs={{0,3},{1,2},{2,1},{3,0},{4,7},{5,6},{6,5},{7,4},{8,11},{9,10},{10,... | collective-permute-start | bytes 393224 | tf_op jit(solution)/shard_map/ppermute | solution.py:43
  11.6 0.0 collective-permute-done.2.block_ref
  11.6 3.6 %collective-permute-done.arrived_ref.first_ref = bf16[256,256]{1,0:T(8,128)(2,1)S(1)} collective-permute-done((bf16[256,256]{1,0:T(8,128)(2,1)}, bf16[256,256]{1,0:T(8,128)(2,1)S(1)}, u32[]{:S(2)}, u32[]{:S(2)}) %collective-permute-start) | collective-permute-done | bytes 131104 | tf_op jit(solution)/shard_map/ppermute | solution.py:43
  15.2 0.8 spread.1
  16.0 4.0 %all-to-all-start = ((bf16[4,256,256]{2,1,0:T(8,128)(2,1)}), bf16[4,256,256]{2,1,0:T(8,128)(2,1)S(1)}, u32[]{:S(2)}, u32[]{:S(2)}) async-start(bf16[4,256,256]{2,1,0:T(8,128)(2,1)} %spread.1), calls=%async_computation | async-start | bytes 1048576 | tf_op jit(solution)/shard_map/all_to_all | solution.py:257
  20.0 0.7 pad_maximum_fusion
  20.8 3.9 %collective-permute-start.1 = (bf16[2,256,256]{2,1,0:T(8,128)(2,1)}, bf16[2,256,256]{2,1,0:T(8,128)(2,1)S(1)}, u32[]{:S(2)}, u32[]{:S(2)}) collective-permute-start(bf16[2,256,256]{2,1,0:T(8,128)(2,1)} %pad_maximum_fusion), channel_id=1, source_target_pairs={{0,1},{1,0},{2,3},{3,2},{4,5},{5,4},{6,7},{7,6},{8,9},{9,8},{10,11... | collective-permute-start | bytes 786440 | tf_op jit(solution)/shard_map/ppermute | solution.py:43
  24.8 1.8 %lookup.1 = (f32[16,128]{1,0:T(8,128)S(1)}, f32[1,256]{1,0:T(1,128)S(1)}, bf16[2048,256]{1,0:T(8,128)(2,1)S(1)}) custom-call(s32[1]{0:T(128)} %bitcast.3.place_ref, s32[512,128]{1,0:T(8,128)S(1)} %bitcast.24, s32[16,128]{1,0:T(8,128)S(1)} %bitcast.25, s32[2,128]{1,0:T(2,128)S(1)} %bitcast.26, bf16[256,256]{1,0:T(8,128)(2,1)S(1)} %copy-done.2, ...), custom_call_target="tpu_custom_call" | custom-call | flops 1000000000 | bytes 2000000 | tf_op jit(solution)/shard_map/lookup/pallas_call | solution.py:277
  26.6 0.0 copy-start.6
  26.6 5.7 %collective-permute-done.1.second_ref = bf16[2,256,256]{2,1,0:T(8,128)(2,1)S(1)} collective-permute-done((bf16[2,256,256]{2,1,0:T(8,128)(2,1)}, bf16[2,256,256]{2,1,0:T(8,128)(2,1)S(1)}, u32[]{:S(2)}, u32[]{:S(2)}) %collective-permute-start.1) | collective-permute-done | bytes 262176 | tf_op jit(solution)/shard_map/ppermute | solution.py:43
  32.2 2.5 %near_stats.1.near_ref = f32[4,256]{1,0:T(4,128)S(1)} custom-call(s32[1]{0:T(128)} %bitcast.spot_ref, bf16[256,256]{1,0:T(8,128)(2,1)S(1)} %copy-done.2, bf16[256,256]{1,0:T(8,128)(2,1)S(1)} %collective-permute-done.arrived_ref.first_ref, bf16[2,256,256]{2,1,0:T(8,128)(2,1)S(1)} %collective-permute-done.1.second_ref, ...), custom_call_target="tpu_custom_call" | custom-call | flops 1073741824 | bytes 2000000 | tf_op jit(solution)/shard_map/near_stats/pallas_call | solution.py:319
  34.8 0.0 copy-start.14
  34.8 0.6 copy-done.14
  35.4 0.0 all-to-all-done.blocks_hbm
  35.4 0.7 copy-done.15
  36.1 2.9 %far_stats.1 = f32[4,8,256]{2,1,0:T(8,128)S(1)} custom-call(bf16[4,256,256]{2,1,0:T(8,128)(2,1)S(1)} %all-to-all-done.blocks_hbm, bf16[2048,256]{1,0:T(8,128)(2,1)S(1)} %get-tuple-element.15.negatives_ref, f32[16,128]{1,0:T(8,128)S(1)} %copy-done.15, f32[4,256]{1,0:T(4,128)S(1)} %near_stats.1.near_ref), custom_call_target="tpu_custom_call" | custom-call | flops 1073741824 | bytes 2000000 | tf_op jit(solution)/shard_map/far_stats/pallas_call | solution.py:329
  39.0 9.2 %all_to_all.15.parts_ref = f32[4,8,256]{2,1,0:T(8,128)S(1)} all-to-all(f32[4,8,256]{2,1,0:T(8,128)S(1)} %far_stats.1), channel_id=1, replica_groups={{0,1,2,3},{4,5,6,7},{8,9,10,11},{12,13,14,15},{16,17,18,19},{20,21,22,2..., dimensions={0} | all-to-all | bytes 65536 | tf_op jit(solution)/shard_map/all_to_all | solution.py:257
  48.2 3.2 %collective-permute-start.3 = (f32[8,256]{1,0:T(8,128)S(1)}, f32[8,256]{1,0:T(8,128)S(1)}, u32[]{:S(2)}, u32[]{:S(2)}) collective-permute-start(f32[8,256]{1,0:T(8,128)S(1)} %join.1.joined_ref), channel_id=1, source_target_pairs={{0,388},{1,389},{2,390},{3,391},{4,384},{5,385},{6,386},{7,387},{8... | collective-permute-start | bytes 24584 | tf_op jit(solution)/shard_map/ppermute | solution.py:38
  51.5 0.6 copy.10
  52.1 4.6 %collective-permute-done.3.other_ref = f32[8,256]{1,0:T(8,128)S(1)} collective-permute-done((f32[8,256]{1,0:T(8,128)S(1)}, f32[8,256]{1,0:T(8,128)S(1)}, u32[]{:S(2)}, u32[]{:S(2)}) %collective-permute-start.3) | collective-permute-done | bytes 8224 | tf_op jit(solution)/shard_map/ppermute | solution.py:38
  56.7 0.9 copy-done.11
  57.7 0.7 copy-done.16
  58.4 7.3 %grads.1 = (f32[2,256,256]{2,1,0:T(8,128)S(1)}, f32[2,256,256]{2,1,0:T(8,128)S(1)}, f32[2,256,256]{2,1,0:T(8,128)S(1)}, f32[2,256,256]{2,1,0:T(8,128)S(1)}, f32[...) custom-call(s32[1]{0:T(128)} %bitcast.spot_ref, bf16[256,256]{1,0:T(8,128)(2,1)S(1)} %copy-done.2, ...), custom_call_target="tpu_custom_call" | custom-call | flops 6442450944 | bytes 8000000 | tf_op jit(solution)/shard_map/grads/pallas_call | solution.py:349
  65.7 0.0 copy-start.4
  65.7 1.9 %collective-permute-start.9 = (f32[1024,256]{1,0:T(8,128)S(1)}, f32[1024,256]{1,0:T(8,128)S(1)}, u32[]{:S(2)}, u32[]{:S(2)}) collective-permute-start(f32[1024,256]{1,0:T(8,128)S(1)} %get-tuple-element.26), channel_id=1, source_target_pairs={{0,8},{8,0},{16,24},{24,16},{32,40},{40,32},{48,56},{56,48},{64,72... | collective-permute-start | bytes 3145736 | tf_op jit(solution)/shard_map/ppermute | solution.py:48
  67.7 2.5 %collective-permute-start.6 = (f16[2,256,256]{2,1,0:T(8,128)(2,1)S(1)}, f16[2,256,256]{2,1,0:T(8,128)(2,1)S(1)}, u32[]{:S(2)}, u32[]{:S(2)}) collective-permute-start(f16[2,256,256]{2,1,0:T(8,128)(2,1)S(1)} %convert_element_type.66), channel_id=1, source_target_pairs={{0,1},{1,0},{2,3},{3,2},{4,5},{5,4},{6,7},{7,6},{8,9},{9,8},{10,11... | collective-permute-start | bytes 786440 | tf_op jit(solution)/shard_map/ppermute | solution.py:43
  70.2 3.0 %collective-permute-start.4 = (f16[2,256,256]{2,1,0:T(8,128)(2,1)S(1)}, f16[2,256,256]{2,1,0:T(8,128)(2,1)S(1)}, u32[]{:S(2)}, u32[]{:S(2)}) collective-permute-start(f16[2,256,256]{2,1,0:T(8,128)(2,1)S(1)} %convert_element_type.60), channel_id=1, source_target_pairs={{0,3},{1,2},{2,1},{3,0},{4,7},{5,6},{6,5},{7,4},{8,11},{9,10},{10,... | collective-permute-start | bytes 786440 | tf_op jit(solution)/shard_map/ppermute | solution.py:43
  73.2 5.1 %collective-permute-done.6 = f16[2,256,256]{2,1,0:T(8,128)(2,1)S(1)} collective-permute-done((f16[2,256,256]{2,1,0:T(8,128)(2,1)S(1)}, f16[2,256,256]{2,1,0:T(8,128)(2,1)S(1)}, u32[]{:S(2)}, u32[]{:S(2)}) %collective-permute-start.6) | collective-permute-done | bytes 262176 | tf_op jit(solution)/shard_map/ppermute | solution.py:43
  78.3 3.4 %collective-permute-done.4 = f16[2,256,256]{2,1,0:T(8,128)(2,1)S(1)} collective-permute-done((f16[2,256,256]{2,1,0:T(8,128)(2,1)S(1)}, f16[2,256,256]{2,1,0:T(8,128)(2,1)S(1)}, u32[]{:S(2)}, u32[]{:S(2)}) %collective-permute-start.4) | collective-permute-done | bytes 262176 | tf_op jit(solution)/shard_map/ppermute | solution.py:43
  81.8 0.0 collective-permute-done.9.got_ref
  81.8 0.3 sum_cores.1
  82.1 1.0 convert_element_type.76
  83.1 12.9 %all-to-all-start.2 = ((f16[32,40,256]{2,1,0:T(8,128)(2,1)}), f16[32,40,256]{2,1,0:T(8,128)(2,1)S(1)}, u32[]{:S(2)}, u32[]{:S(2)}) async-start(f16[32,40,256]{2,1,0:T(8,128)(2,1)} %convert_element_type.76), calls=%async_computation.2 | async-start | bytes 1310720 | tf_op jit(solution)/shard_map/all_to_all | solution.py:257
  96.0 0.0 copy-start.5
  96.0 0.0 copy-start.7
  96.0 3.0 %collective-permute-start.7 = (f16[256,256]{1,0:T(8,128)(2,1)S(1)}, f16[256,256]{1,0:T(8,128)(2,1)S(1)}, u32[]{:S(2)}, u32[]{:S(2)}) collective-permute-start(f16[256,256]{1,0:T(8,128)(2,1)S(1)} %fusion.3), channel_id=1, source_target_pairs={{0,3},{1,2},{2,1},{3,0},{4,7},{5,6},{6,5},{7,4},{8,11},{9,10},{10,... | collective-permute-start | bytes 393224 | tf_op jit(solution)/shard_map/ppermute | solution.py:43
  99.1 1.9 %collective-permute-start.5 = (f16[256,256]{1,0:T(8,128)(2,1)S(1)}, f16[256,256]{1,0:T(8,128)(2,1)S(1)}, u32[]{:S(2)}, u32[]{:S(2)}) collective-permute-start(f16[256,256]{1,0:T(8,128)(2,1)S(1)} %fusion.2), channel_id=1, source_target_pairs={{0,1},{1,0},{2,3},{3,2},{4,5},{5,4},{6,7},{7,6},{8,9},{9,8},{10,11... | collective-permute-start | bytes 393224 | tf_op jit(solution)/shard_map/ppermute | solution.py:43
  101.0 3.1 %collective-permute-done.7 = f16[256,256]{1,0:T(8,128)(2,1)S(1)} collective-permute-done((f16[256,256]{1,0:T(8,128)(2,1)S(1)}, f16[256,256]{1,0:T(8,128)(2,1)S(1)}, u32[]{:S(2)}, u32[]{:S(2)}) %collective-permute-start.7) | collective-permute-done | bytes 131104 | tf_op jit(solution)/shard_map/ppermute | solution.py:43
  104.1 0.1 fusion.1
  104.2 3.3 %collective-permute-start.8 = (f16[256,256]{1,0:T(8,128)(2,1)S(1)}, f16[256,256]{1,0:T(8,128)(2,1)S(1)}, u32[]{:S(2)}, u32[]{:S(2)}) collective-permute-start(f16[256,256]{1,0:T(8,128)(2,1)S(1)} %fusion.1), channel_id=1, source_target_pairs={{0,388},{1,389},{2,390},{3,391},{4,384},{5,385},{6,386},{7,387},{8... | collective-permute-start | bytes 393224 | tf_op jit(solution)/shard_map/ppermute | solution.py:38
  107.4 0.0 collective-permute-done.5
  107.5 6.6 %collective-permute-done.8 = f16[256,256]{1,0:T(8,128)(2,1)S(1)} collective-permute-done((f16[256,256]{1,0:T(8,128)(2,1)S(1)}, f16[256,256]{1,0:T(8,128)(2,1)S(1)}, u32[]{:S(2)}, u32[]{:S(2)}) %collective-permute-start.8) | collective-permute-done | bytes 131104 | tf_op jit(solution)/shard_map/ppermute | solution.py:38
  114.1 0.9 finish.1
  115.0 0.0 all-to-all-done.2
  115.1 0.1 convert_element_type.77
  115.2 0.3 fusion.6
  115.5 0.8 fusion
  (33 shorter events, 0.3 us)
Async XLA Ops:
  0.6 19.4 %copy-start.2 = (bf16[256,256]{1,0:T(8,128)(2,1)S(1)}, bf16[256,256]{1,0:T(8,128)(2,1)}, u32[]{:S(2)}) copy-start(bf16[256,256]{1,0:T(8,128)(2,1)} %own_ref.3) | copy-start | bytes 393220
  0.6 24.1 %copy-start.3 = (bf16[256,256]{1,0:T(8,128)(2,1)S(1)}, bf16[256,256]{1,0:T(8,128)(2,1)}, u32[]{:S(2)}) copy-start(bf16[256,256]{1,0:T(8,128)(2,1)} %pos_ref.3) | copy-start | bytes 393220
  0.7 24.1 %copy-start.9 = (s32[65536]{0:T(1024)S(1)}, s32[65536]{0:T(1024)}, u32[]{:S(2)}) copy-start(s32[65536]{0:T(1024)} %param.11) | copy-start | bytes 786436
  0.7 24.1 %copy-start.12 = (s32[2048]{0:T(1024)S(1)}, s32[2048]{0:T(1024)}, u32[]{:S(2)}) copy-start(s32[2048]{0:T(1024)} %param.10) | copy-start | bytes 24580
  0.7 24.1 %copy-start.13 = (s32[256]{0:T(256)S(1)}, s32[256]{0:T(256)}, u32[]{:S(2)}) copy-start(s32[256]{0:T(256)} %param.9) | copy-start | bytes 3076
  0.7 24.1 %copy-start.8 = (bf16[2048,256]{1,0:T(8,128)(2,1)S(1)}, bf16[2048,256]{1,0:T(8,128)(2,1)}, u32[]{:S(2)}) copy-start(bf16[2048,256]{1,0:T(8,128)(2,1)} %negatives_ref.1) | copy-start | bytes 3145732
  0.7 10.9 %collective-permute-start.2 = (bf16[256,256]{1,0:T(8,128)(2,1)}, bf16[256,256]{1,0:T(8,128)(2,1)S(1)}, u32[]{:S(2)}, u32[]{:S(2)}) collective-permute-start(bf16[256,256]{1,0:T(8,128)(2,1)} %own_ref.3), channel_id=1, source_target_pairs={{0,388},{1,389},{2,390},{3,391},{4,384},{5,385},{6,386},{7,387},{8... | collective-permute-start | bytes 393224 | tf_op jit(solution)/shard_map/ppermute | solution.py:38
  6.9 8.3 %collective-permute-start = (bf16[256,256]{1,0:T(8,128)(2,1)}, bf16[256,256]{1,0:T(8,128)(2,1)S(1)}, u32[]{:S(2)}, u32[]{:S(2)}) collective-permute-start(bf16[256,256]{1,0:T(8,128)(2,1)} %own_ref.3), channel_id=1, source_target_pairs={{0,3},{1,2},{2,1},{3,0},{4,7},{5,6},{6,5},{7,4},{8,11},{9,10},{10,... | collective-permute-start | bytes 393224 | tf_op jit(solution)/shard_map/ppermute | solution.py:43
  16.0 19.4 %all-to-all-start = ((bf16[4,256,256]{2,1,0:T(8,128)(2,1)}), bf16[4,256,256]{2,1,0:T(8,128)(2,1)S(1)}, u32[]{:S(2)}, u32[]{:S(2)}) async-start(bf16[4,256,256]{2,1,0:T(8,128)(2,1)} %spread.1), calls=%async_computation | async-start | bytes 1048576 | tf_op jit(solution)/shard_map/all_to_all | solution.py:257
  20.8 11.5 %collective-permute-start.1 = (bf16[2,256,256]{2,1,0:T(8,128)(2,1)}, bf16[2,256,256]{2,1,0:T(8,128)(2,1)S(1)}, u32[]{:S(2)}, u32[]{:S(2)}) collective-permute-start(bf16[2,256,256]{2,1,0:T(8,128)(2,1)} %pad_maximum_fusion), channel_id=1, source_target_pairs={{0,1},{1,0},{2,3},{3,2},{4,5},{5,4},{6,7},{7,6},{8,9},{9,8},{10,11... | collective-permute-start | bytes 786440 | tf_op jit(solution)/shard_map/ppermute | solution.py:43
  26.6 5.7 %copy-start.6 = (f32[1,256]{1,0:T(1,128)}, f32[1,256]{1,0:T(1,128)S(1)}, u32[]{:S(2)}) copy-start(f32[1,256]{1,0:T(1,128)S(1)} %get-tuple-element.17.score_ref) | copy-start | bytes 3076
  32.2 2.5 %copy-start.10 = (bf16[2,256,256]{2,1,0:T(8,128)(2,1)}, bf16[2,256,256]{2,1,0:T(8,128)(2,1)S(1)}, u32[]{:S(2)}) copy-start(bf16[2,256,256]{2,1,0:T(8,128)(2,1)S(1)} %collective-permute-done.1.second_ref) | copy-start | bytes 786436
  34.8 0.6 copy-start.14
  35.4 0.7 copy-start.15
  48.2 8.6 %collective-permute-start.3 = (f32[8,256]{1,0:T(8,128)S(1)}, f32[8,256]{1,0:T(8,128)S(1)}, u32[]{:S(2)}, u32[]{:S(2)}) collective-permute-start(f32[8,256]{1,0:T(8,128)S(1)} %join.1.joined_ref), channel_id=1, source_target_pairs={{0,388},{1,389},{2,390},{3,391},{4,384},{5,385},{6,386},{7,387},{8... | collective-permute-start | bytes 24584 | tf_op jit(solution)/shard_map/ppermute | solution.py:38
  56.7 1.0 copy-start.11
  57.7 0.7 copy-start.16
  65.7 16.4 %copy-start = (f32[2,256,256]{2,1,0:T(8,128)}, f32[2,256,256]{2,1,0:T(8,128)S(1)}, u32[]{:S(2)}) copy-start(f32[2,256,256]{2,1,0:T(8,128)S(1)} %get-tuple-element.20) | copy-start | bytes 1572868
  65.7 16.4 %copy-start.4 = (f32[8,256]{1,0:T(8,128)}, f32[8,256]{1,0:T(8,128)S(1)}, u32[]{:S(2)}) copy-start(f32[8,256]{1,0:T(8,128)S(1)} %get-tuple-element.22.lse_ref) | copy-start | bytes 24580
  65.7 16.0 %collective-permute-start.9 = (f32[1024,256]{1,0:T(8,128)S(1)}, f32[1024,256]{1,0:T(8,128)S(1)}, u32[]{:S(2)}, u32[]{:S(2)}) collective-permute-start(f32[1024,256]{1,0:T(8,128)S(1)} %get-tuple-element.26), channel_id=1, source_target_pairs={{0,8},{8,0},{16,24},{24,16},{32,40},{40,32},{48,56},{56,48},{64,72... | collective-permute-start | bytes 3145736 | tf_op jit(solution)/shard_map/ppermute | solution.py:48
  67.7 10.6 %collective-permute-start.6 = (f16[2,256,256]{2,1,0:T(8,128)(2,1)S(1)}, f16[2,256,256]{2,1,0:T(8,128)(2,1)S(1)}, u32[]{:S(2)}, u32[]{:S(2)}) collective-permute-start(f16[2,256,256]{2,1,0:T(8,128)(2,1)S(1)} %convert_element_type.66), channel_id=1, source_target_pairs={{0,1},{1,0},{2,3},{3,2},{4,5},{5,4},{6,7},{7,6},{8,9},{9,8},{10,11... | collective-permute-start | bytes 786440 | tf_op jit(solution)/shard_map/ppermute | solution.py:43
  70.2 11.5 %collective-permute-start.4 = (f16[2,256,256]{2,1,0:T(8,128)(2,1)S(1)}, f16[2,256,256]{2,1,0:T(8,128)(2,1)S(1)}, u32[]{:S(2)}, u32[]{:S(2)}) collective-permute-start(f16[2,256,256]{2,1,0:T(8,128)(2,1)S(1)} %convert_element_type.60), channel_id=1, source_target_pairs={{0,3},{1,2},{2,1},{3,0},{4,7},{5,6},{6,5},{7,4},{8,11},{9,10},{10,... | collective-permute-start | bytes 786440 | tf_op jit(solution)/shard_map/ppermute | solution.py:43
  83.1 12.9 %copy-start.1 = (f32[2,256,256]{2,1,0:T(8,128)S(1)}, f32[2,256,256]{2,1,0:T(8,128)}, u32[]{:S(2)}) copy-start(f32[2,256,256]{2,1,0:T(8,128)} %copy-done) | copy-start | bytes 1572868
  83.1 32.0 %all-to-all-start.2 = ((f16[32,40,256]{2,1,0:T(8,128)(2,1)}), f16[32,40,256]{2,1,0:T(8,128)(2,1)S(1)}, u32[]{:S(2)}, u32[]{:S(2)}) async-start(f16[32,40,256]{2,1,0:T(8,128)(2,1)} %convert_element_type.76), calls=%async_computation.2 | async-start | bytes 1310720 | tf_op jit(solution)/shard_map/all_to_all | solution.py:257
  96.0 18.1 %copy-start.5 = (f32[8,256]{1,0:T(8,128)S(1)}, f32[8,256]{1,0:T(8,128)}, u32[]{:S(2)}) copy-start(f32[8,256]{1,0:T(8,128)} %copy-done.4) | copy-start | bytes 24580
  96.0 18.1 %copy-start.7 = (f32[1,256]{1,0:T(1,128)S(1)}, f32[1,256]{1,0:T(1,128)}, u32[]{:S(2)}) copy-start(f32[1,256]{1,0:T(1,128)} %copy-done.6) | copy-start | bytes 3076
  96.0 8.1 %collective-permute-start.7 = (f16[256,256]{1,0:T(8,128)(2,1)S(1)}, f16[256,256]{1,0:T(8,128)(2,1)S(1)}, u32[]{:S(2)}, u32[]{:S(2)}) collective-permute-start(f16[256,256]{1,0:T(8,128)(2,1)S(1)} %fusion.3), channel_id=1, source_target_pairs={{0,3},{1,2},{2,1},{3,0},{4,7},{5,6},{6,5},{7,4},{8,11},{9,10},{10,... | collective-permute-start | bytes 393224 | tf_op jit(solution)/shard_map/ppermute | solution.py:43
  99.1 8.4 %collective-permute-start.5 = (f16[256,256]{1,0:T(8,128)(2,1)S(1)}, f16[256,256]{1,0:T(8,128)(2,1)S(1)}, u32[]{:S(2)}, u32[]{:S(2)}) collective-permute-start(f16[256,256]{1,0:T(8,128)(2,1)S(1)} %fusion.2), channel_id=1, source_target_pairs={{0,1},{1,0},{2,3},{3,2},{4,5},{5,4},{6,7},{7,6},{8,9},{9,8},{10,11... | collective-permute-start | bytes 393224 | tf_op jit(solution)/shard_map/ppermute | solution.py:43
  104.2 9.9 %collective-permute-start.8 = (f16[256,256]{1,0:T(8,128)(2,1)S(1)}, f16[256,256]{1,0:T(8,128)(2,1)S(1)}, u32[]{:S(2)}, u32[]{:S(2)}) collective-permute-start(f16[256,256]{1,0:T(8,128)(2,1)S(1)} %fusion.1), channel_id=1, source_target_pairs={{0,388},{1,389},{2,390},{3,391},{4,384},{5,385},{6,386},{7,387},{8... | collective-permute-start | bytes 393224 | tf_op jit(solution)/shard_map/ppermute | solution.py:38

commit v5 on v3

--- a/solution.py
+++ b/solution.py
@@ -210,7 +210,15 @@
         out_ref[k, 1] = far_ref[...]
 
 
-def sum_cores_kernel(keep_ref, got_ref, arrived_ref, out_ref):
+def halve_kernel(near_keep_ref, near_got_ref, far_keep_ref, far_got_ref, mine_ref, onward_ref):
+    for side, (keep, got) in enumerate(
+        ((near_keep_ref, near_got_ref), (far_keep_ref, far_got_ref))
+    ):
+        mine_ref[side] = keep[0] + got[0]
+        onward_ref[side] = keep[1] + got[1]
+
+
+def sum_cores_kernel(keep_ref, got_ref, out_ref):
     total = keep_ref[...] + got_ref[...]
     top = jnp.max(jnp.max(jnp.abs(total), axis=0, keepdims=True), axis=1, keepdims=True)
     power = jnp.clip(jnp.floor(jnp.log2(jnp.maximum(top, 1e-30))), -99.0, 99.0)
@@ -339,29 +347,32 @@
     )(spot, blocks, joined, other, ordered, turned, corr)
     from_core = other_core(send)
 
-    def halve(side, keep, got):
-        sent = (keep[1] + got[1].astype(f32)).astype(f16)
-        sent = swap_near(sent, HALVING[side][1])
-        return keep[0] + got[0].astype(f32) + sent.astype(f32)
-
-    far_got = swap_near(far_send.astype(f16), HALVING[1][0])
-    near_got = swap_near(near_send.astype(f16), HALVING[0][0])
-    arrived = near_got[0, :8, :LANES].astype(f32) + far_got[0, :8, :LANES].astype(f32)
-    far_acc = halve(1, far_keep, far_got)
-    near_acc = halve(0, near_keep, near_got)
+    far_got = swap_near(far_send.astype(f16), HALVING[1][0]).astype(f32)
+    near_got = swap_near(near_send.astype(f16), HALVING[0][0]).astype(f32)
+    mine, onward = pl.pallas_call(
+        halve_kernel,
+        in_specs=[vmem] * 4,
+        out_specs=(vmem,) * 2,
+        out_shape=(like((FAR, width, own), f32),) * 2,
+        compiler_params=params(),
+        cost_estimate=cost(10**6, 2 * 10**8, 0),
+        name="halve",
+    )(near_keep, near_got, far_keep, far_got)
+    far_acc = mine[1] + swap_near(onward[1].astype(f16), HALVING[1][1]).astype(f32)
+    near_acc = mine[0] + swap_near(onward[0].astype(f16), HALVING[0][1]).astype(f32)
     query_far = mirror(far_acc.astype(f16)).astype(f32)
 
     count = LINE * RING
     block = shard // CORES // count
     neg_acc = pl.pallas_call(
         sum_cores_kernel,
-        in_specs=[vmem] * 3,
+        in_specs=[vmem] * 2,
         out_specs=vmem,
         out_shape=like((count, block + 8, width), f32),
         compiler_params=params(),
         cost_estimate=cost(10**6, 10**6, 0),
         name="sum_cores",
-    )(keep, from_core, arrived)
+    )(keep, from_core)
     neg_acc = trade(neg_acc.astype(f16), "dp", sheets).astype(f32)
     power = jnp.exp2(neg_acc[:, block : block + 1, :1] - 13.0)
     neg_grad = jnp.sum(neg_acc[:, :block, :] * power, axis=0)

time: 113 us -> 116 us (1.027)
  waiting for transfers between devices: 33.5 us -> 36.6 us
    ppermute x1, waiting for transfers between devices: 0.01 us -> 2.63 us  [other_core(): return lax.ppermute(value, 'dp', perm)]
  transfers between devices with their start and end apart: 10 -> 10, of which waited for: 7 -> 9; matrix products, arithmetic and copies ran while one was open for 1% -> 1% of each run, Pallas kernels for 2% -> 2%
where the time goes in v5:
time: 116 us
  starting transfers between devices  48.2 us (42%)
  waiting for transfers between devices  36.6 us (32%)
  Pallas kernels  17 us (15%)
  blocking collectives  7.8 us (7%)
  local copies, waits for them, and re-layouts  2.87 us (2%)
  other arithmetic  2.4 us (2%)
    all_to_all x2, starting transfers between devices, trade(): lax.all_to_all(value, axis, 0, 0, tiled=True, axis_index_groups=groups)  18 us
    ppermute x3, starting transfers between devices, mirror(): return lax.ppermute(value, ('dp', 'neg'), perm)  17.8 us
    ppermute x4, waiting for transfers between devices, swap_near(): return lax.ppermute(value, 'neg', perm)  12.5 us
    all_to_all x2, waiting for transfers between devices, trade(): lax.all_to_all(value, axis, 0, 0, tiled=True, axis_index_groups=groups)  11.1 us
    ppermute x4, starting transfers between devices, swap_near(): return lax.ppermute(value, 'neg', perm)  10.5 us
    ppermute x3, waiting for transfers between devices, mirror(): return lax.ppermute(value, ('dp', 'neg'), perm)  10.3 us
    all_to_all x1, blocking collectives, trade(): lax.all_to_all(value, axis, 0, 0, tiled=True, axis_index_groups=groups)  7.8 us
    pallas_call x1, Pallas kernels, per_device(): pl.pallas_call(grads_kernel, in_specs=[smem, hbm] + [vmem] * 5, out_specs...  7.41 us
  transfers between devices with their start and end apart: 10, of which 9 were waited for; matrix products, arithmetic and copies ran while one was open for 1% of the time, Pallas kernels for 2%

profile of v5, /device:TPU:8, one launch (start us, length us, event | category | flops | bytes accessed | tf_op | source)
XLA Modules:
  0.0 115.9 jit_solution(4856080953718445960)
XLA Ops:
  0.6 6.1 %collective-permute-start = (bf16[256,256]{1,0:T(8,128)(2,1)}, bf16[256,256]{1,0:T(8,128)(2,1)S(1)}, u32[]{:S(2)}, u32[]{:S(2)}) collective-permute-start(bf16[256,256]{1,0:T(8,128)(2,1)} %queries_ref.1), channel_id=1, source_target_pairs={{0,388},{1,389},{2,390},{3,391},{4,384},{5,385},{6,386},{7,387},{8... | collective-permute-start | bytes 393224 | tf_op jit(solution)/shard_map/ppermute | solution.py:38
  6.7 4.3 %collective-permute-done.far_ref = bf16[256,256]{1,0:T(8,128)(2,1)S(1)} collective-permute-done((bf16[256,256]{1,0:T(8,128)(2,1)}, bf16[256,256]{1,0:T(8,128)(2,1)S(1)}, u32[]{:S(2)}, u32[]{:S(2)}) %collective-permute-start) | collective-permute-done | bytes 131104 | tf_op jit(solution)/shard_map/ppermute | solution.py:38
  11.0 0.9 copy-done.8
  11.9 1.1 spread.1
  13.0 0.0 copy-start.14
  13.0 4.5 %all-to-all-start = ((bf16[4,2,256,256]{3,2,1,0:T(8,128)(2,1)}), bf16[4,2,256,256]{3,2,1,0:T(8,128)(2,1)S(1)}, u32[]{:S(2)}, u32[]{:S(2)}) async-start(bf16[4,2,256,256]{3,2,1,0:T(8,128)(2,1)} %spread.1), calls=%async_computation | async-start | bytes 2097152 | tf_op jit(solution)/shard_map/all_to_all | solution.py:250
  17.5 0.0 copy-done.9
  17.5 0.0 copy-done.10
  17.5 0.0 copy-done.12
  17.5 0.0 copy-done.13
  17.6 0.0 copy-start.11
  17.6 1.2 %copy-done.11 = bf16[2048,256]{1,0:T(8,128)(2,1)S(1)} copy-done((bf16[2048,256]{1,0:T(8,128)(2,1)S(1)}, bf16[2048,256]{1,0:T(8,128)(2,1)}, u32[]{:S(2)}) %copy-start.11) | copy-done | bytes 1048600
  18.8 1.8 %lookup.1 = (f32[16,128]{1,0:T(8,128)S(1)}, f32[1,256]{1,0:T(1,128)S(1)}, bf16[2048,256]{1,0:T(8,128)(2,1)S(1)}) custom-call(s32[1]{0:T(128)} %bitcast.1.place_ref, s32[512,128]{1,0:T(8,128)S(1)} %bitcast.18, s32[16,128]{1,0:T(8,128)S(1)} %bitcast.19, s32[2,128]{1,0:T(2,128)S(1)} %bitcast.20, bf16[256,256]{1,0:T(8,128)(2,1)S(1)} %copy-done.9, ...), custom_call_target="tpu_custom_call" | custom-call | flops 1000000000 | bytes 2000000 | tf_op jit(solution)/shard_map/lookup/pallas_call | solution.py:269
  20.6 11.1 %all-to-all-done.blocks_hbm = bf16[4,2,256,256]{3,2,1,0:T(8,128)(2,1)S(1)} async-done(((bf16[4,2,256,256]{3,2,1,0:T(8,128)(2,1)}), bf16[4,2,256,256]{3,2,1,0:T(8,128)(2,1)S(1)}, u32[]{:S(2)}, u32[]{:S(2)}) %all-to-all-start) | async-done | bytes 1048608 | tf_op jit(solution)/shard_map/all_to_all | solution.py:250
  31.7 5.3 %stats.1 = f32[4,8,256]{2,1,0:T(8,128)S(1)} custom-call(s32[1]{0:T(128)} %bitcast.spot_ref, bf16[4,2,256,256]{3,2,1,0:T(8,128)(2,1)S(1)} %all-to-all-done.blocks_hbm, bf16[2048,256]{1,0:T(8,128)(2,1)S(1)} %get-tuple-element.17.negatives_ref, f32[16,128]{1,0:T(8,128)S(1)} %get-tuple-element.18.rows_ref, f32[1,256]{1,0:T(1,128)S(1)} %get-tuple-element.19.score_ref), custom_call_target="tpu_custom_call" | custom-call | flops 2147483648 | bytes 4000000 | tf_op jit(solution)/shard_map/stats/pallas_call | solution.py:309
  37.1 7.8 %all_to_all.15.parts_ref = f32[4,8,256]{2,1,0:T(8,128)S(1)} all-to-all(f32[4,8,256]{2,1,0:T(8,128)S(1)} %stats.1), channel_id=1, replica_groups={{0,1,2,3},{4,5,6,7},{8,9,10,11},{12,13,14,15},{16,17,18,19},{20,21,22,2..., dimensions={0} | all-to-all | bytes 65536 | tf_op jit(solution)/shard_map/all_to_all | solution.py:250
  44.9 6.2 %collective-permute-start.1 = (f32[8,256]{1,0:T(8,128)S(1)}, f32[8,256]{1,0:T(8,128)S(1)}, u32[]{:S(2)}, u32[]{:S(2)}) collective-permute-start(f32[8,256]{1,0:T(8,128)S(1)} %join.1.joined_ref), channel_id=1, source_target_pairs={{0,388},{1,389},{2,390},{3,391},{4,384},{5,385},{6,386},{7,387},{8... | collective-permute-start | bytes 24584 | tf_op jit(solution)/shard_map/ppermute | solution.py:38
  51.1 0.6 copy.10
  51.8 1.7 %collective-permute-done.1.other_ref = f32[8,256]{1,0:T(8,128)S(1)} collective-permute-done((f32[8,256]{1,0:T(8,128)S(1)}, f32[8,256]{1,0:T(8,128)S(1)}, u32[]{:S(2)}, u32[]{:S(2)}) %collective-permute-start.1) | collective-permute-done | bytes 8224 | tf_op jit(solution)/shard_map/ppermute | solution.py:38
  53.4 7.4 %grads.1 = (f32[2,256,256]{2,1,0:T(8,128)S(1)}, f32[2,256,256]{2,1,0:T(8,128)S(1)}, f32[2,256,256]{2,1,0:T(8,128)S(1)}, f32[2,256,256]{2,1,0:T(8,128)S(1)}, f32[...) custom-call(s32[1]{0:T(128)} %bitcast.spot_ref, ...), custom_call_target="tpu_custom_call" | custom-call | flops 6442450944 | bytes 8000000 | tf_op jit(solution)/shard_map/grads/pallas_call | solution.py:329
  60.9 0.0 copy-start
  60.9 0.0 copy-start.2
  60.9 0.0 copy-start.4
  60.9 0.0 copy-start.6
  60.9 1.9 %collective-permute-start.7 = (f32[1024,256]{1,0:T(8,128)S(1)}, f32[1024,256]{1,0:T(8,128)S(1)}, u32[]{:S(2)}, u32[]{:S(2)}) collective-permute-start(f32[1024,256]{1,0:T(8,128)S(1)} %get-tuple-element.30), channel_id=1, source_target_pairs={{0,8},{8,0},{16,24},{24,16},{32,40},{40,32},{48,56},{56,48},{64,72... | collective-permute-start | bytes 3145736 | tf_op jit(solution)/shard_map/ppermute | solution.py:48
  62.8 2.6 %collective-permute-done.7.got_ref = f32[1024,256]{1,0:T(8,128)S(1)} collective-permute-done((f32[1024,256]{1,0:T(8,128)S(1)}, f32[1024,256]{1,0:T(8,128)S(1)}, u32[]{:S(2)}, u32[]{:S(2)}) %collective-permute-start.7) | collective-permute-done | bytes 1048608 | tf_op jit(solution)/shard_map/ppermute | solution.py:48
  65.5 0.3 sum_cores.1
  65.8 1.0 convert_element_type.48
  66.8 13.5 %all-to-all-start.2 = ((f16[32,40,256]{2,1,0:T(8,128)(2,1)}), f16[32,40,256]{2,1,0:T(8,128)(2,1)S(1)}, u32[]{:S(2)}, u32[]{:S(2)}) async-start(f16[32,40,256]{2,1,0:T(8,128)(2,1)} %convert_element_type.48), calls=%async_computation.2 | async-start | bytes 1310720 | tf_op jit(solution)/shard_map/all_to_all | solution.py:250
  80.2 0.0 copy-done.3
  80.3 2.6 %collective-permute-start.3 = (f16[2,256,256]{2,1,0:T(8,128)(2,1)S(1)}, f16[2,256,256]{2,1,0:T(8,128)(2,1)S(1)}, u32[]{:S(2)}, u32[]{:S(2)}) collective-permute-start(f16[2,256,256]{2,1,0:T(8,128)(2,1)S(1)} %convert_element_type.40), channel_id=1, source_target_pairs={{0,1},{1,0},{2,3},{3,2},{4,5},{5,4},{6,7},{7,6},{8,9},{9,8},{10,11... | collective-permute-start | bytes 786440 | tf_op jit(solution)/shard_map/ppermute | solution.py:43
  83.0 3.0 %collective-permute-start.2 = (f16[2,256,256]{2,1,0:T(8,128)(2,1)S(1)}, f16[2,256,256]{2,1,0:T(8,128)(2,1)S(1)}, u32[]{:S(2)}, u32[]{:S(2)}) collective-permute-start(f16[2,256,256]{2,1,0:T(8,128)(2,1)S(1)} %convert_element_type.38), channel_id=1, source_target_pairs={{0,3},{1,2},{2,1},{3,0},{4,7},{5,6},{6,5},{7,4},{8,11},{9,10},{10,... | collective-permute-start | bytes 786440 | tf_op jit(solution)/shard_map/ppermute | solution.py:43
  86.0 4.1 %collective-permute-done.3 = f16[2,256,256]{2,1,0:T(8,128)(2,1)S(1)} collective-permute-done((f16[2,256,256]{2,1,0:T(8,128)(2,1)S(1)}, f16[2,256,256]{2,1,0:T(8,128)(2,1)S(1)}, u32[]{:S(2)}, u32[]{:S(2)}) %collective-permute-start.3) | collective-permute-done | bytes 262176 | tf_op jit(solution)/shard_map/ppermute | solution.py:43
  90.2 3.4 %collective-permute-done.2 = f16[2,256,256]{2,1,0:T(8,128)(2,1)S(1)} collective-permute-done((f16[2,256,256]{2,1,0:T(8,128)(2,1)S(1)}, f16[2,256,256]{2,1,0:T(8,128)(2,1)S(1)}, u32[]{:S(2)}, u32[]{:S(2)}) %collective-permute-start.2) | collective-permute-done | bytes 262176 | tf_op jit(solution)/shard_map/ppermute | solution.py:43
  93.7 0.1 halve.1
  93.8 0.1 slice_bitcast_fusion
  93.9 3.0 %collective-permute-start.5 = (f16[256,256]{1,0:T(8,128)(2,1)S(1)}, f16[256,256]{1,0:T(8,128)(2,1)S(1)}, u32[]{:S(2)}, u32[]{:S(2)}) collective-permute-start(f16[256,256]{1,0:T(8,128)(2,1)S(1)} %get-tuple-element.33), channel_id=1, source_target_pairs={{0,3},{1,2},{2,1},{3,0},{4,7},{5,6},{6,5},{7,4},{8,11},{9,10},{10,... | collective-permute-start | bytes 393224 | tf_op jit(solution)/shard_map/ppermute | solution.py:43
  96.9 1.9 %collective-permute-start.4 = (f16[256,256]{1,0:T(8,128)(2,1)S(1)}, f16[256,256]{1,0:T(8,128)(2,1)S(1)}, u32[]{:S(2)}, u32[]{:S(2)}) collective-permute-start(f16[256,256]{1,0:T(8,128)(2,1)S(1)} %get-tuple-element.34), channel_id=1, source_target_pairs={{0,1},{1,0},{2,3},{3,2},{4,5},{5,4},{6,7},{7,6},{8,9},{9,8},{10,11... | collective-permute-start | bytes 393224 | tf_op jit(solution)/shard_map/ppermute | solution.py:43
  98.8 3.1 %collective-permute-done.5 = f16[256,256]{1,0:T(8,128)(2,1)S(1)} collective-permute-done((f16[256,256]{1,0:T(8,128)(2,1)S(1)}, f16[256,256]{1,0:T(8,128)(2,1)S(1)}, u32[]{:S(2)}, u32[]{:S(2)}) %collective-permute-start.5) | collective-permute-done | bytes 131104 | tf_op jit(solution)/shard_map/ppermute | solution.py:43
  102.0 1.8 %collective-permute-done.4 = f16[256,256]{1,0:T(8,128)(2,1)S(1)} collective-permute-done((f16[256,256]{1,0:T(8,128)(2,1)S(1)}, f16[256,256]{1,0:T(8,128)(2,1)S(1)}, u32[]{:S(2)}, u32[]{:S(2)}) %collective-permute-start.4) | collective-permute-done | bytes 131104 | tf_op jit(solution)/shard_map/ppermute | solution.py:43
  103.8 0.1 fusion.1
  103.8 5.5 %collective-permute-start.6 = (f16[256,256]{1,0:T(8,128)(2,1)S(1)}, f16[256,256]{1,0:T(8,128)(2,1)S(1)}, u32[]{:S(2)}, u32[]{:S(2)}) collective-permute-start(f16[256,256]{1,0:T(8,128)(2,1)S(1)} %get-tuple-element.31), channel_id=1, source_target_pairs={{0,388},{1,389},{2,390},{3,391},{4,384},{5,385},{6,386},{7,387},{8... | collective-permute-start | bytes 393224 | tf_op jit(solution)/shard_map/ppermute | solution.py:38
  109.4 4.4 %collective-permute-done.6 = f16[256,256]{1,0:T(8,128)(2,1)S(1)} collective-permute-done((f16[256,256]{1,0:T(8,128)(2,1)S(1)}, f16[256,256]{1,0:T(8,128)(2,1)S(1)}, u32[]{:S(2)}, u32[]{:S(2)}) %collective-permute-start.6) | collective-permute-done | bytes 131104 | tf_op jit(solution)/shard_map/ppermute | solution.py:38
  113.8 0.9 finish.1
  114.7 0.0 all-to-all-done.2
  114.7 0.1 convert_element_type.49
  114.8 0.3 fusion.4
  115.1 0.8 fusion
  (24 shorter events, 0.3 us)
Async XLA Ops:
  0.6 10.4 %collective-permute-start = (bf16[256,256]{1,0:T(8,128)(2,1)}, bf16[256,256]{1,0:T(8,128)(2,1)S(1)}, u32[]{:S(2)}, u32[]{:S(2)}) collective-permute-start(bf16[256,256]{1,0:T(8,128)(2,1)} %queries_ref.1), channel_id=1, source_target_pairs={{0,388},{1,389},{2,390},{3,391},{4,384},{5,385},{6,386},{7,387},{8... | collective-permute-start | bytes 393224 | tf_op jit(solution)/shard_map/ppermute | solution.py:38
  11.0 0.9 copy-start.8
  13.0 4.5 %copy-start.9 = (bf16[256,256]{1,0:T(8,128)(2,1)S(1)}, bf16[256,256]{1,0:T(8,128)(2,1)}, u32[]{:S(2)}) copy-start(bf16[256,256]{1,0:T(8,128)(2,1)} %queries_ref.1) | copy-start | bytes 393220
  13.0 4.5 %copy-start.10 = (bf16[256,256]{1,0:T(8,128)(2,1)S(1)}, bf16[256,256]{1,0:T(8,128)(2,1)}, u32[]{:S(2)}) copy-start(bf16[256,256]{1,0:T(8,128)(2,1)} %pos_ref.3) | copy-start | bytes 393220
  13.0 4.6 %copy-start.12 = (s32[65536]{0:T(1024)S(1)}, s32[65536]{0:T(1024)}, u32[]{:S(2)}) copy-start(s32[65536]{0:T(1024)} %param.11) | copy-start | bytes 786436
  13.0 4.6 %copy-start.13 = (s32[2048]{0:T(1024)S(1)}, s32[2048]{0:T(1024)}, u32[]{:S(2)}) copy-start(s32[2048]{0:T(1024)} %param.10) | copy-start | bytes 24580
  13.0 4.6 %copy-start.14 = (s32[256]{0:T(256)S(1)}, s32[256]{0:T(256)}, u32[]{:S(2)}) copy-start(s32[256]{0:T(256)} %param.9) | copy-start | bytes 3076
  13.0 18.7 %all-to-all-start = ((bf16[4,2,256,256]{3,2,1,0:T(8,128)(2,1)}), bf16[4,2,256,256]{3,2,1,0:T(8,128)(2,1)S(1)}, u32[]{:S(2)}, u32[]{:S(2)}) async-start(bf16[4,2,256,256]{3,2,1,0:T(8,128)(2,1)} %spread.1), calls=%async_computation | async-start | bytes 2097152 | tf_op jit(solution)/shard_map/all_to_all | solution.py:250
  17.6 1.2 %copy-start.11 = (bf16[2048,256]{1,0:T(8,128)(2,1)S(1)}, bf16[2048,256]{1,0:T(8,128)(2,1)}, u32[]{:S(2)}) copy-start(bf16[2048,256]{1,0:T(8,128)(2,1)} %negatives_ref.1) | copy-start | bytes 3145732
  44.9 8.6 %collective-permute-start.1 = (f32[8,256]{1,0:T(8,128)S(1)}, f32[8,256]{1,0:T(8,128)S(1)}, u32[]{:S(2)}, u32[]{:S(2)}) collective-permute-start(f32[8,256]{1,0:T(8,128)S(1)} %join.1.joined_ref), channel_id=1, source_target_pairs={{0,388},{1,389},{2,390},{3,391},{4,384},{5,385},{6,386},{7,387},{8... | collective-permute-start | bytes 24584 | tf_op jit(solution)/shard_map/ppermute | solution.py:38
  60.9 4.9 %copy-start = (f32[2,256,256]{2,1,0:T(8,128)}, f32[2,256,256]{2,1,0:T(8,128)S(1)}, u32[]{:S(2)}) copy-start(f32[2,256,256]{2,1,0:T(8,128)S(1)} %get-tuple-element.21) | copy-start | bytes 1572868
  60.9 4.9 %copy-start.2 = (f32[2,256,256]{2,1,0:T(8,128)}, f32[2,256,256]{2,1,0:T(8,128)S(1)}, u32[]{:S(2)}) copy-start(f32[2,256,256]{2,1,0:T(8,128)S(1)} %get-tuple-element.23) | copy-start | bytes 1572868
  60.9 4.9 %copy-start.4 = (f32[2,256,256]{2,1,0:T(8,128)}, f32[2,256,256]{2,1,0:T(8,128)S(1)}, u32[]{:S(2)}) copy-start(f32[2,256,256]{2,1,0:T(8,128)S(1)} %get-tuple-element.20.near_keep_ref) | copy-start | bytes 1572868
  60.9 4.9 %copy-start.6 = (f32[2,256,256]{2,1,0:T(8,128)}, f32[2,256,256]{2,1,0:T(8,128)S(1)}, u32[]{:S(2)}) copy-start(f32[2,256,256]{2,1,0:T(8,128)S(1)} %get-tuple-element.22.far_keep_ref) | copy-start | bytes 1572868
  60.9 4.6 %collective-permute-start.7 = (f32[1024,256]{1,0:T(8,128)S(1)}, f32[1024,256]{1,0:T(8,128)S(1)}, u32[]{:S(2)}, u32[]{:S(2)}) collective-permute-start(f32[1024,256]{1,0:T(8,128)S(1)} %get-tuple-element.30), channel_id=1, source_target_pairs={{0,8},{8,0},{16,24},{24,16},{32,40},{40,32},{48,56},{56,48},{64,72... | collective-permute-start | bytes 3145736 | tf_op jit(solution)/shard_map/ppermute | solution.py:48
  66.8 13.5 %copy-start.3 = (f32[2,256,256]{2,1,0:T(8,128)S(1)}, f32[2,256,256]{2,1,0:T(8,128)}, u32[]{:S(2)}) copy-start(f32[2,256,256]{2,1,0:T(8,128)} %copy-done.2) | copy-start | bytes 1572868
  66.8 16.2 %copy-start.1 = (f32[2,256,256]{2,1,0:T(8,128)S(1)}, f32[2,256,256]{2,1,0:T(8,128)}, u32[]{:S(2)}) copy-start(f32[2,256,256]{2,1,0:T(8,128)} %copy-done) | copy-start | bytes 1572868
  66.8 47.9 %all-to-all-start.2 = ((f16[32,40,256]{2,1,0:T(8,128)(2,1)}), f16[32,40,256]{2,1,0:T(8,128)(2,1)S(1)}, u32[]{:S(2)}, u32[]{:S(2)}) async-start(f16[32,40,256]{2,1,0:T(8,128)(2,1)} %convert_element_type.48), calls=%async_computation.2 | async-start | bytes 1310720 | tf_op jit(solution)/shard_map/all_to_all | solution.py:250
  80.3 13.3 %copy-start.5 = (f32[2,256,256]{2,1,0:T(8,128)S(1)}, f32[2,256,256]{2,1,0:T(8,128)}, u32[]{:S(2)}) copy-start(f32[2,256,256]{2,1,0:T(8,128)} %copy-done.4) | copy-start | bytes 1572868
  80.3 13.3 %copy-start.7 = (f32[2,256,256]{2,1,0:T(8,128)S(1)}, f32[2,256,256]{2,1,0:T(8,128)}, u32[]{:S(2)}) copy-start(f32[2,256,256]{2,1,0:T(8,128)} %copy-done.6) | copy-start | bytes 1572868
  80.3 9.8 %collective-permute-start.3 = (f16[2,256,256]{2,1,0:T(8,128)(2,1)S(1)}, f16[2,256,256]{2,1,0:T(8,128)(2,1)S(1)}, u32[]{:S(2)}, u32[]{:S(2)}) collective-permute-start(f16[2,256,256]{2,1,0:T(8,128)(2,1)S(1)} %convert_element_type.40), channel_id=1, source_target_pairs={{0,1},{1,0},{2,3},{3,2},{4,5},{5,4},{6,7},{7,6},{8,9},{9,8},{10,11... | collective-permute-start | bytes 786440 | tf_op jit(solution)/shard_map/ppermute | solution.py:43
  83.0 10.6 %collective-permute-start.2 = (f16[2,256,256]{2,1,0:T(8,128)(2,1)S(1)}, f16[2,256,256]{2,1,0:T(8,128)(2,1)S(1)}, u32[]{:S(2)}, u32[]{:S(2)}) collective-permute-start(f16[2,256,256]{2,1,0:T(8,128)(2,1)S(1)} %convert_element_type.38), channel_id=1, source_target_pairs={{0,3},{1,2},{2,1},{3,0},{4,7},{5,6},{6,5},{7,4},{8,11},{9,10},{10,... | collective-permute-start | bytes 786440 | tf_op jit(solution)/shard_map/ppermute | solution.py:43
  93.9 8.1 %collective-permute-start.5 = (f16[256,256]{1,0:T(8,128)(2,1)S(1)}, f16[256,256]{1,0:T(8,128)(2,1)S(1)}, u32[]{:S(2)}, u32[]{:S(2)}) collective-permute-start(f16[256,256]{1,0:T(8,128)(2,1)S(1)} %get-tuple-element.33), channel_id=1, source_target_pairs={{0,3},{1,2},{2,1},{3,0},{4,7},{5,6},{6,5},{7,4},{8,11},{9,10},{10,... | collective-permute-start | bytes 393224 | tf_op jit(solution)/shard_map/ppermute | solution.py:43
  96.9 6.9 %collective-permute-start.4 = (f16[256,256]{1,0:T(8,128)(2,1)S(1)}, f16[256,256]{1,0:T(8,128)(2,1)S(1)}, u32[]{:S(2)}, u32[]{:S(2)}) collective-permute-start(f16[256,256]{1,0:T(8,128)(2,1)S(1)} %get-tuple-element.34), channel_id=1, source_target_pairs={{0,1},{1,0},{2,3},{3,2},{4,5},{5,4},{6,7},{7,6},{8,9},{9,8},{10,11... | collective-permute-start | bytes 393224 | tf_op jit(solution)/shard_map/ppermute | solution.py:43
  103.8 9.9 %collective-permute-start.6 = (f16[256,256]{1,0:T(8,128)(2,1)S(1)}, f16[256,256]{1,0:T(8,128)(2,1)S(1)}, u32[]{:S(2)}, u32[]{:S(2)}) collective-permute-start(f16[256,256]{1,0:T(8,128)(2,1)S(1)} %get-tuple-element.31), channel_id=1, source_target_pairs={{0,388},{1,389},{2,390},{3,391},{4,384},{5,385},{6,386},{7,387},{8... | collective-permute-start | bytes 393224 | tf_op jit(solution)/shard_map/ppermute | solution.py:38

commit v6 on v3

--- a/solution.py
+++ b/solution.py
@@ -28,12 +28,12 @@
     return pl.CostEstimate(flops=flops, bytes_accessed=nbytes, transcendentals=exps)
 
 
-def mirror(value):
+def mirror(value, bits=0):
     perm = []
     for l in range(LINE):
         for g in range(RING * CORES):
             for n in range(FAR * NEAR):
-                to = ((LINE - 1 - l) * RING * CORES + g) * FAR * NEAR + (n + NEAR) % (FAR * NEAR)
+                to = ((LINE - 1 - l) * RING * CORES + g) * FAR * NEAR + (n ^ NEAR ^ bits)
                 perm.append(((l * RING * CORES + g) * FAR * NEAR + n, to))
     return lax.ppermute(value, ("dp", "neg"), perm)
 
@@ -224,7 +224,7 @@
 
 def finish_kernel(
     spot_ref, near_ref, far_ref, pos_ref, score_ref, lse_ref, joined_ref, other_ref,
-    grad_ref, loss_ref,
+    neg_grad_ref, grad_ref, loss_ref,
 ):
     spot = spot_ref[0]
     lse = lse_ref[pl.ds(spot, 1), :]
@@ -339,17 +339,14 @@
     )(spot, blocks, joined, other, ordered, turned, corr)
     from_core = other_core(send)
 
-    def halve(side, keep, got):
-        sent = (keep[1] + got[1].astype(f32)).astype(f16)
-        sent = swap_near(sent, HALVING[side][1])
-        return keep[0] + got[0].astype(f32) + sent.astype(f32)
-
     far_got = swap_near(far_send.astype(f16), HALVING[1][0])
     near_got = swap_near(near_send.astype(f16), HALVING[0][0])
     arrived = near_got[0, :8, :LANES].astype(f32) + far_got[0, :8, :LANES].astype(f32)
-    far_acc = halve(1, far_keep, far_got)
-    near_acc = halve(0, near_keep, near_got)
-    query_far = mirror(far_acc.astype(f16)).astype(f32)
+    far_sums = (far_keep + far_got.astype(f32)).astype(f16)
+    query_far = mirror(far_sums[0]).astype(f32) + mirror(far_sums[1], HALVING[1][1]).astype(f32)
+    onward = (near_keep[1] + near_got[1].astype(f32)).astype(f16)
+    near_acc = near_keep[0] + near_got[0].astype(f32)
+    near_acc = near_acc + swap_near(onward, HALVING[0][1]).astype(f32)
 
     count = LINE * RING
     block = shard // CORES // count
@@ -368,12 +365,12 @@
 
     query_grad, row_loss = pl.pallas_call(
         finish_kernel,
-        in_specs=[smem] + [vmem] * 7,
+        in_specs=[smem] + [vmem] * 7 + [hbm],
         out_specs=(vmem, vmem),
         out_shape=(like((own, width), f32), like((1, own), f32)),
         compiler_params=params(),
         name="finish",
-    )(spot, near_acc, query_far, positives, score, lse, joined, other)
+    )(spot, near_acc, query_far, positives, score, lse, joined, other, neg_grad)
     return (query_grad, row_loss.reshape(own), neg_grad)
 
 

time: 113 us -> 115 us (1.018)
  waiting for transfers between devices: 33.5 us -> 34.9 us
    ppermute x3 -> x4, waiting for transfers between devices: 10.7 us -> 15.2 us  [mirror(): return lax.ppermute(value, ('dp', 'neg'), perm)]
    ppermute x3 -> x4, starting transfers between devices: 17.8 us -> 21.6 us  [mirror(): return lax.ppermute(value, ('dp', 'neg'), perm)]
    ppermute x4 -> x3, waiting for transfers between devices: 11.6 us -> 8.54 us  [swap_near(): return lax.ppermute(value, 'neg', perm)]
    ppermute x4 -> x3, starting transfers between devices: 10.4 us -> 7.39 us  [swap_near(): return lax.ppermute(value, 'neg', perm)]
where the time goes in v6:
time: 115 us; the launch traced here: 114 us
  starting transfers between devices  48.9 us (43%)
  waiting for transfers between devices  34.9 us (30%)
  Pallas kernels  16.8 us (15%)
  blocking collectives  7.8 us (7%)
  local copies, waits for them, and re-layouts  2.86 us (2%)
  other arithmetic  1.82 us (2%)
    ppermute x4, starting transfers between devices, mirror(): return lax.ppermute(value, ('dp', 'neg'), perm)  21.6 us
    all_to_all x2, starting transfers between devices, trade(): lax.all_to_all(value, axis, 0, 0, tiled=True, axis_index_groups=groups)  18 us
    ppermute x4, waiting for transfers between devices, mirror(): return lax.ppermute(value, ('dp', 'neg'), perm)  15.2 us
    all_to_all x2, waiting for transfers between devices, trade(): lax.all_to_all(value, axis, 0, 0, tiled=True, axis_index_groups=groups)  11.1 us
    ppermute x3, waiting for transfers between devices, swap_near(): return lax.ppermute(value, 'neg', perm)  8.54 us
    all_to_all x1, blocking collectives, trade(): lax.all_to_all(value, axis, 0, 0, tiled=True, axis_index_groups=groups)  7.8 us
    pallas_call x1, Pallas kernels, per_device(): pl.pallas_call(grads_kernel, in_specs=[smem, hbm] + [vmem] * 5, out_specs...  7.41 us
    ppermute x3, starting transfers between devices, swap_near(): return lax.ppermute(value, 'neg', perm)  7.39 us
  transfers between devices with their start and end apart: 10, of which 7 were waited for; matrix products, arithmetic and copies ran while one was open for 1% of the time, Pallas kernels for 2%

profile of v6, /device:TPU:8, one launch (start us, length us, event | category | flops | bytes accessed | tf_op | source)
XLA Modules:
  0.0 114.1 jit_solution(4394402669436018143)
XLA Ops:
  0.6 6.1 %collective-permute-start = (bf16[256,256]{1,0:T(8,128)(2,1)}, bf16[256,256]{1,0:T(8,128)(2,1)S(1)}, u32[]{:S(2)}, u32[]{:S(2)}) collective-permute-start(bf16[256,256]{1,0:T(8,128)(2,1)} %queries_ref.1), channel_id=1, source_target_pairs={{0,388},{1,389},{2,390},{3,391},{4,384},{5,385},{6,386},{7,387},{8... | collective-permute-start | bytes 393224 | tf_op jit(solution)/shard_map/ppermute | solution.py:38
  6.7 4.3 %collective-permute-done.far_ref = bf16[256,256]{1,0:T(8,128)(2,1)S(1)} collective-permute-done((bf16[256,256]{1,0:T(8,128)(2,1)}, bf16[256,256]{1,0:T(8,128)(2,1)S(1)}, u32[]{:S(2)}, u32[]{:S(2)}) %collective-permute-start) | collective-permute-done | bytes 131104 | tf_op jit(solution)/shard_map/ppermute | solution.py:38
  11.0 0.9 copy-done.4
  11.9 1.1 spread.1
  13.0 0.0 copy-start.11
  13.0 4.5 %all-to-all-start = ((bf16[4,2,256,256]{3,2,1,0:T(8,128)(2,1)}), bf16[4,2,256,256]{3,2,1,0:T(8,128)(2,1)S(1)}, u32[]{:S(2)}, u32[]{:S(2)}) async-start(bf16[4,2,256,256]{3,2,1,0:T(8,128)(2,1)} %spread.1), calls=%async_computation | async-start | bytes 2097152 | tf_op jit(solution)/shard_map/all_to_all | solution.py:242
  17.5 0.0 copy-done.5
  17.5 0.0 copy-done.6
  17.5 0.0 copy-done.9
  17.5 0.0 copy-done.10
  17.5 0.0 copy-done.11
  17.6 0.0 copy-start.8
  17.6 1.2 %copy-done.8 = bf16[2048,256]{1,0:T(8,128)(2,1)S(1)} copy-done((bf16[2048,256]{1,0:T(8,128)(2,1)S(1)}, bf16[2048,256]{1,0:T(8,128)(2,1)}, u32[]{:S(2)}) %copy-start.8) | copy-done | bytes 1048600
  18.8 1.8 %lookup.1 = (f32[16,128]{1,0:T(8,128)S(1)}, f32[1,256]{1,0:T(1,128)S(1)}, bf16[2048,256]{1,0:T(8,128)(2,1)S(1)}) custom-call(s32[1]{0:T(128)} %bitcast.1.place_ref, s32[512,128]{1,0:T(8,128)S(1)} %bitcast.18, s32[16,128]{1,0:T(8,128)S(1)} %bitcast.19, s32[2,128]{1,0:T(2,128)S(1)} %bitcast.20, bf16[256,256]{1,0:T(8,128)(2,1)S(1)} %copy-done.5, ...), custom_call_target="tpu_custom_call" | custom-call | flops 1000000000 | bytes 2000000 | tf_op jit(solution)/shard_map/lookup/pallas_call | solution.py:261
  20.6 11.1 %all-to-all-done.blocks_hbm = bf16[4,2,256,256]{3,2,1,0:T(8,128)(2,1)S(1)} async-done(((bf16[4,2,256,256]{3,2,1,0:T(8,128)(2,1)}), bf16[4,2,256,256]{3,2,1,0:T(8,128)(2,1)S(1)}, u32[]{:S(2)}, u32[]{:S(2)}) %all-to-all-start) | async-done | bytes 1048608 | tf_op jit(solution)/shard_map/all_to_all | solution.py:242
  31.7 5.3 %stats.1 = f32[4,8,256]{2,1,0:T(8,128)S(1)} custom-call(s32[1]{0:T(128)} %bitcast.spot_ref, bf16[4,2,256,256]{3,2,1,0:T(8,128)(2,1)S(1)} %all-to-all-done.blocks_hbm, bf16[2048,256]{1,0:T(8,128)(2,1)S(1)} %get-tuple-element.15.negatives_ref, f32[16,128]{1,0:T(8,128)S(1)} %get-tuple-element.16.rows_ref, f32[1,256]{1,0:T(1,128)S(1)} %get-tuple-element.17.score_ref), custom_call_target="tpu_custom_call" | custom-call | flops 2147483648 | bytes 4000000 | tf_op jit(solution)/shard_map/stats/pallas_call | solution.py:301
  37.1 7.8 %all_to_all.15.parts_ref = f32[4,8,256]{2,1,0:T(8,128)S(1)} all-to-all(f32[4,8,256]{2,1,0:T(8,128)S(1)} %stats.1), channel_id=1, replica_groups={{0,1,2,3},{4,5,6,7},{8,9,10,11},{12,13,14,15},{16,17,18,19},{20,21,22,2..., dimensions={0} | all-to-all | bytes 65536 | tf_op jit(solution)/shard_map/all_to_all | solution.py:242
  44.9 6.2 %collective-permute-start.1 = (f32[8,256]{1,0:T(8,128)S(1)}, f32[8,256]{1,0:T(8,128)S(1)}, u32[]{:S(2)}, u32[]{:S(2)}) collective-permute-start(f32[8,256]{1,0:T(8,128)S(1)} %join.1.joined_ref), channel_id=1, source_target_pairs={{0,388},{1,389},{2,390},{3,391},{4,384},{5,385},{6,386},{7,387},{8... | collective-permute-start | bytes 24584 | tf_op jit(solution)/shard_map/ppermute | solution.py:38
  51.1 0.6 copy.10
  51.8 1.7 %collective-permute-done.1.other_ref = f32[8,256]{1,0:T(8,128)S(1)} collective-permute-done((f32[8,256]{1,0:T(8,128)S(1)}, f32[8,256]{1,0:T(8,128)S(1)}, u32[]{:S(2)}, u32[]{:S(2)}) %collective-permute-start.1) | collective-permute-done | bytes 8224 | tf_op jit(solution)/shard_map/ppermute | solution.py:38
  53.4 7.4 %grads.1 = (f32[2,256,256]{2,1,0:T(8,128)S(1)}, f32[2,256,256]{2,1,0:T(8,128)S(1)}, f32[2,256,256]{2,1,0:T(8,128)S(1)}, f32[2,256,256]{2,1,0:T(8,128)S(1)}, f32[...) custom-call(s32[1]{0:T(128)} %bitcast.spot_ref, ...), custom_call_target="tpu_custom_call" | custom-call | flops 6442450944 | bytes 8000000 | tf_op jit(solution)/shard_map/grads/pallas_call | solution.py:321
  60.8 0.0 copy-start
  60.9 1.9 %collective-permute-start.7 = (f32[1024,256]{1,0:T(8,128)S(1)}, f32[1024,256]{1,0:T(8,128)S(1)}, u32[]{:S(2)}, u32[]{:S(2)}) collective-permute-start(f32[1024,256]{1,0:T(8,128)S(1)} %get-tuple-element.24), channel_id=1, source_target_pairs={{0,8},{8,0},{16,24},{24,16},{32,40},{40,32},{48,56},{56,48},{64,72... | collective-permute-start | bytes 3145736 | tf_op jit(solution)/shard_map/ppermute | solution.py:48
  62.9 2.5 %collective-permute-start.4 = (f16[2,256,256]{2,1,0:T(8,128)(2,1)S(1)}, f16[2,256,256]{2,1,0:T(8,128)(2,1)S(1)}, u32[]{:S(2)}, u32[]{:S(2)}) collective-permute-start(f16[2,256,256]{2,1,0:T(8,128)(2,1)S(1)} %convert_element_type.55), channel_id=1, source_target_pairs={{0,1},{1,0},{2,3},{3,2},{4,5},{5,4},{6,7},{7,6},{8,9},{9,8},{10,11... | collective-permute-start | bytes 786440 | tf_op jit(solution)/shard_map/ppermute | solution.py:43
  65.4 3.0 %collective-permute-start.2 = (f16[2,256,256]{2,1,0:T(8,128)(2,1)S(1)}, f16[2,256,256]{2,1,0:T(8,128)(2,1)S(1)}, u32[]{:S(2)}, u32[]{:S(2)}) collective-permute-start(f16[2,256,256]{2,1,0:T(8,128)(2,1)S(1)} %convert_element_type.49), channel_id=1, source_target_pairs={{0,3},{1,2},{2,1},{3,0},{4,7},{5,6},{6,5},{7,4},{8,11},{9,10},{10,... | collective-permute-start | bytes 786440 | tf_op jit(solution)/shard_map/ppermute | solution.py:43
  68.4 5.1 %collective-permute-done.4 = f16[2,256,256]{2,1,0:T(8,128)(2,1)S(1)} collective-permute-done((f16[2,256,256]{2,1,0:T(8,128)(2,1)S(1)}, f16[2,256,256]{2,1,0:T(8,128)(2,1)S(1)}, u32[]{:S(2)}, u32[]{:S(2)}) %collective-permute-start.4) | collective-permute-done | bytes 262176 | tf_op jit(solution)/shard_map/ppermute | solution.py:43
  73.5 3.4 %collective-permute-done.2 = f16[2,256,256]{2,1,0:T(8,128)(2,1)S(1)} collective-permute-done((f16[2,256,256]{2,1,0:T(8,128)(2,1)S(1)}, f16[2,256,256]{2,1,0:T(8,128)(2,1)S(1)}, u32[]{:S(2)}, u32[]{:S(2)}) %collective-permute-start.2) | collective-permute-done | bytes 262176 | tf_op jit(solution)/shard_map/ppermute | solution.py:43
  76.9 0.0 collective-permute-done.7.got_ref
  76.9 0.3 sum_cores.1
  77.2 0.0 copy-done
  77.3 0.0 copy-done.2
  77.3 1.0 convert_element_type.62
  78.3 13.5 %all-to-all-start.2 = ((f16[32,40,256]{2,1,0:T(8,128)(2,1)}), f16[32,40,256]{2,1,0:T(8,128)(2,1)S(1)}, u32[]{:S(2)}, u32[]{:S(2)}) async-start(f16[32,40,256]{2,1,0:T(8,128)(2,1)} %convert_element_type.62), calls=%async_computation.2 | async-start | bytes 1310720 | tf_op jit(solution)/shard_map/all_to_all | solution.py:242
  91.7 0.0 copy-done.3
  91.7 0.1 add_convert_fusion
  91.8 0.1 slice_bitcast_fusion.1
  91.9 5.5 %collective-permute-start.5 = (f16[256,256]{1,0:T(8,128)(2,1)S(1)}, f16[256,256]{1,0:T(8,128)(2,1)S(1)}, u32[]{:S(2)}, u32[]{:S(2)}) collective-permute-start(f16[256,256]{1,0:T(8,128)(2,1)S(1)} %get-tuple-element.27), channel_id=1, source_target_pairs={{0,388},{1,389},{2,390},{3,391},{4,384},{5,385},{6,386},{7,387},{8... | collective-permute-start | bytes 393224 | tf_op jit(solution)/shard_map/ppermute | solution.py:38
  97.4 3.8 %collective-permute-start.6 = (f16[256,256]{1,0:T(8,128)(2,1)S(1)}, f16[256,256]{1,0:T(8,128)(2,1)S(1)}, u32[]{:S(2)}, u32[]{:S(2)}) collective-permute-start(f16[256,256]{1,0:T(8,128)(2,1)S(1)} %get-tuple-element.28), channel_id=1, source_target_pairs={{0,391},{1,390},{2,389},{3,388},{4,387},{5,386},{6,385},{7,384},{8... | collective-permute-start | bytes 393224 | tf_op jit(solution)/shard_map/ppermute | solution.py:38
  101.3 1.9 %collective-permute-start.3 = (f16[256,256]{1,0:T(8,128)(2,1)S(1)}, f16[256,256]{1,0:T(8,128)(2,1)S(1)}, u32[]{:S(2)}, u32[]{:S(2)}) collective-permute-start(f16[256,256]{1,0:T(8,128)(2,1)S(1)} %fusion.1), channel_id=1, source_target_pairs={{0,1},{1,0},{2,3},{3,2},{4,5},{5,4},{6,7},{7,6},{8,9},{9,8},{10,11... | collective-permute-start | bytes 393224 | tf_op jit(solution)/shard_map/ppermute | solution.py:43
  103.2 7.0 %collective-permute-done.5 = f16[256,256]{1,0:T(8,128)(2,1)S(1)} collective-permute-done((f16[256,256]{1,0:T(8,128)(2,1)S(1)}, f16[256,256]{1,0:T(8,128)(2,1)S(1)}, u32[]{:S(2)}, u32[]{:S(2)}) %collective-permute-start.5) | collective-permute-done | bytes 131104 | tf_op jit(solution)/shard_map/ppermute | solution.py:38
  110.2 2.3 %collective-permute-done.6 = f16[256,256]{1,0:T(8,128)(2,1)S(1)} collective-permute-done((f16[256,256]{1,0:T(8,128)(2,1)S(1)}, f16[256,256]{1,0:T(8,128)(2,1)S(1)}, u32[]{:S(2)}, u32[]{:S(2)}) %collective-permute-start.6) | collective-permute-done | bytes 131104 | tf_op jit(solution)/shard_map/ppermute | solution.py:38
  112.5 0.0 collective-permute-done.3
  112.6 0.0 all-to-all-done.2
  112.6 0.1 convert_element_type.63
  112.7 0.3 fusion.4
  113.0 0.1 fusion.neg_grad_ref
  113.2 0.0 copy-start.7
  113.2 0.9 finish.1
  (17 shorter events, 0.2 us)
Async XLA Ops:
  0.6 10.4 %collective-permute-start = (bf16[256,256]{1,0:T(8,128)(2,1)}, bf16[256,256]{1,0:T(8,128)(2,1)S(1)}, u32[]{:S(2)}, u32[]{:S(2)}) collective-permute-start(bf16[256,256]{1,0:T(8,128)(2,1)} %queries_ref.1), channel_id=1, source_target_pairs={{0,388},{1,389},{2,390},{3,391},{4,384},{5,385},{6,386},{7,387},{8... | collective-permute-start | bytes 393224 | tf_op jit(solution)/shard_map/ppermute | solution.py:38
  11.0 0.9 copy-start.4
  13.0 4.5 %copy-start.5 = (bf16[256,256]{1,0:T(8,128)(2,1)S(1)}, bf16[256,256]{1,0:T(8,128)(2,1)}, u32[]{:S(2)}) copy-start(bf16[256,256]{1,0:T(8,128)(2,1)} %queries_ref.1) | copy-start | bytes 393220
  13.0 4.5 %copy-start.6 = (bf16[256,256]{1,0:T(8,128)(2,1)S(1)}, bf16[256,256]{1,0:T(8,128)(2,1)}, u32[]{:S(2)}) copy-start(bf16[256,256]{1,0:T(8,128)(2,1)} %pos_ref.3) | copy-start | bytes 393220
  13.0 4.6 %copy-start.9 = (s32[65536]{0:T(1024)S(1)}, s32[65536]{0:T(1024)}, u32[]{:S(2)}) copy-start(s32[65536]{0:T(1024)} %param.11) | copy-start | bytes 786436
  13.0 4.6 %copy-start.10 = (s32[2048]{0:T(1024)S(1)}, s32[2048]{0:T(1024)}, u32[]{:S(2)}) copy-start(s32[2048]{0:T(1024)} %param.10) | copy-start | bytes 24580
  13.0 4.6 %copy-start.11 = (s32[256]{0:T(256)S(1)}, s32[256]{0:T(256)}, u32[]{:S(2)}) copy-start(s32[256]{0:T(256)} %param.9) | copy-start | bytes 3076
  13.0 18.7 %all-to-all-start = ((bf16[4,2,256,256]{3,2,1,0:T(8,128)(2,1)}), bf16[4,2,256,256]{3,2,1,0:T(8,128)(2,1)S(1)}, u32[]{:S(2)}, u32[]{:S(2)}) async-start(bf16[4,2,256,256]{3,2,1,0:T(8,128)(2,1)} %spread.1), calls=%async_computation | async-start | bytes 2097152 | tf_op jit(solution)/shard_map/all_to_all | solution.py:242
  17.6 1.2 %copy-start.8 = (bf16[2048,256]{1,0:T(8,128)(2,1)S(1)}, bf16[2048,256]{1,0:T(8,128)(2,1)}, u32[]{:S(2)}) copy-start(bf16[2048,256]{1,0:T(8,128)(2,1)} %negatives_ref.1) | copy-start | bytes 3145732
  44.9 8.6 %collective-permute-start.1 = (f32[8,256]{1,0:T(8,128)S(1)}, f32[8,256]{1,0:T(8,128)S(1)}, u32[]{:S(2)}, u32[]{:S(2)}) collective-permute-start(f32[8,256]{1,0:T(8,128)S(1)} %join.1.joined_ref), channel_id=1, source_target_pairs={{0,388},{1,389},{2,390},{3,391},{4,384},{5,385},{6,386},{7,387},{8... | collective-permute-start | bytes 24584 | tf_op jit(solution)/shard_map/ppermute | solution.py:38
  60.8 16.4 %copy-start = (f32[2,256,256]{2,1,0:T(8,128)}, f32[2,256,256]{2,1,0:T(8,128)S(1)}, u32[]{:S(2)}) copy-start(f32[2,256,256]{2,1,0:T(8,128)S(1)} %get-tuple-element.18) | copy-start | bytes 1572868
  60.9 16.4 %copy-start.2 = (f32[2,256,256]{2,1,0:T(8,128)}, f32[2,256,256]{2,1,0:T(8,128)S(1)}, u32[]{:S(2)}) copy-start(f32[2,256,256]{2,1,0:T(8,128)S(1)} %get-tuple-element.20) | copy-start | bytes 1572868
  60.9 16.0 %collective-permute-start.7 = (f32[1024,256]{1,0:T(8,128)S(1)}, f32[1024,256]{1,0:T(8,128)S(1)}, u32[]{:S(2)}, u32[]{:S(2)}) collective-permute-start(f32[1024,256]{1,0:T(8,128)S(1)} %get-tuple-element.24), channel_id=1, source_target_pairs={{0,8},{8,0},{16,24},{24,16},{32,40},{40,32},{48,56},{56,48},{64,72... | collective-permute-start | bytes 3145736 | tf_op jit(solution)/shard_map/ppermute | solution.py:48
  62.9 10.6 %collective-permute-start.4 = (f16[2,256,256]{2,1,0:T(8,128)(2,1)S(1)}, f16[2,256,256]{2,1,0:T(8,128)(2,1)S(1)}, u32[]{:S(2)}, u32[]{:S(2)}) collective-permute-start(f16[2,256,256]{2,1,0:T(8,128)(2,1)S(1)} %convert_element_type.55), channel_id=1, source_target_pairs={{0,1},{1,0},{2,3},{3,2},{4,5},{5,4},{6,7},{7,6},{8,9},{9,8},{10,11... | collective-permute-start | bytes 786440 | tf_op jit(solution)/shard_map/ppermute | solution.py:43
  65.4 11.5 %collective-permute-start.2 = (f16[2,256,256]{2,1,0:T(8,128)(2,1)S(1)}, f16[2,256,256]{2,1,0:T(8,128)(2,1)S(1)}, u32[]{:S(2)}, u32[]{:S(2)}) collective-permute-start(f16[2,256,256]{2,1,0:T(8,128)(2,1)S(1)} %convert_element_type.49), channel_id=1, source_target_pairs={{0,3},{1,2},{2,1},{3,0},{4,7},{5,6},{6,5},{7,4},{8,11},{9,10},{10,... | collective-permute-start | bytes 786440 | tf_op jit(solution)/shard_map/ppermute | solution.py:43
  78.3 13.5 %copy-start.3 = (f32[2,256,256]{2,1,0:T(8,128)S(1)}, f32[2,256,256]{2,1,0:T(8,128)}, u32[]{:S(2)}) copy-start(f32[2,256,256]{2,1,0:T(8,128)} %copy-done.2) | copy-start | bytes 1572868
  78.3 23.0 %copy-start.1 = (f32[2,256,256]{2,1,0:T(8,128)S(1)}, f32[2,256,256]{2,1,0:T(8,128)}, u32[]{:S(2)}) copy-start(f32[2,256,256]{2,1,0:T(8,128)} %copy-done) | copy-start | bytes 1572868
  78.3 34.3 %all-to-all-start.2 = ((f16[32,40,256]{2,1,0:T(8,128)(2,1)}), f16[32,40,256]{2,1,0:T(8,128)(2,1)S(1)}, u32[]{:S(2)}, u32[]{:S(2)}) async-start(f16[32,40,256]{2,1,0:T(8,128)(2,1)} %convert_element_type.62), calls=%async_computation.2 | async-start | bytes 1310720 | tf_op jit(solution)/shard_map/all_to_all | solution.py:242
  91.9 18.3 %collective-permute-start.5 = (f16[256,256]{1,0:T(8,128)(2,1)S(1)}, f16[256,256]{1,0:T(8,128)(2,1)S(1)}, u32[]{:S(2)}, u32[]{:S(2)}) collective-permute-start(f16[256,256]{1,0:T(8,128)(2,1)S(1)} %get-tuple-element.27), channel_id=1, source_target_pairs={{0,388},{1,389},{2,390},{3,391},{4,384},{5,385},{6,386},{7,387},{8... | collective-permute-start | bytes 393224 | tf_op jit(solution)/shard_map/ppermute | solution.py:38
  97.4 15.1 %collective-permute-start.6 = (f16[256,256]{1,0:T(8,128)(2,1)S(1)}, f16[256,256]{1,0:T(8,128)(2,1)S(1)}, u32[]{:S(2)}, u32[]{:S(2)}) collective-permute-start(f16[256,256]{1,0:T(8,128)(2,1)S(1)} %get-tuple-element.28), channel_id=1, source_target_pairs={{0,391},{1,390},{2,389},{3,388},{4,387},{5,386},{6,385},{7,384},{8... | collective-permute-start | bytes 393224 | tf_op jit(solution)/shard_map/ppermute | solution.py:38
  101.3 11.2 %collective-permute-start.3 = (f16[256,256]{1,0:T(8,128)(2,1)S(1)}, f16[256,256]{1,0:T(8,128)(2,1)S(1)}, u32[]{:S(2)}, u32[]{:S(2)}) collective-permute-start(f16[256,256]{1,0:T(8,128)(2,1)S(1)} %fusion.1), channel_id=1, source_target_pairs={{0,1},{1,0},{2,3},{3,2},{4,5},{5,4},{6,7},{7,6},{8,9},{9,8},{10,11... | collective-permute-start | bytes 393224 | tf_op jit(solution)/shard_map/ppermute | solution.py:43
  113.2 0.9 copy-start.7
